TPU v7x, 512 devices: a whole 4x8x8 slice. The times are simulated.
512 devices in a mesh: pipe: 8 (over y_hi, core), mp: 64 (over z, x, y_lo).
Axes of the slice: x: 4, y: 8 (y_hi: 4, y_lo: 2; y = y_hi * 2 + y_lo), z: 8, core: 2. Of those that a mesh axis runs over, the one named last changes fastest.
Arguments:
- token_ids: int32 [8, 576], replicated, may hold values from 0 to 32767
- replica_table: int32 [8, 2], replicated, may hold values from 0 to 2, as said below
- embedding: bfloat16 [32768, 4096], P('pipe', 'mp'), may hold values from -150 to 150
- ln_gain: bfloat16 [8, 4096], P('pipe'), may hold values from 0.25 to 1.75
- ln_bias: bfloat16 [8, 4096], P('pipe'), may hold values from -3 to 3
- weight_in: bfloat16 [8, 12288, 4096], P('pipe', 'mp'), may hold values from -0.09375 to 0.09375
- weight_out: bfloat16 [8, 12288, 4096], P('pipe', 'mp'), may hold values from -0.0546875 to 0.0546875
- cotangent: bfloat16 [8, 576, 4096], P('pipe', None, 'mp'), may hold values from -0.1875 to 0.1875
Outputs:
- grad_in: bfloat16 [12288, 4096], P('mp', 'pipe')
- grad_out: bfloat16 [12288, 4096], P('mp', 'pipe')
Inputs may be any that keep to these rules, and one draw needn't show every extreme that they name: `replica_table`: column 0 of a row is the replica's template: 0, 1 or 2: the first 8, 10 or 12 twelfths of the replica's 576 slots are live; some replica has template 2. Column 1 is 1 for a surviving replica and 0 for a failed one; at least one replica survives.
All inputs are finite; a program needn't handle non-finite values.
Results may differ from a plain program's by a relative error of at most 0.017.
Values may be sent and summed in bfloat16 or wider, within the bound.
No kernel may reach another device: no remote copies, remote signals or barrier semaphores. Data moves between devices by JAX's collectives and lax.ppermute only.
A program may use at most 64 MiB of HBM per device.

v0:
```python
import jax
import jax.numpy as jnp
from jax import lax
from jax.sharding import PartitionSpec as P

epsilon = 1e-05


def spread(value, axis, source):
    kept = jnp.where(lax.axis_index(axis) == source, value, 0).astype(value.dtype)
    return lax.psum(kept, axis)


def smooth_gate(values):
    return jax.nn.gelu(values, approximate=True)


def on_device(
    token_ids, replica_table, embedding, ln_gain, ln_bias, weight_in, weight_out, cotangent
):
    replica_count = replica_table.shape[0]
    tok_count = cotangent.shape[1]
    col_count = cotangent.shape[2]
    replica_index = jnp.arange(replica_count, dtype=jnp.int32)
    source_replica = jnp.min(jnp.where(replica_table[:, 1] == 1, replica_index, replica_count))
    live_counts = tok_count * (4 + replica_table[:, 0]) // 6
    first_proj, gain_root, bias_root = (
        spread(weight_in, "pipe", source_replica),
        spread(ln_gain, "pipe", source_replica),
        spread(ln_bias, "pipe", source_replica),
    )
    position = lax.axis_index("pipe")
    own_ids = lax.dynamic_index_in_dim(token_ids, position, 0, keepdims=False)
    whole_table = lax.all_gather(embedding, "pipe", axis=0, tiled=True)
    emb_cols = jnp.take(whole_table, own_ids, axis=0)
    full_width = col_count * lax.axis_size("mp")
    gain_vec = gain_root[0].astype(jnp.float32)
    bias_vec = bias_root[0].astype(jnp.float32)
    gathered = lax.all_gather(emb_cols, "mp", axis=1, tiled=True).astype(jnp.float32)
    row_mean = jnp.sum(gathered, axis=1, keepdims=True) / full_width
    row_square = jnp.sum(gathered * gathered, axis=1, keepdims=True) / full_width
    scaled = (gathered - row_mean) * lax.rsqrt(row_square - row_mean * row_mean + epsilon)
    normed = (scaled * gain_vec + bias_vec).astype(jnp.bfloat16)
    preact = lax.dot_general(
        normed, first_proj[0], (((1,), (1,)), ((), ())), preferred_element_type=jnp.float32
    )
    activated = smooth_gate(preact).astype(jnp.bfloat16)
    second_proj = spread(weight_out, "pipe", source_replica)[0]
    upstream = lax.all_gather(cotangent[0], "mp", axis=1, tiled=True)
    live_here = lax.dynamic_index_in_dim(live_counts, position, 0, keepdims=False)
    row_index = jnp.arange(tok_count, dtype=jnp.int32)
    upstream = jnp.where((row_index < live_here)[:, None], upstream, jnp.zeros_like(upstream))
    out_part = lax.dot_general(
        activated, upstream, (((0,), (0,)), ((), ())), preferred_element_type=jnp.float32
    )
    grad_out = lax.psum_scatter(
        out_part.astype(jnp.bfloat16), "pipe", scatter_dimension=1, tiled=True
    )
    act_grad = lax.dot_general(
        upstream, second_proj, (((1,), (1,)), ((), ())), preferred_element_type=jnp.float32
    )
    pullback = jax.vjp(smooth_gate, preact)[1]
    dpreact = pullback(act_grad)[0].astype(jnp.bfloat16)
    in_part = lax.dot_general(
        dpreact, normed, (((0,), (0,)), ((), ())), preferred_element_type=jnp.float32
    )
    grad_in = lax.psum_scatter(
        in_part.astype(jnp.bfloat16), "pipe", scatter_dimension=1, tiled=True
    )
    return (grad_in, grad_out)


def solution(mesh):
    placed = (
        P(),
        P(),
        P("pipe", "mp"),
        P("pipe", None),
        P("pipe", None),
        P("pipe", "mp", None),
        P("pipe", "mp", None),
        P("pipe", None, "mp"),
    )
    return jax.shard_map(
        on_device,
        mesh=mesh,
        in_specs=placed,
        out_specs=(P("mp", "pipe"), P("mp", "pipe")),
        check_vma=False,
    )
```

profile of v0, /device:TPU:1, one launch (start us, length us, event | category | flops | bytes accessed | tf_op | source)
XLA Modules:
  0.0 953.9 jit_solution(15488569807223325492)
XLA Ops:
  7.2 0.0 copy-start.1
  7.2 0.0 copy-start.2
  7.2 0.0 all-gather.5.cloned.1.call-start
  7.2 2.6 copy.12
  9.8 0.0 all-gather.5.cloned.1.call-update
  9.9 0.0 all-gather.7.cloned.1.call-start
  9.9 0.7 dynamic-slice_reduce_fusion
  10.7 0.8 fusion.30
  11.4 94.1 %all-gather.5.cloned.1.call-done = bf16[32768,64]{1,0:T(8,128)(2,1)} async-done(((bf16[4096,64]{1,0:T(8,128)(2,1)}), bf16[32768,64]{1,0:T(8,128)(2,1)}) %all-gather.5.cloned.1.call-update) | async-done | bytes 4194320 | tf_op jit(solution)/shard_map/all_gather | solution.py:34
  105.5 6.1 gather_fusion
  111.6 0.0 copy-start.3
  111.7 0.0 copy-start.4
  111.7 0.1 broadcast_select_fusion
  111.8 0.8 copy.13
  112.6 0.0 all-gather.7.cloned.1.call-update
  112.6 0.0 all-reduce.4.cloned.1.call-start
  112.7 1.4 bitcast_select_fusion.8
  114.7 0.0 copy-done.1
  114.7 0.0 copy-done.2
  114.7 1.9 select_bitcast_fusion
  116.6 0.0 all-reduce.4.cloned.1.call-update
  116.6 0.0 all-gather.9.cloned.1.call-start
  116.7 0.5 all-gather.9.cloned.1.call-update
  117.2 0.0 reduce-scatter.3.cloned.1.call-start
  117.2 0.0 copy-done.3
  117.2 0.0 copy-done.4
  117.3 0.1 fusion.28
  117.4 26.3 %all-reduce = (bf16[4096]{0:T(1024)(128)(2,1)S(1)}, bf16[4096]{0:T(1024)(128)(2,1)S(1)}) all-reduce(bf16[4096]{0:T(1024)(128)(2,1)S(1)} %get-tuple-element.15, bf16[4096]{0:T(1024)(128)(2,1)S(1)} %get-tuple-element.14), channel_id=1, replica_groups=mesh['pipe'=8,'mp'=64] {'pipe'}, use_global_device_ids=true, to_apply=%region_5.6 | all-reduce | flops 8192 | bytes 32768 | tf_op jit(solution)/shard_map/psum | solution.py:11
  143.6 0.6 dynamic_slice.8
  144.2 0.6 iota_compare_fusion
  144.9 245.7 %all-gather.7.cloned.1.call-done = bf16[576,4096]{0,1:T(8,128)(2,1)} async-done(((bf16[576,64]{0,1:T(8,128)(2,1)}), bf16[576,4096]{0,1:T(8,128)(2,1)}) %all-gather.7.cloned.1.call-update) | async-done | bytes 4718608 | tf_op jit(solution)/shard_map/all_gather | solution.py:39
  390.6 0.0 copy-start
  390.6 4.2 convert_reduce_fusion
  394.8 0.0 copy-done
  394.8 4.1 fusion.3
  398.9 135.3 %all-reduce.4.cloned.1.call-done = (bf16[192,4096]{1,0:T(8,128)(2,1)}, bf16[192,4096]{1,0:T(8,128)(2,1)}) async-done(((bf16[192,4096]{1,0:T(8,128)(2,1)}, bf16[192,4096]{1,0:T(8,128)(2,1)}), (bf16[192,4096]{1,0:T(8,128)(2,1)}, bf16[192,4096]{1,0:T(8,128)(2,1)})) %all-reduce.4.cloned.1.call-update) | async-done | bytes 3145744 | tf_op jit(solution)/shard_map/psum | solution.py:11
  534.2 0.0 copy-start.5
  534.2 4.5 fusion.45
  538.7 273.0 %all-gather.9.cloned.1.call-done = bf16[1,576,4096]{1,2,0:T(8,128)(2,1)} async-done(((bf16[1,576,64]{1,2,0:T(8,128)(2,1)}), bf16[1,576,4096]{1,2,0:T(8,128)(2,1)}) %all-gather.9.cloned.1.call-update) | async-done | bytes 4718608 | tf_op jit(solution)/shard_map/all_gather | solution.py:49
  811.7 0.0 copy-done.5
  811.7 8.6 convolution_convert_fusion.1
  820.3 0.0 reduce-scatter.3.cloned.1.call-update
  820.3 0.0 reduce-scatter.5.cloned.1.call-start
  820.3 5.6 convolution_convert_fusion
  826.0 0.0 reduce-scatter.5.cloned.1.call-update
  826.0 74.1 %reduce-scatter.3.cloned.1.call-done = bf16[192,512]{1,0:T(8,128)(2,1)} async-done(((bf16[192,4096]{1,0:T(8,128)(2,1)}), bf16[192,512]{1,0:T(8,128)(2,1)}) %reduce-scatter.3.cloned.1.call-update) | async-done | bytes 196624 | tf_op jit(solution)/shard_map/reduce_scatter | solution.py:67
  900.1 47.0 %reduce-scatter.5.cloned.1.call-done = bf16[192,512]{1,0:T(8,128)(2,1)} async-done(((bf16[192,4096]{1,0:T(8,128)(2,1)}), bf16[192,512]{1,0:T(8,128)(2,1)}) %reduce-scatter.5.cloned.1.call-update) | async-done | bytes 196624 | tf_op jit(solution)/shard_map/reduce_scatter | solution.py:56
  (5 shorter events, 0.0 us)
Async XLA Ops:
  7.2 107.5 %copy-start.1 = (bf16[1,192,4096]{2,1,0:T(8,128)(2,1)S(1)}, bf16[1,192,4096]{2,1,0:T(8,128)(2,1)}, u32[]{:S(2)}) copy-start(bf16[1,192,4096]{2,1,0:T(8,128)(2,1)} %param.13) | copy-start | bytes 4718596
  7.2 107.5 %copy-start.2 = (bf16[1,192,4096]{2,1,0:T(8,128)(2,1)S(1)}, bf16[1,192,4096]{2,1,0:T(8,128)(2,1)}, u32[]{:S(2)}) copy-start(bf16[1,192,4096]{2,1,0:T(8,128)(2,1)} %param.14) | copy-start | bytes 4718596
  7.2 98.3 %all-gather.5.cloned.1.call-start = ((), (), s32[]{:S(2)}) async-start(), calls=%async_computation.2 | async-start | bytes 9437184 | tf_op jit(solution)/shard_map/all_gather | solution.py:34
  9.9 380.7 %all-gather.7.cloned.1.call-start = ((), (), s32[]{:S(2)}) async-start(), calls=%async_computation.3 | async-start | bytes 5324800 | tf_op jit(solution)/shard_map/all_gather | solution.py:39
  111.6 5.6 copy-start.3
  111.7 5.6 copy-start.4
  112.6 421.6 %all-reduce.4.cloned.1.call-start = ((), (), s32[]{:S(2)}) async-start(), calls=%async_computation.7 | async-start | bytes 6291456 | tf_op jit(solution)/shard_map/psum | solution.py:11
  116.6 695.1 %all-gather.9.cloned.1.call-start = ((), (), s32[]{:S(2)}) async-start(), calls=%async_computation.6 | async-start | bytes 5324800 | tf_op jit(solution)/shard_map/all_gather | solution.py:49
  117.2 782.9 %reduce-scatter.3.cloned.1.call-start = ((), (), s32[]{:S(2)}) async-start(), calls=%async_computation.4 | async-start | bytes 1769472 | tf_op jit(solution)/shard_map/reduce_scatter | solution.py:67
  390.6 4.2 copy-start
  534.2 277.5 %copy-start.5 = (bf16[192,4096]{1,0:T(8,128)(2,1)S(1)}, bf16[192,4096]{1,0:T(8,128)(2,1)}, u32[]{:S(2)}) copy-start(bf16[192,4096]{1,0:T(8,128)(2,1)} %get-tuple-element.7) | copy-start | bytes 4718596
  820.3 126.8 %reduce-scatter.5.cloned.1.call-start = ((), (), s32[]{:S(2)}) async-start(), calls=%async_computation.5 | async-start | bytes 1769472 | tf_op jit(solution)/shard_map/reduce_scatter | solution.py:56
Sparse Core Ops, SparseCore 0:
  10.2 95.2 all-gather.4
  112.7 277.8 all-gather.6
  393.6 140.6 all-reduce.3
  536.2 275.4 all-gather.8
  820.4 79.6 reduce-scatter.2
  903.4 43.6 reduce-scatter.4
where the time goes:
time: 956 us; the launch traced here: 954 us
  waiting for transfers between devices  870 us (91%)
  blocking collectives  26.3 us (3%)
  matrix products  18.7 us (2%)
  between operations  14.9 us (2%)
  other arithmetic  13.2 us (1%)
  local copies, waits for them, and re-layouts  10.8 us (1%)
    all_gather x1, waiting for transfers between devices, on_device(): upstream = lax.all_gather(cotangent[0], 'mp', axis=1, tiled=True)  273 us
    all_gather x1, waiting for transfers between devices, on_device(): lax.all_gather(emb_cols, 'mp', axis=1, tiled=True).astype(jnp.float32)  246 us
    psum x1, waiting for transfers between devices, spread(): return lax.psum(kept, axis)  135 us
    all_gather x1, waiting for transfers between devices, on_device(): whole_table = lax.all_gather(embedding, 'pipe', axis=0, tiled=True)  94.1 us
    reduce_scatter x1, waiting for transfers between devices, on_device(): lax.psum_scatter(in_part.astype(jnp.bfloat16), 'pipe', scatter_dimension=...  74.1 us
    reduce_scatter x1, waiting for transfers between devices, on_device(): lax.psum_scatter(out_part.astype(jnp.bfloat16), 'pipe', scatter_dimension...  47 us
    psum x1, blocking collectives, spread(): return lax.psum(kept, axis)  26.3 us
  transfers between devices with their start and end apart: 6, of which 6 were waited for; matrix products, arithmetic and copies ran while one was open for 3% of the time, Pallas kernels for 0%

commit v1 on v0

v1 whole, which is shorter than its diff:
```python
import math

import jax
import jax.numpy as jnp
from jax import lax
from jax.experimental import pallas as pl
from jax.experimental.pallas import tpu as pltpu
from jax.sharding import Mesh, PartitionSpec as P

epsilon = 1e-05
bf16, f32 = jnp.bfloat16, jnp.float32
MIB = 1 << 20
SLOPE, CUBE = math.sqrt(2 / math.pi), 0.044715


def shift(value, axis, size, by):
    return lax.ppermute(value, axis, [(i, (i + by) % size) for i in range(size)])


def lookup_kernel(low_ref, high_ref, table_ref, out_ref, groups):
    width, vocab = table_ref.shape
    count = 8
    depth = vocab // count

    @pl.when(pl.program_id(0) == 0)
    def _():
        for k in range(count):
            groups[k * width:(k + 1) * width, :] = table_ref[:, k * depth:(k + 1) * depth]

    rows = out_ref.shape[0]
    place = lax.broadcasted_iota(jnp.int32, (rows, depth), 1)
    lane = lax.broadcasted_iota(jnp.int32, (rows, 2 * width), 1)
    total = jnp.zeros((rows, 2 * width), f32)
    for side, ref in enumerate((low_ref, high_ref)):
        ids = ref[...]
        group = jnp.right_shift(ids, 9)
        inner = jnp.bitwise_and(ids, depth - 1)
        hot = (place == inner).astype(f32).astype(bf16)
        picked = lax.dot_general(
            hot, groups[...], (((1,), (1,)), ((), ())), preferred_element_type=f32
        )
        pair = jnp.right_shift(group, 1)
        found = jnp.zeros((rows, 2 * width), f32)
        for j in range(count // 2):
            found += jnp.where(pair == j, picked[:, 2 * j * width:2 * (j + 1) * width], 0.0)
        turned = pltpu.roll(found, width, 1)
        found = jnp.where(jnp.bitwise_and(group, 1) == side, found, turned)
        total += jnp.where((lane >= width) == (side == 1), found, 0.0)
    out_ref[...] = total.astype(bf16)


def lookup(low, high, table):
    rows = low.shape[0]
    width, vocab = table.shape
    step = rows // 4
    return pl.pallas_call(
        lookup_kernel,
        grid=(4,),
        in_specs=[
            pl.BlockSpec((step, 1), lambda i: (i, 0)),
            pl.BlockSpec((step, 1), lambda i: (i, 0)),
            pl.BlockSpec((width, vocab), lambda i: (0, 0)),
        ],
        out_specs=pl.BlockSpec((step, 2 * width), lambda i: (i, 0)),
        out_shape=jax.ShapeDtypeStruct((rows, 2 * width), bf16),
        scratch_shapes=[pltpu.VMEM((8 * width, vocab // 8), bf16)],
        compiler_params=pltpu.CompilerParams(vmem_limit_bytes=32 * MIB),
        name="lookup",
    )(low, high, table)


def laid_out(info_ref, blocks):
    x = info_ref[0]
    own, right, left, far0, far1 = blocks
    depth, rows, lanes = own.shape
    half = depth // 2
    for k in range(depth):
        far = far0.at[k] if k < half else far1.at[k - half]
        for by, ref in ((0, own.at[k]), (3, right.at[k]), (1, left.at[k]), (2, far)):
            spot = 4 * k + jnp.bitwise_and(x + by, 3)
            yield ref, spot, pl.ds(pl.multiple_of(spot * lanes, lanes), lanes)


def unpacked(ref, start, step):
    rows, lanes = ref.shape
    half = lanes // 2
    first = ref[pl.ds(start, step), :].astype(f32)
    second = ref[pl.ds(rows // 2 + start, step), :].astype(f32)
    low = lax.broadcasted_iota(jnp.int32, (step, lanes), 1) < half
    return (
        jnp.where(low, first, pltpu.roll(second, half, 1)),
        jnp.where(low, pltpu.roll(first, half, 1), second),
    )


STEP = 48


def merge_kernel(info_ref, *refs):
    *blocks, out_ref = refs
    live, first = info_ref[1], info_ref[2]
    _, rows, lanes = blocks[0].shape

    @pl.loop(0, rows // 2 // STEP)
    def _(i):
        start = pl.multiple_of(i * STEP, STEP)
        slot = lax.broadcasted_iota(jnp.int32, (STEP, lanes), 0) + first + start
        for ref, _, here in laid_out(info_ref, blocks):
            for side, v in enumerate(unpacked(ref, start, STEP)):
                base = side * (rows // 2)
                v = jnp.where(slot + base < live, v, 0.0)
                out_ref[pl.ds(pl.multiple_of(base + start, STEP), STEP), here] = v.astype(bf16)


def norm_kernel(info_ref, *refs):
    *blocks, gain_ref, bias_ref, out_ref = refs
    _, rows, lanes = blocks[0].shape
    full = out_ref.shape[1]

    @pl.loop(0, rows // 2 // STEP)
    def _(i):
        start = pl.multiple_of(i * STEP, STEP)
        here = [pl.ds(pl.multiple_of(start + s * (rows // 2), STEP), STEP) for s in range(2)]
        zeros = jnp.zeros((STEP, lanes), f32)
        total, square = [zeros, zeros], [zeros, zeros]
        for ref, _, columns in laid_out(info_ref, blocks):
            for side, v in enumerate(unpacked(ref, start, STEP)):
                total[side] += v
                square[side] += v * v
                out_ref[here[side], columns] = v.astype(bf16)
        for side in range(2):
            mean = jnp.sum(total[side], axis=1, keepdims=True) / full
            power = jnp.sum(square[side], axis=1, keepdims=True) / full
            scale = lax.rsqrt(power - mean * mean + epsilon)
            for k in range(full // lanes):
                columns = slice(k * lanes, (k + 1) * lanes)
                v = (out_ref[here[side], columns].astype(f32) - mean) * scale
                v = v * gain_ref[k:k + 1, :] + bias_ref[k:k + 1, :]
                out_ref[here[side], columns] = v.astype(bf16)


def assemble(kernel, name, info, blocks, extra=()):
    depth, rows, lanes = blocks[0].shape
    return pl.pallas_call(
        kernel,
        in_specs=[pl.BlockSpec(memory_space=pltpu.SMEM)]
        + [pl.BlockSpec(memory_space=pltpu.VMEM)] * (len(blocks) + len(extra)),
        out_specs=pl.BlockSpec(memory_space=pltpu.VMEM),
        out_shape=jax.ShapeDtypeStruct((rows, 4 * depth * lanes), bf16),
        compiler_params=pltpu.CompilerParams(vmem_limit_bytes=32 * MIB),
        name=name,
    )(info, *blocks, *extra)


def gradient_kernel(normed0, normed1, up0, up1, weights, out_ref, acc, factors, ends):
    units, width = weights.shape[1:]
    rows = normed0.shape[0]
    tokens = ((normed0, up0), (normed1, up1))
    step = 1024
    for i, refs in enumerate(tokens):
        for j in range(2):
            total = jnp.zeros((rows, units), f32)
            for k in range(0, width, step):
                total += lax.dot_general(
                    refs[j][:, k:k + step], weights[j, :, k:k + step],
                    (((1,), (1,)), ((), ())), preferred_element_type=f32,
                )
            acc[j, i * rows:(i + 1) * rows, :] = total

    value = acc[0]
    bent = jnp.tanh(SLOPE * (value + CUBE * value * value * value))
    slope = 0.5 * (1.0 + bent) + 0.5 * value * (1.0 - bent * bent) * (
        SLOPE * (1.0 + 3.0 * CUBE * value * value)
    )
    factors[0] = jnp.transpose(acc[1] * slope).astype(bf16)
    factors[1] = jnp.transpose(0.5 * value * (1.0 + bent)).astype(bf16)

    main = 256
    rest = rows - main
    for j in range(2):
        for i, refs in enumerate(tokens):
            ends[j, i * rest:(i + 1) * rest, :] = refs[j][main:, :]

    out_width = out_ref.shape[-1]
    half = units // 2
    for q in range(width // out_width):
        columns = slice(q * out_width, (q + 1) * out_width)
        for j in range(2):
            end = jnp.concatenate([factors[j, :, main:rows], factors[j, :, rows + main:]], axis=1)
            total = jnp.dot(end, ends[j, :, columns], preferred_element_type=f32)
            for i, refs in enumerate(tokens):
                total += jnp.dot(
                    factors[j, :, i * rows:i * rows + main], refs[j][:main, columns],
                    preferred_element_type=f32,
                )
            total = total.astype(bf16)
            for y in range(2):
                out_ref[2 * q + y, j] = total[y * half:(y + 1) * half]


def gradients(normed, normed_other, upstream, upstream_other, weights):
    units, width = weights.shape[1:]
    rows = normed.shape[0]
    return pl.pallas_call(
        gradient_kernel,
        in_specs=[pl.BlockSpec(memory_space=pltpu.VMEM)] * 5,
        out_specs=pl.BlockSpec(memory_space=pltpu.VMEM),
        out_shape=jax.ShapeDtypeStruct((8, 2, units // 2, width // 4), bf16),
        scratch_shapes=[
            pltpu.VMEM((2, 2 * rows, units), f32),
            pltpu.VMEM((2, units, 2 * rows), bf16),
            pltpu.VMEM((2, 2 * (rows - 256), width), bf16),
        ],
        compiler_params=pltpu.CompilerParams(vmem_limit_bytes=48 * MIB),
        name="gradients",
    )(normed, normed_other, upstream, upstream_other, weights)


def gather_z(block):
    depth = lax.axis_size("z")
    return lax.all_to_all(jnp.broadcast_to(block, (depth,) + block.shape), "z", 0, 0)


def gather_x(own):
    return shift(own, "x", 4, 1), shift(own, "x", 4, -1)


def gather_far(right, left):
    half = right.shape[0] // 2
    return shift(right[:half], "x", 4, 1), shift(left[half:], "x", 4, -1)


def on_device(
    token_ids, replica_table, embedding, ln_gain, ln_bias, weight_in, weight_out, cotangent
):
    replicas = replica_table.shape[0]
    tok = cotangent.shape[1]
    cols = cotangent.shape[2]
    half = tok // 2
    vocab_block = embedding.shape[0]
    units, width = weight_in.shape[1:]
    part = units // 2

    yh, core, x, yl = (lax.axis_index(a) for a in ("yh", "core", "x", "yl"))
    position = 2 * yh + core
    replica_index = jnp.arange(replicas, dtype=jnp.int32)
    source = jnp.min(jnp.where(replica_table[:, 1] == 1, replica_index, replicas))
    live_counts = tok * (4 + replica_table[:, 0]) // 6
    live = lax.dynamic_index_in_dim(live_counts, position, 0, keepdims=False)

    pair = jnp.stack([weight_in[0], weight_out[0]]).reshape(2, 2, part, width)
    theirs = jnp.where(core == 0, pair[:, 1], pair[:, 0])
    mine = jnp.where(core == 0, pair[:, 0], pair[:, 1])
    mine = jnp.where(core == source % 2, mine, shift(theirs, "core", 2, 1))
    slot = jnp.arange(2).reshape(1, 2, 1, 1)
    spread = jnp.where((slot == yl) & (yh == source // 2), mine[:, None], jnp.zeros((), bf16))
    spread = spread.reshape(2, 2 * part, width)

    cot = cotangent[0].reshape(2, 2, half // 2, cols)
    cot = jnp.concatenate([cot[:, 0], cot[:, 1]], axis=2)
    cot = jnp.broadcast_to(cot, (8,) + cot.shape).reshape((16,) + cot.shape[1:])
    cot = lax.all_to_all(cot, ("z", "yl"), 0, 0).reshape(8, half, 2 * cols)

    local = (token_ids - position * vocab_block).reshape(replicas * 2, 2, half // 2)
    low = local[:, 0].reshape(-1, 1)
    high = local[:, 1].reshape(-1, 1)
    rows = lookup(low, high, embedding.T).reshape(2 * replicas, half // 2, 2 * cols)
    vectors = jnp.concatenate([ln_gain.reshape(-1, 2 * cols), ln_bias.reshape(-1, 2 * cols)])
    share = vectors.shape[0] // 2
    vectors = lax.dynamic_slice_in_dim(vectors, yl * share, share, 0)
    sent = jnp.concatenate(
        [rows, jnp.broadcast_to(vectors, (2 * replicas,) + vectors.shape)], axis=1
    )
    weights = lax.psum(spread, ("yh", "yl"))

    def slots(sent, cot):
        got = lax.all_to_all(sent, ("yh", "core", "yl"), 0, 0)
        info = jnp.stack([x, live, yl * half]).astype(jnp.int32)
        got, sides = lax.optimization_barrier((got, gather_x(cot)))
        upstream = assemble(merge_kernel, "merge", info, (cot, *sides, *gather_far(*sides)))
        upstream_other = shift(upstream, "core", 2, 1)
        got = got.reshape((replicas, 2) + got.shape[1:])
        emb = jnp.sum(got[:, :, : half // 2].astype(f32), axis=0).astype(bf16)
        emb = emb.reshape(half, 2 * cols)
        root = lax.dynamic_index_in_dim(got[:, :, half // 2 :], source, 0, keepdims=False)
        root = root.reshape(2, -1, 2 * cols).astype(f32)
        emb = gather_z(emb)
        sides = gather_x(emb)
        blocks = (emb, *sides, *gather_far(*sides))
        normed = assemble(norm_kernel, "norm", info, blocks, (root[0], root[1]))
        return normed, shift(normed, "core", 2, 1), upstream, upstream_other

    def nothing(sent, cot):
        return (jnp.zeros((half, width), bf16),) * 4

    normed, normed_other, upstream, upstream_other = lax.cond(
        source < replicas, slots, nothing, sent, cot
    )
    terms = gradients(normed, normed_other, upstream, upstream_other, weights)
    sums = lax.psum_scatter(terms, ("yh", "yl"), scatter_dimension=0)
    sums = sums.reshape(2, part, 2, width // 8)
    left, right = sums[:, :, 0], sums[:, :, 1]
    theirs = shift(jnp.where(core == 0, right, left), "core", 2, 1)
    mine = jnp.where(core == 0, left, right)
    top = jnp.where(core == 0, mine, theirs)
    bottom = jnp.where(core == 0, theirs, mine)
    done = jnp.concatenate([top, bottom], axis=1)
    return done[0], done[1]


def solution(mesh):
    fine = Mesh(mesh.devices.reshape(4, 2, 8, 4, 2), ("yh", "core", "z", "x", "yl"))
    pipe, mp = ("yh", "core"), ("z", "x", "yl")
    placed = (
        P(),
        P(),
        P(pipe, mp),
        P(pipe, None),
        P(pipe, None),
        P(pipe, mp, None),
        P(pipe, mp, None),
        P(pipe, None, mp),
    )
    return jax.shard_map(
        on_device,
        mesh=fine,
        in_specs=placed,
        out_specs=(P(mp, pipe), P(mp, pipe)),
        check_vma=False,
    )
```

time: 956 us -> 222 us (0.23)
  waiting for transfers between devices: 870 us -> 75.4 us
  starting transfers between devices: 0.24 us -> 65.1 us
  Pallas kernels: 0 us -> 24.8 us
  matrix products: 18.7 us -> 0 us
    all_gather x3 -> x0, waiting for transfers between devices: 613 us -> none  [the longest x1 273 us: on_device(): upstream = lax.all_gather(cotangent[0], 'mp', axis=1, tiled=True)]
    psum x1, waiting for transfers between devices: 135 us -> 0.01 us  [on_device(): weights = lax.psum(spread, ('yh', 'yl'))]
    reduce_scatter x2 -> x1, waiting for transfers between devices: 121 us -> 41.8 us  [on_device(): sums = lax.psum_scatter(terms, ('yh', 'yl'), scatter_dimension=0)]
    ppermute x0 -> x12, starting transfers between devices: none -> 49.8 us  [shift(): lax.ppermute(value, axis, [(i, (i + by) % size) for i in range(size)])]
    psum x1 -> x0, blocking collectives: 26.3 us -> none  [spread(): return lax.psum(kept, axis)]
    pallas_call x0 -> x4, Pallas kernels: none -> 24.8 us  [the longest x1 11.8 us: gradients(): pl.pallas_call(gradient_kernel, in_specs=[pl.BlockSpec(memory_space=pltpu...]
    all_to_all x0 -> x1, blocking collectives: none -> 19.1 us  [gather_z(): lax.all_to_all(jnp.broadcast_to(block, (depth,) + block.shape), 'z', 0, 0)]
    ppermute x0 -> x12, waiting for transfers between devices: none -> 19.1 us  [shift(): lax.ppermute(value, axis, [(i, (i + by) % size) for i in range(size)])]
  transfers between devices with their start and end apart: 6 -> 16, of which waited for: 6 -> 7; matrix products, arithmetic and copies ran while one was open for 3% -> 3% of each run, Pallas kernels for 0% -> 6%
where the time goes in v1:
time: 222 us; the launch traced here: 221 us
  waiting for transfers between devices  75.4 us (34%)
  starting transfers between devices  65.1 us (29%)
  Pallas kernels  24.8 us (11%)
  blocking collectives  19.1 us (9%)
  between operations  17.6 us (8%)
  other arithmetic  9.16 us (4%)
  local copies, waits for them, and re-layouts  7.84 us (4%)
    ppermute x12, starting transfers between devices, shift(): lax.ppermute(value, axis, [(i, (i + by) % size) for i in range(size)])  49.8 us
    reduce_scatter x1, waiting for transfers between devices, on_device(): sums = lax.psum_scatter(terms, ('yh', 'yl'), scatter_dimension=0)  41.8 us
    all_to_all x1, blocking collectives, gather_z(): lax.all_to_all(jnp.broadcast_to(block, (depth,) + block.shape), 'z', 0, 0)  19.1 us
    ppermute x12, waiting for transfers between devices, shift(): lax.ppermute(value, axis, [(i, (i + by) % size) for i in range(size)])  19.1 us
    pallas_call x1, Pallas kernels, gradients(): pl.pallas_call(gradient_kernel, in_specs=[pl.BlockSpec(memory_space=pltpu...  11.8 us
    all_to_all x1, starting transfers between devices, slots(): got = lax.all_to_all(sent, ('yh', 'core', 'yl'), 0, 0)  9.42 us
    all_to_all x1, waiting for transfers between devices, on_device(): cot = lax.all_to_all(cot, ('z', 'yl'), 0, 0).reshape(8, half, 2 * cols)  8.08 us
    pallas_call x2, Pallas kernels, assemble(): pl.pallas_call(kernel, in_specs=[pl.BlockSpec(memory_space=pltpu.SMEM)] +...  8.05 us
  transfers between devices with their start and end apart: 16, of which 7 were waited for; matrix products, arithmetic and copies ran while one was open for 3% of the time, Pallas kernels for 6%

profile of v1, /device:TPU:1, one launch (start us, length us, event | category | flops | bytes accessed | tf_op | source)
XLA Modules:
  0.0 221.1 jit_solution(9798177708610740403)
XLA Ops:
  7.2 2.2 pad_maximum_fusion
  9.4 1.3 fusion
  10.7 8.8 %collective-permute-start.10 = (bf16[2,96,4096]{2,1,0:T(8,128)(2,1)}, bf16[2,96,4096]{2,1,0:T(8,128)(2,1)}, u32[]{:S(2)}, u32[]{:S(2)}) collective-permute-start(bf16[2,96,4096]{2,1,0:T(8,128)(2,1)} %fusion), channel_id=1, source_target_pairs={{0,64},{64,0},{1,65},{65,1},{2,66},{66,2},{3,67},{67,3},{4,68},{68... | collective-permute-start | bytes 4718600 | tf_op jit(solution)/shard_map/ppermute | solution.py:17
  19.5 0.6 fusion.7
  23.0 0.2 fusion.2
  23.2 2.0 bitcast_select_fusion.1
  25.2 0.9 copy-done.2
  26.0 0.1 reshape_squeeze.11
  26.2 0.2 fusion.9
  26.4 0.1 copy.50
  26.6 0.9 broadcast_in_dim.42
  27.5 5.8 %all-to-all-start.2 = ((bf16[16,144,128]{2,1,0:T(8,128)(2,1)}), bf16[16,144,128]{2,1,0:T(8,128)(2,1)S(1)}, u32[]{:S(2)}, u32[]{:S(2)}) async-start(bf16[16,144,128]{2,1,0:T(8,128)(2,1)} %bitcast.14), calls=%async_computation.2 | async-start | bytes 1179648 | tf_op jit(solution)/shard_map/all_to_all | solution.py:262
  34.1 0.1 reshape.71
  34.3 0.4 reshape.84.low_ref
  34.8 0.4 reshape.85.high_ref
  35.2 5.0 %lookup.1 = bf16[2304,128]{1,0:T(8,128)(2,1)S(1)} custom-call(s32[2304,1]{1,0:T(8,128)S(1)} %reshape.84.low_ref, s32[2304,1]{1,0:T(8,128)S(1)} %reshape.85.high_ref, bf16[64,4096]{1,0:T(8,128)(2,1)S(1)} %bitcast.63), custom_call_target="tpu_custom_call" | custom-call | tf_op jit(solution)/shard_map/lookup/pallas_call | solution.py:56
  40.3 1.0 pad_maximum_fusion.1
  41.3 8.1 %all-to-all-done.2 = bf16[16,144,128]{2,1,0:T(8,128)(2,1)S(1)} async-done(((bf16[16,144,128]{2,1,0:T(8,128)(2,1)}), bf16[16,144,128]{2,1,0:T(8,128)(2,1)S(1)}, u32[]{:S(2)}, u32[]{:S(2)}) %all-to-all-start.2) | async-done | bytes 589856 | tf_op jit(solution)/shard_map/all_to_all | solution.py:262
  49.4 102.2 %conditional.1 = (bf16[288,4096]{1,0:T(8,128)(2,1)}, bf16[288,4096]{1,0:T(8,128)(2,1)}, bf16[288,4096]{1,0:T(8,128)(2,1)}, bf16[288,4096]{1,0:T(8,128)(2,1)}) conditional(s32[]{:T(128)} %convert_element_type.9, () %tuple.31, (s32[]{:T(128)}, s32[8,2]{0,1:T(2,128)S(1)}, s32[]{:T(128)}, s32[]{:T(128)}, s32[]{:T(128)}, ...), branch_computations={%region_1.2_spmd, %region_2.4_spmd} | conditional | flops 266333 | bytes 43319976 | solution.py:296
  49.4 9.4 %all-to-all-start = ((bf16[16,176,128]{2,1,0:T(8,128)(2,1)}), bf16[16,176,128]{2,1,0:T(8,128)(2,1)S(1)}, u32[]{:S(2)}, u32[]{:S(2)}) async-start(bf16[16,176,128]{2,1,0:T(8,128)(2,1)} %get-tuple-element.57), calls=%async_computation | async-start | bytes 1441792 | tf_op jit(solution)/shard_map/cond/branch_1_fun/all_to_all | solution.py:277
  58.8 3.1 %collective-permute-start = (bf16[8,288,128]{2,1,0:T(8,128)(2,1)S(1)}, bf16[8,288,128]{2,1,0:T(8,128)(2,1)S(1)}, u32[]{:S(2)}, u32[]{:S(2)}) collective-permute-start(bf16[8,288,128]{2,1,0:T(8,128)(2,1)S(1)} %bitcast.68), channel_id=1, source_target_pairs={{0,2},{2,4},{4,6},{6,0},{1,3},{3,5},{5,7},{7,1},{8,10},{10,12},{12... | collective-permute-start | bytes 1769480 | tf_op jit(solution)/shard_map/cond/branch_1_fun/ppermute | solution.py:17
  62.0 3.4 %collective-permute-start.1 = (bf16[8,288,128]{2,1,0:T(8,128)(2,1)S(1)}, bf16[8,288,128]{2,1,0:T(8,128)(2,1)S(1)}, u32[]{:S(2)}, u32[]{:S(2)}) collective-permute-start(bf16[8,288,128]{2,1,0:T(8,128)(2,1)S(1)} %bitcast.69), channel_id=1, source_target_pairs={{0,6},{2,0},{4,2},{6,4},{1,7},{3,1},{5,3},{7,5},{8,14},{10,8},{12,... | collective-permute-start | bytes 1769480 | tf_op jit(solution)/shard_map/cond/branch_1_fun/ppermute | solution.py:17
  65.3 11.6 %collective-permute-done.refs_1_ = bf16[8,288,128]{2,1,0:T(8,128)(2,1)S(1)} collective-permute-done((bf16[8,288,128]{2,1,0:T(8,128)(2,1)S(1)}, bf16[8,288,128]{2,1,0:T(8,128)(2,1)S(1)}, u32[]{:S(2)}, u32[]{:S(2)}) %collective-permute-start) | collective-permute-done | bytes 589856 | tf_op jit(solution)/shard_map/cond/branch_1_fun/ppermute | solution.py:17
  76.9 1.6 collective-permute-done.1.refs_2_
  78.5 6.4 %all-to-all-done = bf16[16,176,128]{2,1,0:T(8,128)(2,1)S(1)} async-done(((bf16[16,176,128]{2,1,0:T(8,128)(2,1)}), bf16[16,176,128]{2,1,0:T(8,128)(2,1)S(1)}, u32[]{:S(2)}, u32[]{:S(2)}) %all-to-all-start) | async-done | bytes 720928 | tf_op jit(solution)/shard_map/cond/branch_1_fun/all_to_all | solution.py:277
  85.0 0.8 copy-done.1
  85.9 19.1 %all_to_all.13.refs_0_ = bf16[8,288,128]{2,1,0:T(8,128)(2,1)S(1)} all-to-all(bf16[8,288,128]{2,1,0:T(8,128)(2,1)S(1)} %broadcast_in_dim.30), channel_id=1, replica_groups=mesh['yh'=4,'core'=2,'z'=8,'x'=4,'yl'=2] {'z'}, dimensions={0} | all-to-all | bytes 1179648 | tf_op jit(solution)/shard_map/cond/branch_1_fun/all_to_all | solution.py:221
  105.0 3.1 %collective-permute-start.2 = (bf16[8,288,128]{2,1,0:T(8,128)(2,1)S(1)}, bf16[8,288,128]{2,1,0:T(8,128)(2,1)S(1)}, u32[]{:S(2)}, u32[]{:S(2)}) collective-permute-start(bf16[8,288,128]{2,1,0:T(8,128)(2,1)S(1)} %all_to_all.13.refs_0_), channel_id=1, source_target_pairs={{0,2},{2,4},{4,6},{6,0},{1,3},{3,5},{5,7},{7,1},{8,10},{10,12},{12... | collective-permute-start | bytes 1769480 | tf_op jit(solution)/shard_map/cond/branch_1_fun/ppermute | solution.py:17
  108.2 3.4 %collective-permute-start.3 = (bf16[8,288,128]{2,1,0:T(8,128)(2,1)S(1)}, bf16[8,288,128]{2,1,0:T(8,128)(2,1)S(1)}, u32[]{:S(2)}, u32[]{:S(2)}) collective-permute-start(bf16[8,288,128]{2,1,0:T(8,128)(2,1)S(1)} %all_to_all.13.refs_0_), channel_id=1, source_target_pairs={{0,6},{2,0},{4,2},{6,4},{1,7},{3,1},{5,3},{7,5},{8,14},{10,8},{12,... | collective-permute-start | bytes 1769480 | tf_op jit(solution)/shard_map/cond/branch_1_fun/ppermute | solution.py:17
  112.9 0.7 dynamic_slice.9
  114.2 0.7 pad_add_fusion.info_ref
  114.9 0.9 slice.79
  115.8 1.9 collective-permute-start.7
  117.8 4.6 %collective-permute-start.8 = (bf16[4,288,128]{2,1,0:T(8,128)(2,1)S(1)}, bf16[4,288,128]{2,1,0:T(8,128)(2,1)S(1)}, u32[]{:S(2)}, u32[]{:S(2)}) collective-permute-start(bf16[4,288,128]{2,1,0:T(8,128)(2,1)S(1)} %slice.53), channel_id=1, source_target_pairs={{0,6},{2,0},{4,2},{6,4},{1,7},{3,1},{5,3},{7,5},{8,14},{10,8},{12,... | collective-permute-start | bytes 884744 | tf_op jit(solution)/shard_map/cond/branch_1_fun/ppermute | solution.py:17
  122.4 1.9 collective-permute-start.4
  124.3 4.6 %collective-permute-start.5 = (bf16[4,288,128]{2,1,0:T(8,128)(2,1)S(1)}, bf16[4,288,128]{2,1,0:T(8,128)(2,1)S(1)}, u32[]{:S(2)}, u32[]{:S(2)}) collective-permute-start(bf16[4,288,128]{2,1,0:T(8,128)(2,1)S(1)} %slice.78), channel_id=1, source_target_pairs={{0,6},{2,0},{4,2},{6,4},{1,7},{3,1},{5,3},{7,5},{8,14},{10,8},{12,... | collective-permute-start | bytes 884744 | tf_op jit(solution)/shard_map/cond/branch_1_fun/ppermute | solution.py:17
  129.0 3.2 %merge.1 = bf16[288,4096]{1,0:T(8,128)(2,1)} custom-call(s32[3]{0:T(128)S(1)} %pad_add_fusion.info_ref, bf16[8,288,128]{2,1,0:T(8,128)(2,1)S(1)} %bitcast.70, bf16[8,288,128]{2,1,0:T(8,128)(2,1)S(1)} %collective-permute-done.refs_1_, bf16[8,288,128]{2,1,0:T(8,128)(2,1)S(1)} %collective-permute-done.1.refs_2_, ...), custom_call_target="tpu_custom_call" | custom-call | tf_op jit(solution)/shard_map/cond/branch_1_fun/merge/pallas_call | solution.py:144
  132.2 7.7 %collective-permute-start.9 = (bf16[288,4096]{1,0:T(8,128)(2,1)}, bf16[288,4096]{1,0:T(8,128)(2,1)}, u32[]{:S(2)}, u32[]{:S(2)}) collective-permute-start(bf16[288,4096]{1,0:T(8,128)(2,1)} %merge.1), channel_id=1, source_target_pairs={{0,64},{64,0},{1,65},{65,1},{2,66},{66,2},{3,67},{67,3},{4,68},{68... | collective-permute-start | bytes 7077896 | tf_op jit(solution)/shard_map/cond/branch_1_fun/ppermute | solution.py:17
  140.0 4.8 %norm.1 = bf16[288,4096]{1,0:T(8,128)(2,1)} custom-call(s32[3]{0:T(128)S(1)} %pad_add_fusion.info_ref, bf16[8,288,128]{2,1,0:T(8,128)(2,1)S(1)} %all_to_all.13.refs_0_, bf16[8,288,128]{2,1,0:T(8,128)(2,1)S(1)} %collective-permute-done.2.refs_1_, bf16[8,288,128]{2,1,0:T(8,128)(2,1)S(1)} %collective-permute-done.3.refs_2_, ...), custom_call_target="tpu_custom_call" | custom-call | tf_op jit(solution)/shard_map/cond/branch_1_fun/norm/pallas_call | solution.py:144
  144.8 1.9 collective-permute-start.6
  146.7 4.8 %collective-permute-done.6 = bf16[288,4096]{1,0:T(8,128)(2,1)} collective-permute-done((bf16[288,4096]{1,0:T(8,128)(2,1)}, bf16[288,4096]{1,0:T(8,128)(2,1)}, u32[]{:S(2)}, u32[]{:S(2)}) %collective-permute-start.6) | collective-permute-done | bytes 2359328 | tf_op jit(solution)/shard_map/cond/branch_1_fun/ppermute | solution.py:17
  151.6 11.8 %gradients.1 = bf16[8,2,96,1024]{3,2,1,0:T(8,128)(2,1)} custom-call(bf16[288,4096]{1,0:T(8,128)(2,1)} %get-tuple-element.69.normed0, bf16[288,4096]{1,0:T(8,128)(2,1)} %get-tuple-element.70.normed1, bf16[288,4096]{1,0:T(8,128)(2,1)} %get-tuple-element.71.up0, bf16[288,4096]{1,0:T(8,128)(2,1)} %get-tuple-element.72.up1, ...), custom_call_target="tpu_custom_call" | custom-call | tf_op jit(solution)/shard_map/gradients/pallas_call | solution.py:204
  163.3 41.8 %reduce-scatter.2.cloned.1.call-done = bf16[1,2,96,1024]{3,2,1,0:T(8,128)(2,1)} async-done(((bf16[8,2,96,1024]{3,2,1,0:T(8,128)(2,1)}), bf16[1,2,96,1024]{3,2,1,0:T(8,128)(2,1)}) %reduce-scatter.2.cloned.1.call-update) | async-done | bytes 393232 | tf_op jit(solution)/shard_map/reduce_scatter | solution.py:300
  205.1 1.3 reshape_reduce_scatter.3
  206.4 0.5 fusion.8
  207.0 5.4 %collective-permute-start.11 = (bf16[2,96,512]{2,1,0:T(8,128)(2,1)S(1)}, bf16[2,96,512]{2,1,0:T(8,128)(2,1)S(1)}, u32[]{:S(2)}, u32[]{:S(2)}) collective-permute-start(bf16[2,96,512]{2,1,0:T(8,128)(2,1)S(1)} %select_bitcast_fusion), channel_id=1, source_target_pairs={{0,64},{64,0},{1,65},{65,1},{2,66},{66,2},{3,67},{67,3},{4,68},{68... | collective-permute-start | bytes 589832 | tf_op jit(solution)/shard_map/ppermute | solution.py:17
  212.4 1.0 collective-permute-done.11
  213.5 0.8 fusion.5
  (48 shorter events, 1.0 us)
Async XLA Ops:
  7.2 144.4 %all-reduce.2.cloned.1.call-start = ((), (), s32[]{:S(2)}) async-start(), calls=%async_computation.4 | async-start | bytes 6291456 | tf_op jit(solution)/shard_map/psum | solution.py:274
  9.4 10.1 %copy-start.6 = (s32[8,2]{0,1:T(2,128)S(1)}, s32[8,2]{0,1:T(2,128)}, u32[]{:S(2)}) copy-start(s32[8,2]{0,1:T(2,128)} %param.11) | copy-start | bytes 196
  10.7 12.2 %collective-permute-start.10 = (bf16[2,96,4096]{2,1,0:T(8,128)(2,1)}, bf16[2,96,4096]{2,1,0:T(8,128)(2,1)}, u32[]{:S(2)}, u32[]{:S(2)}) collective-permute-start(bf16[2,96,4096]{2,1,0:T(8,128)(2,1)} %fusion), channel_id=1, source_target_pairs={{0,64},{64,0},{1,65},{65,1},{2,66},{66,2},{3,67},{67,3},{4,68},{68... | collective-permute-start | bytes 4718600 | tf_op jit(solution)/shard_map/ppermute | solution.py:17
  25.2 0.9 copy-start.2
  26.0 7.9 %copy-start.4 = (bf16[1,4096]{1,0:T(2,128)(2,1)S(1)}, bf16[1,4096]{1,0:T(2,128)(2,1)}, u32[]{:S(2)}) copy-start(bf16[1,4096]{1,0:T(2,128)(2,1)} %param.13) | copy-start | bytes 24580
  26.0 8.0 %copy-start.5 = (bf16[1,4096]{1,0:T(2,128)(2,1)S(1)}, bf16[1,4096]{1,0:T(2,128)(2,1)}, u32[]{:S(2)}) copy-start(bf16[1,4096]{1,0:T(2,128)(2,1)} %param.14) | copy-start | bytes 24580
  26.0 8.1 %copy-start.3 = (s32[8,576]{1,0:T(8,128)S(1)}, s32[8,576]{1,0:T(8,128)}, u32[]{:S(2)}) copy-start(s32[8,576]{1,0:T(8,128)} %param.10) | copy-start | bytes 55300
  26.4 8.8 %copy-start = (bf16[4096,64]{0,1:T(8,128)(2,1)S(1)}, bf16[4096,64]{0,1:T(8,128)(2,1)}, u32[]{:S(2)}) copy-start(bf16[4096,64]{0,1:T(8,128)(2,1)} %param.12) | copy-start | bytes 1572868
  27.5 21.9 %all-to-all-start.2 = ((bf16[16,144,128]{2,1,0:T(8,128)(2,1)}), bf16[16,144,128]{2,1,0:T(8,128)(2,1)S(1)}, u32[]{:S(2)}, u32[]{:S(2)}) async-start(bf16[16,144,128]{2,1,0:T(8,128)(2,1)} %bitcast.14), calls=%async_computation.2 | async-start | bytes 1179648 | tf_op jit(solution)/shard_map/all_to_all | solution.py:262
  33.2 171.8 %reduce-scatter.2.cloned.1.call-start = ((), (), s32[]{:S(2)}) async-start(), calls=%async_computation.5 | async-start | bytes 3538944 | tf_op jit(solution)/shard_map/reduce_scatter | solution.py:300
  49.4 35.6 %all-to-all-start = ((bf16[16,176,128]{2,1,0:T(8,128)(2,1)}), bf16[16,176,128]{2,1,0:T(8,128)(2,1)S(1)}, u32[]{:S(2)}, u32[]{:S(2)}) async-start(bf16[16,176,128]{2,1,0:T(8,128)(2,1)} %get-tuple-element.57), calls=%async_computation | async-start | bytes 1441792 | tf_op jit(solution)/shard_map/cond/branch_1_fun/all_to_all | solution.py:277
  58.8 18.1 %collective-permute-start = (bf16[8,288,128]{2,1,0:T(8,128)(2,1)S(1)}, bf16[8,288,128]{2,1,0:T(8,128)(2,1)S(1)}, u32[]{:S(2)}, u32[]{:S(2)}) collective-permute-start(bf16[8,288,128]{2,1,0:T(8,128)(2,1)S(1)} %bitcast.68), channel_id=1, source_target_pairs={{0,2},{2,4},{4,6},{6,0},{1,3},{3,5},{5,7},{7,1},{8,10},{10,12},{12... | collective-permute-start | bytes 1769480 | tf_op jit(solution)/shard_map/cond/branch_1_fun/ppermute | solution.py:17
  62.0 16.6 %collective-permute-start.1 = (bf16[8,288,128]{2,1,0:T(8,128)(2,1)S(1)}, bf16[8,288,128]{2,1,0:T(8,128)(2,1)S(1)}, u32[]{:S(2)}, u32[]{:S(2)}) collective-permute-start(bf16[8,288,128]{2,1,0:T(8,128)(2,1)S(1)} %bitcast.69), channel_id=1, source_target_pairs={{0,6},{2,0},{4,2},{6,4},{1,7},{3,1},{5,3},{7,5},{8,14},{10,8},{12,... | collective-permute-start | bytes 1769480 | tf_op jit(solution)/shard_map/cond/branch_1_fun/ppermute | solution.py:17
  85.0 0.9 copy-start.1
  105.0 17.3 %collective-permute-start.2 = (bf16[8,288,128]{2,1,0:T(8,128)(2,1)S(1)}, bf16[8,288,128]{2,1,0:T(8,128)(2,1)S(1)}, u32[]{:S(2)}, u32[]{:S(2)}) collective-permute-start(bf16[8,288,128]{2,1,0:T(8,128)(2,1)S(1)} %all_to_all.13.refs_0_), channel_id=1, source_target_pairs={{0,2},{2,4},{4,6},{6,0},{1,3},{3,5},{5,7},{7,1},{8,10},{10,12},{12... | collective-permute-start | bytes 1769480 | tf_op jit(solution)/shard_map/cond/branch_1_fun/ppermute | solution.py:17
  108.2 16.1 %collective-permute-start.3 = (bf16[8,288,128]{2,1,0:T(8,128)(2,1)S(1)}, bf16[8,288,128]{2,1,0:T(8,128)(2,1)S(1)}, u32[]{:S(2)}, u32[]{:S(2)}) collective-permute-start(bf16[8,288,128]{2,1,0:T(8,128)(2,1)S(1)} %all_to_all.13.refs_0_), channel_id=1, source_target_pairs={{0,6},{2,0},{4,2},{6,4},{1,7},{3,1},{5,3},{7,5},{8,14},{10,8},{12,... | collective-permute-start | bytes 1769480 | tf_op jit(solution)/shard_map/cond/branch_1_fun/ppermute | solution.py:17
  115.8 13.2 %collective-permute-start.7 = (bf16[4,288,128]{2,1,0:T(8,128)(2,1)S(1)}, bf16[4,288,128]{2,1,0:T(8,128)(2,1)S(1)}, u32[]{:S(2)}, u32[]{:S(2)}) collective-permute-start(bf16[4,288,128]{2,1,0:T(8,128)(2,1)S(1)} %slice.52), channel_id=1, source_target_pairs={{0,2},{2,4},{4,6},{6,0},{1,3},{3,5},{5,7},{7,1},{8,10},{10,12},{12... | collective-permute-start | bytes 884744 | tf_op jit(solution)/shard_map/cond/branch_1_fun/ppermute | solution.py:17
  117.8 11.2 %collective-permute-start.8 = (bf16[4,288,128]{2,1,0:T(8,128)(2,1)S(1)}, bf16[4,288,128]{2,1,0:T(8,128)(2,1)S(1)}, u32[]{:S(2)}, u32[]{:S(2)}) collective-permute-start(bf16[4,288,128]{2,1,0:T(8,128)(2,1)S(1)} %slice.53), channel_id=1, source_target_pairs={{0,6},{2,0},{4,2},{6,4},{1,7},{3,1},{5,3},{7,5},{8,14},{10,8},{12,... | collective-permute-start | bytes 884744 | tf_op jit(solution)/shard_map/cond/branch_1_fun/ppermute | solution.py:17
  122.4 17.6 %collective-permute-start.4 = (bf16[4,288,128]{2,1,0:T(8,128)(2,1)S(1)}, bf16[4,288,128]{2,1,0:T(8,128)(2,1)S(1)}, u32[]{:S(2)}, u32[]{:S(2)}) collective-permute-start(bf16[4,288,128]{2,1,0:T(8,128)(2,1)S(1)} %slice.77), channel_id=1, source_target_pairs={{0,2},{2,4},{4,6},{6,0},{1,3},{3,5},{5,7},{7,1},{8,10},{10,12},{12... | collective-permute-start | bytes 884744 | tf_op jit(solution)/shard_map/cond/branch_1_fun/ppermute | solution.py:17
  124.3 15.6 %collective-permute-start.5 = (bf16[4,288,128]{2,1,0:T(8,128)(2,1)S(1)}, bf16[4,288,128]{2,1,0:T(8,128)(2,1)S(1)}, u32[]{:S(2)}, u32[]{:S(2)}) collective-permute-start(bf16[4,288,128]{2,1,0:T(8,128)(2,1)S(1)} %slice.78), channel_id=1, source_target_pairs={{0,6},{2,0},{4,2},{6,4},{1,7},{3,1},{5,3},{7,5},{8,14},{10,8},{12,... | collective-permute-start | bytes 884744 | tf_op jit(solution)/shard_map/cond/branch_1_fun/ppermute | solution.py:17
  132.2 14.5 %collective-permute-start.9 = (bf16[288,4096]{1,0:T(8,128)(2,1)}, bf16[288,4096]{1,0:T(8,128)(2,1)}, u32[]{:S(2)}, u32[]{:S(2)}) collective-permute-start(bf16[288,4096]{1,0:T(8,128)(2,1)} %merge.1), channel_id=1, source_target_pairs={{0,64},{64,0},{1,65},{65,1},{2,66},{66,2},{3,67},{67,3},{4,68},{68... | collective-permute-start | bytes 7077896 | tf_op jit(solution)/shard_map/cond/branch_1_fun/ppermute | solution.py:17
  144.8 6.8 %collective-permute-start.6 = (bf16[288,4096]{1,0:T(8,128)(2,1)}, bf16[288,4096]{1,0:T(8,128)(2,1)}, u32[]{:S(2)}, u32[]{:S(2)}) collective-permute-start(bf16[288,4096]{1,0:T(8,128)(2,1)} %norm.1), channel_id=1, source_target_pairs={{0,64},{64,0},{1,65},{65,1},{2,66},{66,2},{3,67},{67,3},{4,68},{68... | collective-permute-start | bytes 7077896 | tf_op jit(solution)/shard_map/cond/branch_1_fun/ppermute | solution.py:17
  207.0 6.4 %collective-permute-start.11 = (bf16[2,96,512]{2,1,0:T(8,128)(2,1)S(1)}, bf16[2,96,512]{2,1,0:T(8,128)(2,1)S(1)}, u32[]{:S(2)}, u32[]{:S(2)}) collective-permute-start(bf16[2,96,512]{2,1,0:T(8,128)(2,1)S(1)} %select_bitcast_fusion), channel_id=1, source_target_pairs={{0,64},{64,0},{1,65},{65,1},{2,66},{66,2},{3,67},{67,3},{4,68},{68... | collective-permute-start | bytes 589832 | tf_op jit(solution)/shard_map/ppermute | solution.py:17
Sparse Core Ops, SparseCore 0:
  25.3 110.7 all-reduce.1
  163.5 41.5 reduce-scatter.1

commit v2 on v1

--- a/solution.py
+++ b/solution.py
@@ -17,15 +17,16 @@
     return lax.ppermute(value, axis, [(i, (i + by) % size) for i in range(size)])
 
 
-def lookup_kernel(low_ref, high_ref, table_ref, out_ref, groups):
-    width, vocab = table_ref.shape
-    count = 8
-    depth = vocab // count
+def lookup_kernel(low_ref, high_ref, own_ref, other_ref, out_ref, groups):
+    width = own_ref.shape[0]
+    count, depth = 8, groups.shape[1]
 
     @pl.when(pl.program_id(0) == 0)
     def _():
-        for k in range(count):
-            groups[k * width:(k + 1) * width, :] = table_ref[:, k * depth:(k + 1) * depth]
+        for b, ref in enumerate((own_ref, other_ref)):
+            for k in range(count):
+                base = (b * count + k) * width
+                groups[base:base + width, :] = ref[:, k * depth:(k + 1) * depth]
 
     rows = out_ref.shape[0]
     place = lax.broadcasted_iota(jnp.int32, (rows, depth), 1)
@@ -41,7 +42,7 @@
         )
         pair = jnp.right_shift(group, 1)
         found = jnp.zeros((rows, 2 * width), f32)
-        for j in range(count // 2):
+        for j in range(count):
             found += jnp.where(pair == j, picked[:, 2 * j * width:2 * (j + 1) * width], 0.0)
         turned = pltpu.roll(found, width, 1)
         found = jnp.where(jnp.bitwise_and(group, 1) == side, found, turned)
@@ -49,24 +50,25 @@
     out_ref[...] = total.astype(bf16)
 
 
-def lookup(low, high, table):
+def lookup(low, high, own, other, depth):
     rows = low.shape[0]
-    width, vocab = table.shape
-    step = rows // 4
+    width, lanes = own.shape
+    step = rows // 2
     return pl.pallas_call(
         lookup_kernel,
-        grid=(4,),
+        grid=(2,),
         in_specs=[
             pl.BlockSpec((step, 1), lambda i: (i, 0)),
             pl.BlockSpec((step, 1), lambda i: (i, 0)),
-            pl.BlockSpec((width, vocab), lambda i: (0, 0)),
+            pl.BlockSpec((width, lanes), lambda i: (0, 0)),
+            pl.BlockSpec((width, lanes), lambda i: (0, 0)),
         ],
         out_specs=pl.BlockSpec((step, 2 * width), lambda i: (i, 0)),
         out_shape=jax.ShapeDtypeStruct((rows, 2 * width), bf16),
-        scratch_shapes=[pltpu.VMEM((8 * width, vocab // 8), bf16)],
+        scratch_shapes=[pltpu.VMEM((16 * width, depth), bf16)],
         compiler_params=pltpu.CompilerParams(vmem_limit_bytes=32 * MIB),
         name="lookup",
-    )(low, high, table)
+    )(low, high, own, other)
 
 
 def laid_out(info_ref, blocks):
@@ -259,42 +261,46 @@
     cot = cotangent[0].reshape(2, 2, half // 2, cols)
     cot = jnp.concatenate([cot[:, 0], cot[:, 1]], axis=2)
     cot = jnp.broadcast_to(cot, (8,) + cot.shape).reshape((16,) + cot.shape[1:])
-    cot = lax.all_to_all(cot, ("z", "yl"), 0, 0).reshape(8, half, 2 * cols)
-
-    local = (token_ids - position * vocab_block).reshape(replicas * 2, 2, half // 2)
-    low = local[:, 0].reshape(-1, 1)
-    high = local[:, 1].reshape(-1, 1)
-    rows = lookup(low, high, embedding.T).reshape(2 * replicas, half // 2, 2 * cols)
+
     vectors = jnp.concatenate([ln_gain.reshape(-1, 2 * cols), ln_bias.reshape(-1, 2 * cols)])
     share = vectors.shape[0] // 2
-    vectors = lax.dynamic_slice_in_dim(vectors, yl * share, share, 0)
-    sent = jnp.concatenate(
-        [rows, jnp.broadcast_to(vectors, (2 * replicas,) + vectors.shape)], axis=1
-    )
+    held = jnp.concatenate([embedding.T, vectors], axis=1)
+    ids = token_ids.reshape(4, 2, 2, 2, half // 2)
+    ids = jnp.where(core == 0, ids[:, 0], ids[:, 1])
+    local = jnp.bitwise_xor(ids - yh * 2 * vocab_block, core * vocab_block)
+    low = local[:, :, 0].reshape(-1, 1)
+    high = local[:, :, 1].reshape(-1, 1)
     weights = lax.psum(spread, ("yh", "yl"))
 
-    def slots(sent, cot):
-        got = lax.all_to_all(sent, ("yh", "core", "yl"), 0, 0)
+    def slots(low, high, held, cot):
+        cot = lax.all_to_all(cot, ("z", "yl"), 0, 0).reshape(8, half, 2 * cols)
+        swapped = shift(held, "core", 2, 1)
+        rows = lookup(low, high, held, swapped, vocab_block // 8).reshape(8, half // 2, 2 * cols)
+        vectors = jnp.where(core == source % 2, held[:, vocab_block:], swapped[:, vocab_block:])
+        vectors = lax.dynamic_slice_in_dim(vectors, yl * share, share, 0)
+        sent = jnp.concatenate([rows, jnp.broadcast_to(vectors, (8,) + vectors.shape)], axis=1)
+        sent, cot = lax.optimization_barrier((sent, cot))
+        got = lax.all_to_all(sent, ("yh", "yl"), 0, 0)
         info = jnp.stack([x, live, yl * half]).astype(jnp.int32)
         got, sides = lax.optimization_barrier((got, gather_x(cot)))
-        upstream = assemble(merge_kernel, "merge", info, (cot, *sides, *gather_far(*sides)))
-        upstream_other = shift(upstream, "core", 2, 1)
-        got = got.reshape((replicas, 2) + got.shape[1:])
+        far = gather_far(*sides)
+        got = got.reshape((4, 2) + got.shape[1:])
         emb = jnp.sum(got[:, :, : half // 2].astype(f32), axis=0).astype(bf16)
         emb = emb.reshape(half, 2 * cols)
-        root = lax.dynamic_index_in_dim(got[:, :, half // 2 :], source, 0, keepdims=False)
+        root = lax.dynamic_index_in_dim(got[:, :, half // 2 :], source // 2, 0, keepdims=False)
         root = root.reshape(2, -1, 2 * cols).astype(f32)
-        emb = gather_z(emb)
-        sides = gather_x(emb)
+        emb, far = lax.optimization_barrier((gather_z(emb), far))
+        upstream = assemble(merge_kernel, "merge", info, (cot, *sides, *far))
+        sides, upstream = lax.optimization_barrier((gather_x(emb), upstream))
         blocks = (emb, *sides, *gather_far(*sides))
         normed = assemble(norm_kernel, "norm", info, blocks, (root[0], root[1]))
-        return normed, shift(normed, "core", 2, 1), upstream, upstream_other
-
-    def nothing(sent, cot):
+        return normed, shift(normed, "core", 2, 1), upstream, shift(upstream, "core", 2, 1)
+
+    def nothing(low, high, held, cot):
         return (jnp.zeros((half, width), bf16),) * 4
 
     normed, normed_other, upstream, upstream_other = lax.cond(
-        source < replicas, slots, nothing, sent, cot
+        source < replicas, slots, nothing, low, high, held, cot
     )
     terms = gradients(normed, normed_other, upstream, upstream_other, weights)
     sums = lax.psum_scatter(terms, ("yh", "yl"), scatter_dimension=0)

time: 222 us -> 215 us (0.968)
  blocking collectives: 19.1 us -> 0 us
  waiting for transfers between devices: 75.4 us -> 82.2 us
  starting transfers between devices: 65.1 us -> 67.7 us
    all_to_all x1 -> x0, blocking collectives: 19.1 us -> none  [gather_z(): lax.all_to_all(jnp.broadcast_to(block, (depth,) + block.shape), 'z', 0, 0)]
    ppermute x12 -> x13, waiting for transfers between devices: 19.1 us -> 25.4 us  [shift(): lax.ppermute(value, axis, [(i, (i + by) % size) for i in range(size)])]
    ppermute x12 -> x13, starting transfers between devices: 49.8 us -> 52.4 us  [shift(): lax.ppermute(value, axis, [(i, (i + by) % size) for i in range(size)])]
    cond x2 -> x12, local copies, waits for them, and re-layouts: 0.8 us -> 3.34 us
    all_to_all x2 -> x3, waiting for transfers between devices: 14.5 us -> 14.3 us  [the longest x1 8.91 us: slots(): cot = lax.all_to_all(cot, ('z', 'yl'), 0, 0).reshape(8, half, 2 * cols)]
    all_to_all x2 -> x3, starting transfers between devices: 15.2 us -> 15.2 us  [the longest x1 5.92 us: slots(): got = lax.all_to_all(sent, ('yh', 'yl'), 0, 0)]
  transfers between devices with their start and end apart: 16 -> 18, of which waited for: 7 -> 11; matrix products, arithmetic and copies ran while one was open for 3% -> 3% of each run, Pallas kernels for 6% -> 6%
where the time goes in v2:
time: 215 us; the launch traced here: 214 us
  waiting for transfers between devices  82.2 us (38%)
  starting transfers between devices  67.7 us (31%)
  Pallas kernels  23.7 us (11%)
  between operations  17.4 us (8%)
  other arithmetic  10.4 us (5%)
  local copies, waits for them, and re-layouts  9.86 us (5%)
  loops' own time  2.84 us (1%)
    ppermute x13, starting transfers between devices, shift(): lax.ppermute(value, axis, [(i, (i + by) % size) for i in range(size)])  52.4 us
    reduce_scatter x1, waiting for transfers between devices, on_device(): sums = lax.psum_scatter(terms, ('yh', 'yl'), scatter_dimension=0)  42.5 us
    ppermute x13, waiting for transfers between devices, shift(): lax.ppermute(value, axis, [(i, (i + by) % size) for i in range(size)])  25.4 us
    pallas_call x1, Pallas kernels, gradients(): pl.pallas_call(gradient_kernel, in_specs=[pl.BlockSpec(memory_space=pltpu...  11.8 us
    all_to_all x1, waiting for transfers between devices, slots(): cot = lax.all_to_all(cot, ('z', 'yl'), 0, 0).reshape(8, half, 2 * cols)  8.91 us
    pallas_call x2, Pallas kernels, assemble(): pl.pallas_call(kernel, in_specs=[pl.BlockSpec(memory_space=pltpu.SMEM)] +...  8.05 us
    all_to_all x1, starting transfers between devices, slots(): got = lax.all_to_all(sent, ('yh', 'yl'), 0, 0)  5.92 us
    all_to_all x1, starting transfers between devices, slots(): cot = lax.all_to_all(cot, ('z', 'yl'), 0, 0).reshape(8, half, 2 * cols)  5.78 us
  transfers between devices with their start and end apart: 18, of which 11 were waited for; matrix products, arithmetic and copies ran while one was open for 3% of the time, Pallas kernels for 6%

profile of v2, /device:TPU:1, one launch (start us, length us, event | category | flops | bytes accessed | tf_op | source)
XLA Modules:
  0.0 214.1 jit_solution(7844258780232105601)
XLA Ops:
  7.2 2.2 %pad_maximum_fusion.1 = bf16[2,192,4096]{2,1,0:T(8,128)(2,1)S(1)} fusion(bf16[1,192,4096]{2,1,0:T(8,128)(2,1)} %param.16, bf16[1,192,4096]{2,1,0:T(8,128)(2,1)} %param.15), kind=kLoop, calls=%fused_computation.12 | loop fusion | flops 1572864 | bytes 6291456 | tf_op jit(solution)/shard_map/stack | solution.py:253
  9.4 1.4 fusion.3
  10.8 8.8 %collective-permute-start.11 = (bf16[2,96,4096]{2,1,0:T(8,128)(2,1)}, bf16[2,96,4096]{2,1,0:T(8,128)(2,1)}, u32[]{:S(2)}, u32[]{:S(2)}) collective-permute-start(bf16[2,96,4096]{2,1,0:T(8,128)(2,1)} %fusion.3), channel_id=1, source_target_pairs={{0,64},{64,0},{1,65},{65,1},{2,66},{66,2},{3,67},{67,3},{4,68},{68... | collective-permute-start | bytes 4718600 | tf_op jit(solution)/shard_map/ppermute | solution.py:17
  19.6 0.6 fusion.9
  22.9 1.6 fusion.5
  24.5 2.0 bitcast_select_fusion.1
  27.9 115.8 %conditional.1 = (bf16[288,4096]{1,0:T(8,128)(2,1)}, bf16[288,4096]{1,0:T(8,128)(2,1)}, bf16[288,4096]{1,0:T(8,128)(2,1)}, bf16[288,4096]{1,0:T(8,128)(2,1)}) conditional(s32[]{:T(128)} %convert_element_type.9, () %tuple.42, (s32[]{:T(128)}, s32[8,2]{0,1:T(2,128)}, s32[]{:T(128)}, s32[]{:T(128)}, s32[]{:T(128)}, /*index=5*/s32[]{:T(128)}, pred[]{:T(512)}, ...), branch_computations={%region_1.2_spmd, %region_2.4_spmd} | conditional | flops 850809 | bytes 51413448 | solution.py:302
  28.0 0.9 broadcast_in_dim.32
  29.0 5.8 %all-to-all-start = ((bf16[16,144,128]{2,1,0:T(8,128)(2,1)}), bf16[16,144,128]{2,1,0:T(8,128)(2,1)S(1)}, u32[]{:S(2)}, u32[]{:S(2)}) async-start(bf16[16,144,128]{2,1,0:T(8,128)(2,1)} %bitcast.6), calls=%async_computation | async-start | bytes 1179648 | tf_op jit(solution)/shard_map/cond/branch_1_fun/all_to_all | solution.py:276
  34.7 1.9 collective-permute-start
  39.3 3.9 %lookup.1 = bf16[1152,128]{1,0:T(8,128)(2,1)S(1)} custom-call(s32[1152,1]{1,0:T(8,128)S(1)} %reshape_squeeze.12.low_ref, s32[1152,1]{1,0:T(8,128)S(1)} %reshape_squeeze.13.high_ref, bf16[64,4224]{1,0:T(8,128)(2,1)S(1)} %get-tuple-element.96.own_ref, bf16[64,4224]{1,0:T(8,128)(2,1)S(1)} %collective-permute-done.other_ref), custom_call_target="tpu_custom_call" | custom-call | tf_op jit(solution)/shard_map/cond/branch_1_fun/lookup/pallas_call | solution.py:57
  43.2 0.7 pad_maximum_fusion
  44.0 8.9 %all-to-all-done = bf16[16,144,128]{2,1,0:T(8,128)(2,1)S(1)} async-done(((bf16[16,144,128]{2,1,0:T(8,128)(2,1)}), bf16[16,144,128]{2,1,0:T(8,128)(2,1)S(1)}, u32[]{:S(2)}, u32[]{:S(2)}) %all-to-all-start) | async-done | bytes 589856 | tf_op jit(solution)/shard_map/cond/branch_1_fun/all_to_all | solution.py:276
  52.9 5.9 %all-to-all-start.1 = ((bf16[8,176,128]{2,1,0:T(8,128)(2,1)}), bf16[8,176,128]{2,1,0:T(8,128)(2,1)S(1)}, u32[]{:S(2)}, u32[]{:S(2)}) async-start(bf16[8,176,128]{2,1,0:T(8,128)(2,1)} %pad_maximum_fusion), calls=%async_computation.1 | async-start | bytes 720896 | tf_op jit(solution)/shard_map/cond/branch_1_fun/all_to_all | solution.py:283
  58.8 3.1 %collective-permute-start.1 = (bf16[8,288,128]{2,1,0:T(8,128)(2,1)S(1)}, bf16[8,288,128]{2,1,0:T(8,128)(2,1)S(1)}, u32[]{:S(2)}, u32[]{:S(2)}) collective-permute-start(bf16[8,288,128]{2,1,0:T(8,128)(2,1)S(1)} %bitcast.68), channel_id=1, source_target_pairs={{0,2},{2,4},{4,6},{6,0},{1,3},{3,5},{5,7},{7,1},{8,10},{10,12},{12... | collective-permute-start | bytes 1769480 | tf_op jit(solution)/shard_map/cond/branch_1_fun/ppermute | solution.py:17
  61.9 3.4 %collective-permute-start.2 = (bf16[8,288,128]{2,1,0:T(8,128)(2,1)S(1)}, bf16[8,288,128]{2,1,0:T(8,128)(2,1)S(1)}, u32[]{:S(2)}, u32[]{:S(2)}) collective-permute-start(bf16[8,288,128]{2,1,0:T(8,128)(2,1)S(1)} %bitcast.69), channel_id=1, source_target_pairs={{0,6},{2,0},{4,2},{6,4},{1,7},{3,1},{5,3},{7,5},{8,14},{10,8},{12,... | collective-permute-start | bytes 1769480 | tf_op jit(solution)/shard_map/cond/branch_1_fun/ppermute | solution.py:17
  65.3 10.9 %collective-permute-done.1.refs_1_ = bf16[8,288,128]{2,1,0:T(8,128)(2,1)S(1)} collective-permute-done((bf16[8,288,128]{2,1,0:T(8,128)(2,1)S(1)}, bf16[8,288,128]{2,1,0:T(8,128)(2,1)S(1)}, u32[]{:S(2)}, u32[]{:S(2)}) %collective-permute-start.1) | collective-permute-done | bytes 589856 | tf_op jit(solution)/shard_map/cond/branch_1_fun/ppermute | solution.py:17
  76.2 1.6 collective-permute-done.2.refs_2_
  77.9 0.9 broadcast_in_dim.33
  78.8 3.5 %all-to-all-start.2 = ((bf16[8,288,128]{2,1,0:T(8,128)(2,1)}), bf16[8,288,128]{2,1,0:T(8,128)(2,1)S(1)}, u32[]{:S(2)}, u32[]{:S(2)}) async-start(bf16[8,288,128]{2,1,0:T(8,128)(2,1)} %broadcast_in_dim.33), calls=%async_computation.2 | async-start | bytes 1179648 | tf_op jit(solution)/shard_map/cond/branch_1_fun/all_to_all | solution.py:223
  82.4 3.1 %collective-permute-start.3 = (bf16[4,288,128]{2,1,0:T(8,128)(2,1)S(1)}, bf16[4,288,128]{2,1,0:T(8,128)(2,1)S(1)}, u32[]{:S(2)}, u32[]{:S(2)}) collective-permute-start(bf16[4,288,128]{2,1,0:T(8,128)(2,1)S(1)} %slice.62), channel_id=1, source_target_pairs={{0,2},{2,4},{4,6},{6,0},{1,3},{3,5},{5,7},{7,1},{8,10},{10,12},{12... | collective-permute-start | bytes 884744 | tf_op jit(solution)/shard_map/cond/branch_1_fun/ppermute | solution.py:17
  85.5 3.4 %collective-permute-start.4 = (bf16[4,288,128]{2,1,0:T(8,128)(2,1)S(1)}, bf16[4,288,128]{2,1,0:T(8,128)(2,1)S(1)}, u32[]{:S(2)}, u32[]{:S(2)}) collective-permute-start(bf16[4,288,128]{2,1,0:T(8,128)(2,1)S(1)} %slice.63), channel_id=1, source_target_pairs={{0,6},{2,0},{4,2},{6,4},{1,7},{3,1},{5,3},{7,5},{8,14},{10,8},{12,... | collective-permute-start | bytes 884744 | tf_op jit(solution)/shard_map/cond/branch_1_fun/ppermute | solution.py:17
  88.9 3.4 %collective-permute-done.3.refs_3_ = bf16[4,288,128]{2,1,0:T(8,128)(2,1)S(1)} collective-permute-done((bf16[4,288,128]{2,1,0:T(8,128)(2,1)S(1)}, bf16[4,288,128]{2,1,0:T(8,128)(2,1)S(1)}, u32[]{:S(2)}, u32[]{:S(2)}) %collective-permute-start.3) | collective-permute-done | bytes 294944 | tf_op jit(solution)/shard_map/cond/branch_1_fun/ppermute | solution.py:17
  92.3 0.7 copy-done
  93.0 0.9 collective-permute-done.4.refs_4_
  93.9 0.7 copy-done.2
  94.6 5.4 %all-to-all-done.2.refs_0_ = bf16[8,288,128]{2,1,0:T(8,128)(2,1)S(1)} async-done(((bf16[8,288,128]{2,1,0:T(8,128)(2,1)}), bf16[8,288,128]{2,1,0:T(8,128)(2,1)S(1)}, u32[]{:S(2)}, u32[]{:S(2)}) %all-to-all-start.2) | async-done | bytes 589856 | tf_op jit(solution)/shard_map/cond/branch_1_fun/all_to_all | solution.py:223
  100.0 3.1 %collective-permute-start.5 = (bf16[8,288,128]{2,1,0:T(8,128)(2,1)S(1)}, bf16[8,288,128]{2,1,0:T(8,128)(2,1)S(1)}, u32[]{:S(2)}, u32[]{:S(2)}) collective-permute-start(bf16[8,288,128]{2,1,0:T(8,128)(2,1)S(1)} %all-to-all-done.2.refs_0_), channel_id=1, source_target_pairs={{0,2},{2,4},{4,6},{6,0},{1,3},{3,5},{5,7},{7,1},{8,10},{10,12},{12... | collective-permute-start | bytes 1769480 | tf_op jit(solution)/shard_map/cond/branch_1_fun/ppermute | solution.py:17
  103.1 3.4 %collective-permute-start.6 = (bf16[8,288,128]{2,1,0:T(8,128)(2,1)S(1)}, bf16[8,288,128]{2,1,0:T(8,128)(2,1)S(1)}, u32[]{:S(2)}, u32[]{:S(2)}) collective-permute-start(bf16[8,288,128]{2,1,0:T(8,128)(2,1)S(1)} %all-to-all-done.2.refs_0_), channel_id=1, source_target_pairs={{0,6},{2,0},{4,2},{6,4},{1,7},{3,1},{5,3},{7,5},{8,14},{10,8},{12,... | collective-permute-start | bytes 1769480 | tf_op jit(solution)/shard_map/cond/branch_1_fun/ppermute | solution.py:17
  107.8 0.7 pad_add_fusion.info_ref
  108.5 0.8 slice.93
  109.3 1.0 copy-done.1
  110.3 1.0 copy-done.3
  111.3 3.2 %merge.1 = bf16[288,4096]{1,0:T(8,128)(2,1)} custom-call(s32[3]{0:T(128)S(1)} %pad_add_fusion.info_ref, bf16[8,288,128]{2,1,0:T(8,128)(2,1)S(1)} %bitcast.70, bf16[8,288,128]{2,1,0:T(8,128)(2,1)S(1)} %collective-permute-done.1.refs_1_, bf16[8,288,128]{2,1,0:T(8,128)(2,1)S(1)} %collective-permute-done.2.refs_2_, bf16[4,288,128]{2,1,0:T(8,128)(2,1)S(1)} %copy-done.1, ...), custom_call_target="tpu_custom_call" | custom-call | tf_op jit(solution)/shard_map/cond/branch_1_fun/merge/pallas_call | solution.py:146
  114.5 1.4 collective-permute-done.5.refs_1_
  115.9 1.6 collective-permute-done.6.refs_2_
  117.6 2.8 %collective-permute-start.7 = (bf16[4,288,128]{2,1,0:T(8,128)(2,1)S(1)}, bf16[4,288,128]{2,1,0:T(8,128)(2,1)S(1)}, u32[]{:S(2)}, u32[]{:S(2)}) collective-permute-start(bf16[4,288,128]{2,1,0:T(8,128)(2,1)S(1)} %slice.64), channel_id=1, source_target_pairs={{0,2},{2,4},{4,6},{6,0},{1,3},{3,5},{5,7},{7,1},{8,10},{10,12},{12... | collective-permute-start | bytes 884744 | tf_op jit(solution)/shard_map/cond/branch_1_fun/ppermute | solution.py:17
  120.4 3.7 %collective-permute-start.8 = (bf16[4,288,128]{2,1,0:T(8,128)(2,1)S(1)}, bf16[4,288,128]{2,1,0:T(8,128)(2,1)S(1)}, u32[]{:S(2)}, u32[]{:S(2)}) collective-permute-start(bf16[4,288,128]{2,1,0:T(8,128)(2,1)S(1)} %slice.65), channel_id=1, source_target_pairs={{0,6},{2,0},{4,2},{6,4},{1,7},{3,1},{5,3},{7,5},{8,14},{10,8},{12,... | collective-permute-start | bytes 884744 | tf_op jit(solution)/shard_map/cond/branch_1_fun/ppermute | solution.py:17
  124.2 5.7 %collective-permute-start.10 = (bf16[288,4096]{1,0:T(8,128)(2,1)}, bf16[288,4096]{1,0:T(8,128)(2,1)}, u32[]{:S(2)}, u32[]{:S(2)}) collective-permute-start(bf16[288,4096]{1,0:T(8,128)(2,1)} %merge.1), channel_id=1, source_target_pairs={{0,64},{64,0},{1,65},{65,1},{2,66},{66,2},{3,67},{67,3},{4,68},{68... | collective-permute-start | bytes 7077896 | tf_op jit(solution)/shard_map/cond/branch_1_fun/ppermute | solution.py:17
  129.8 4.8 %norm.1 = bf16[288,4096]{1,0:T(8,128)(2,1)} custom-call(s32[3]{0:T(128)S(1)} %pad_add_fusion.info_ref, bf16[8,288,128]{2,1,0:T(8,128)(2,1)S(1)} %all-to-all-done.2.refs_0_, bf16[8,288,128]{2,1,0:T(8,128)(2,1)S(1)} %collective-permute-done.5.refs_1_, bf16[8,288,128]{2,1,0:T(8,128)(2,1)S(1)} %collective-permute-done.6.refs_2_, ...), custom_call_target="tpu_custom_call" | custom-call | tf_op jit(solution)/shard_map/cond/branch_1_fun/norm/pallas_call | solution.py:146
  134.7 4.6 %collective-permute-start.9 = (bf16[288,4096]{1,0:T(8,128)(2,1)}, bf16[288,4096]{1,0:T(8,128)(2,1)}, u32[]{:S(2)}, u32[]{:S(2)}) collective-permute-start(bf16[288,4096]{1,0:T(8,128)(2,1)} %norm.1), channel_id=1, source_target_pairs={{0,64},{64,0},{1,65},{65,1},{2,66},{66,2},{3,67},{67,3},{4,68},{68... | collective-permute-start | bytes 7077896 | tf_op jit(solution)/shard_map/cond/branch_1_fun/ppermute | solution.py:17
  139.3 4.5 %collective-permute-done.9 = bf16[288,4096]{1,0:T(8,128)(2,1)} collective-permute-done((bf16[288,4096]{1,0:T(8,128)(2,1)}, bf16[288,4096]{1,0:T(8,128)(2,1)}, u32[]{:S(2)}, u32[]{:S(2)}) %collective-permute-start.9) | collective-permute-done | bytes 2359328 | tf_op jit(solution)/shard_map/cond/branch_1_fun/ppermute | solution.py:17
  143.7 11.8 %gradients.1 = bf16[8,2,96,1024]{3,2,1,0:T(8,128)(2,1)} custom-call(bf16[288,4096]{1,0:T(8,128)(2,1)} %get-tuple-element.117.normed0, bf16[288,4096]{1,0:T(8,128)(2,1)} %get-tuple-element.118.normed1, bf16[288,4096]{1,0:T(8,128)(2,1)} %get-tuple-element.119.up0, bf16[288,4096]{1,0:T(8,128)(2,1)} %get-tuple-element.120.up1, ...), custom_call_target="tpu_custom_call" | custom-call | tf_op jit(solution)/shard_map/gradients/pallas_call | solution.py:206
  155.5 42.5 %reduce-scatter.2.cloned.1.call-done = bf16[1,2,96,1024]{3,2,1,0:T(8,128)(2,1)} async-done(((bf16[8,2,96,1024]{3,2,1,0:T(8,128)(2,1)}), bf16[1,2,96,1024]{3,2,1,0:T(8,128)(2,1)}) %reduce-scatter.2.cloned.1.call-update) | async-done | bytes 393232 | tf_op jit(solution)/shard_map/reduce_scatter | solution.py:306
  198.0 1.3 reshape_reduce_scatter.3
  199.9 5.4 %collective-permute-start.12 = (bf16[2,96,512]{2,1,0:T(8,128)(2,1)S(1)}, bf16[2,96,512]{2,1,0:T(8,128)(2,1)S(1)}, u32[]{:S(2)}, u32[]{:S(2)}) collective-permute-start(bf16[2,96,512]{2,1,0:T(8,128)(2,1)S(1)} %select_bitcast_fusion), channel_id=1, source_target_pairs={{0,64},{64,0},{1,65},{65,1},{2,66},{66,2},{3,67},{67,3},{4,68},{68... | collective-permute-start | bytes 589832 | tf_op jit(solution)/shard_map/ppermute | solution.py:17
  205.3 1.0 collective-permute-done.12
  206.4 0.8 fusion.8
  (65 shorter events, 3.1 us)
Async XLA Ops:
  7.2 136.6 %all-reduce.2.cloned.1.call-start = ((), (), s32[]{:S(2)}) async-start(), calls=%async_computation.4 | async-start | bytes 6291456 | tf_op jit(solution)/shard_map/psum | solution.py:273
  9.4 10.2 %copy-start.10 = (s32[8,2]{0,1:T(2,128)S(1)}, s32[8,2]{0,1:T(2,128)}, u32[]{:S(2)}) copy-start(s32[8,2]{0,1:T(2,128)} %param.11) | copy-start | bytes 196
  10.8 12.1 %collective-permute-start.11 = (bf16[2,96,4096]{2,1,0:T(8,128)(2,1)}, bf16[2,96,4096]{2,1,0:T(8,128)(2,1)}, u32[]{:S(2)}, u32[]{:S(2)}) collective-permute-start(bf16[2,96,4096]{2,1,0:T(8,128)(2,1)} %fusion.3), channel_id=1, source_target_pairs={{0,64},{64,0},{1,65},{65,1},{2,66},{66,2},{3,67},{67,3},{4,68},{68... | collective-permute-start | bytes 4718600 | tf_op jit(solution)/shard_map/ppermute | solution.py:17
  26.5 0.8 copy-start.8
  26.5 0.9 copy-start.9
  26.5 0.9 copy-start.6
  26.5 1.3 copy-start.5
  26.5 1.4 copy-start.7
  26.5 171.4 %reduce-scatter.2.cloned.1.call-start = ((), (), s32[]{:S(2)}) async-start(), calls=%async_computation.5 | async-start | bytes 3538944 | tf_op jit(solution)/shard_map/reduce_scatter | solution.py:306
  29.0 23.9 %all-to-all-start = ((bf16[16,144,128]{2,1,0:T(8,128)(2,1)}), bf16[16,144,128]{2,1,0:T(8,128)(2,1)S(1)}, u32[]{:S(2)}, u32[]{:S(2)}) async-start(bf16[16,144,128]{2,1,0:T(8,128)(2,1)} %bitcast.6), calls=%async_computation | async-start | bytes 1179648 | tf_op jit(solution)/shard_map/cond/branch_1_fun/all_to_all | solution.py:276
  34.7 4.5 %collective-permute-start = (bf16[64,4224]{1,0:T(8,128)(2,1)S(1)}, bf16[64,4224]{1,0:T(8,128)(2,1)S(1)}, u32[]{:S(2)}, u32[]{:S(2)}) collective-permute-start(bf16[64,4224]{1,0:T(8,128)(2,1)S(1)} %get-tuple-element.96.own_ref), channel_id=1, source_target_pairs={{0,64},{64,0},{1,65},{65,1},{2,66},{66,2},{3,67},{67,3},{4,68},{68... | collective-permute-start | bytes 1622024 | tf_op jit(solution)/shard_map/cond/branch_1_fun/ppermute | solution.py:17
  43.2 64.0 %copy-start.11 = (s32[8,2]{0,1:T(2,128)S(1)}, s32[8,2]{0,1:T(2,128)}, u32[]{:S(2)}) copy-start(s32[8,2]{0,1:T(2,128)} %get-tuple-element.89) | copy-start | bytes 196 | tf_op jit(solution)/shard_map/cond
  52.9 25.0 %all-to-all-start.1 = ((bf16[8,176,128]{2,1,0:T(8,128)(2,1)}), bf16[8,176,128]{2,1,0:T(8,128)(2,1)S(1)}, u32[]{:S(2)}, u32[]{:S(2)}) async-start(bf16[8,176,128]{2,1,0:T(8,128)(2,1)} %pad_maximum_fusion), calls=%async_computation.1 | async-start | bytes 720896 | tf_op jit(solution)/shard_map/cond/branch_1_fun/all_to_all | solution.py:283
  58.8 17.4 %collective-permute-start.1 = (bf16[8,288,128]{2,1,0:T(8,128)(2,1)S(1)}, bf16[8,288,128]{2,1,0:T(8,128)(2,1)S(1)}, u32[]{:S(2)}, u32[]{:S(2)}) collective-permute-start(bf16[8,288,128]{2,1,0:T(8,128)(2,1)S(1)} %bitcast.68), channel_id=1, source_target_pairs={{0,2},{2,4},{4,6},{6,0},{1,3},{3,5},{5,7},{7,1},{8,10},{10,12},{12... | collective-permute-start | bytes 1769480 | tf_op jit(solution)/shard_map/cond/branch_1_fun/ppermute | solution.py:17
  61.9 15.9 %collective-permute-start.2 = (bf16[8,288,128]{2,1,0:T(8,128)(2,1)S(1)}, bf16[8,288,128]{2,1,0:T(8,128)(2,1)S(1)}, u32[]{:S(2)}, u32[]{:S(2)}) collective-permute-start(bf16[8,288,128]{2,1,0:T(8,128)(2,1)S(1)} %bitcast.69), channel_id=1, source_target_pairs={{0,6},{2,0},{4,2},{6,4},{1,7},{3,1},{5,3},{7,5},{8,14},{10,8},{12,... | collective-permute-start | bytes 1769480 | tf_op jit(solution)/shard_map/cond/branch_1_fun/ppermute | solution.py:17
  77.8 1.0 copy-start.4
  78.8 21.2 %all-to-all-start.2 = ((bf16[8,288,128]{2,1,0:T(8,128)(2,1)}), bf16[8,288,128]{2,1,0:T(8,128)(2,1)S(1)}, u32[]{:S(2)}, u32[]{:S(2)}) async-start(bf16[8,288,128]{2,1,0:T(8,128)(2,1)} %broadcast_in_dim.33), calls=%async_computation.2 | async-start | bytes 1179648 | tf_op jit(solution)/shard_map/cond/branch_1_fun/all_to_all | solution.py:223
  82.4 9.9 %collective-permute-start.3 = (bf16[4,288,128]{2,1,0:T(8,128)(2,1)S(1)}, bf16[4,288,128]{2,1,0:T(8,128)(2,1)S(1)}, u32[]{:S(2)}, u32[]{:S(2)}) collective-permute-start(bf16[4,288,128]{2,1,0:T(8,128)(2,1)S(1)} %slice.62), channel_id=1, source_target_pairs={{0,2},{2,4},{4,6},{6,0},{1,3},{3,5},{5,7},{7,1},{8,10},{10,12},{12... | collective-permute-start | bytes 884744 | tf_op jit(solution)/shard_map/cond/branch_1_fun/ppermute | solution.py:17
  85.5 8.4 %collective-permute-start.4 = (bf16[4,288,128]{2,1,0:T(8,128)(2,1)S(1)}, bf16[4,288,128]{2,1,0:T(8,128)(2,1)S(1)}, u32[]{:S(2)}, u32[]{:S(2)}) collective-permute-start(bf16[4,288,128]{2,1,0:T(8,128)(2,1)S(1)} %slice.63), channel_id=1, source_target_pairs={{0,6},{2,0},{4,2},{6,4},{1,7},{3,1},{5,3},{7,5},{8,14},{10,8},{12,... | collective-permute-start | bytes 884744 | tf_op jit(solution)/shard_map/cond/branch_1_fun/ppermute | solution.py:17
  92.3 0.7 copy-start
  93.9 0.7 copy-start.2
  100.0 15.9 %collective-permute-start.5 = (bf16[8,288,128]{2,1,0:T(8,128)(2,1)S(1)}, bf16[8,288,128]{2,1,0:T(8,128)(2,1)S(1)}, u32[]{:S(2)}, u32[]{:S(2)}) collective-permute-start(bf16[8,288,128]{2,1,0:T(8,128)(2,1)S(1)} %all-to-all-done.2.refs_0_), channel_id=1, source_target_pairs={{0,2},{2,4},{4,6},{6,0},{1,3},{3,5},{5,7},{7,1},{8,10},{10,12},{12... | collective-permute-start | bytes 1769480 | tf_op jit(solution)/shard_map/cond/branch_1_fun/ppermute | solution.py:17
  103.1 14.4 %collective-permute-start.6 = (bf16[8,288,128]{2,1,0:T(8,128)(2,1)S(1)}, bf16[8,288,128]{2,1,0:T(8,128)(2,1)S(1)}, u32[]{:S(2)}, u32[]{:S(2)}) collective-permute-start(bf16[8,288,128]{2,1,0:T(8,128)(2,1)S(1)} %all-to-all-done.2.refs_0_), channel_id=1, source_target_pairs={{0,6},{2,0},{4,2},{6,4},{1,7},{3,1},{5,3},{7,5},{8,14},{10,8},{12,... | collective-permute-start | bytes 1769480 | tf_op jit(solution)/shard_map/cond/branch_1_fun/ppermute | solution.py:17
  109.3 1.0 copy-start.1
  110.3 1.0 copy-start.3
  117.6 12.3 %collective-permute-start.7 = (bf16[4,288,128]{2,1,0:T(8,128)(2,1)S(1)}, bf16[4,288,128]{2,1,0:T(8,128)(2,1)S(1)}, u32[]{:S(2)}, u32[]{:S(2)}) collective-permute-start(bf16[4,288,128]{2,1,0:T(8,128)(2,1)S(1)} %slice.64), channel_id=1, source_target_pairs={{0,2},{2,4},{4,6},{6,0},{1,3},{3,5},{5,7},{7,1},{8,10},{10,12},{12... | collective-permute-start | bytes 884744 | tf_op jit(solution)/shard_map/cond/branch_1_fun/ppermute | solution.py:17
  120.4 9.4 %collective-permute-start.8 = (bf16[4,288,128]{2,1,0:T(8,128)(2,1)S(1)}, bf16[4,288,128]{2,1,0:T(8,128)(2,1)S(1)}, u32[]{:S(2)}, u32[]{:S(2)}) collective-permute-start(bf16[4,288,128]{2,1,0:T(8,128)(2,1)S(1)} %slice.65), channel_id=1, source_target_pairs={{0,6},{2,0},{4,2},{6,4},{1,7},{3,1},{5,3},{7,5},{8,14},{10,8},{12,... | collective-permute-start | bytes 884744 | tf_op jit(solution)/shard_map/cond/branch_1_fun/ppermute | solution.py:17
  124.2 15.1 %collective-permute-start.10 = (bf16[288,4096]{1,0:T(8,128)(2,1)}, bf16[288,4096]{1,0:T(8,128)(2,1)}, u32[]{:S(2)}, u32[]{:S(2)}) collective-permute-start(bf16[288,4096]{1,0:T(8,128)(2,1)} %merge.1), channel_id=1, source_target_pairs={{0,64},{64,0},{1,65},{65,1},{2,66},{66,2},{3,67},{67,3},{4,68},{68... | collective-permute-start | bytes 7077896 | tf_op jit(solution)/shard_map/cond/branch_1_fun/ppermute | solution.py:17
  134.7 9.1 %collective-permute-start.9 = (bf16[288,4096]{1,0:T(8,128)(2,1)}, bf16[288,4096]{1,0:T(8,128)(2,1)}, u32[]{:S(2)}, u32[]{:S(2)}) collective-permute-start(bf16[288,4096]{1,0:T(8,128)(2,1)} %norm.1), channel_id=1, source_target_pairs={{0,64},{64,0},{1,65},{65,1},{2,66},{66,2},{3,67},{67,3},{4,68},{68... | collective-permute-start | bytes 7077896 | tf_op jit(solution)/shard_map/cond/branch_1_fun/ppermute | solution.py:17
  199.9 6.5 %collective-permute-start.12 = (bf16[2,96,512]{2,1,0:T(8,128)(2,1)S(1)}, bf16[2,96,512]{2,1,0:T(8,128)(2,1)S(1)}, u32[]{:S(2)}, u32[]{:S(2)}) collective-permute-start(bf16[2,96,512]{2,1,0:T(8,128)(2,1)S(1)} %select_bitcast_fusion), channel_id=1, source_target_pairs={{0,64},{64,0},{1,65},{65,1},{2,66},{66,2},{3,67},{67,3},{4,68},{68... | collective-permute-start | bytes 589832 | tf_op jit(solution)/shard_map/ppermute | solution.py:17
Sparse Core Ops, SparseCore 0:
  26.7 103.5 all-reduce.1
  155.6 42.2 reduce-scatter.1

commit v3 on v2

--- a/solution.py
+++ b/solution.py
@@ -154,17 +154,39 @@
     )(info, *blocks, *extra)
 
 
+def stage_kernel(flag_ref, first_ref, second_ref, out_ref):
+    rows = first_ref.shape[0]
+    for j, ref in enumerate((first_ref, second_ref)):
+        kept = jnp.where(flag_ref[0] == 1, ref[...].astype(f32), 0.0)
+        out_ref[0, j * rows:(j + 1) * rows, :] = kept.astype(bf16)
+
+
+def stage(flag, first, second):
+    units, width = first.shape
+    block = pl.BlockSpec((units // 2, width // 4), lambda i: (i % 2, i // 2))
+    return pl.pallas_call(
+        stage_kernel,
+        grid=(8,),
+        in_specs=[pl.BlockSpec(memory_space=pltpu.SMEM), block, block],
+        out_specs=pl.BlockSpec((1, units, width // 4), lambda i: (i, 0, 0)),
+        out_shape=jax.ShapeDtypeStruct((8, units, width // 4), bf16),
+        compiler_params=pltpu.CompilerParams(vmem_limit_bytes=32 * MIB),
+        name="stage",
+    )(flag, first, second)
+
+
 def gradient_kernel(normed0, normed1, up0, up1, weights, out_ref, acc, factors, ends):
-    units, width = weights.shape[1:]
-    rows = normed0.shape[0]
+    units = weights.shape[1]
+    rows, width = normed0.shape
     tokens = ((normed0, up0), (normed1, up1))
-    step = 1024
+    half, step = units // 2, width // 4
     for i, refs in enumerate(tokens):
         for j in range(2):
             total = jnp.zeros((rows, units), f32)
-            for k in range(0, width, step):
+            for k in range(4):
+                both = [weights[2 * k + y, j * half:(j + 1) * half, :] for y in range(2)]
                 total += lax.dot_general(
-                    refs[j][:, k:k + step], weights[j, :, k:k + step],
+                    refs[j][:, k * step:(k + 1) * step], jnp.concatenate(both),
                     (((1,), (1,)), ((), ())), preferred_element_type=f32,
                 )
             acc[j, i * rows:(i + 1) * rows, :] = total
@@ -184,7 +206,6 @@
             ends[j, i * rest:(i + 1) * rest, :] = refs[j][main:, :]
 
     out_width = out_ref.shape[-1]
-    half = units // 2
     for q in range(width // out_width):
         columns = slice(q * out_width, (q + 1) * out_width)
         for j in range(2):
@@ -201,8 +222,8 @@
 
 
 def gradients(normed, normed_other, upstream, upstream_other, weights):
-    units, width = weights.shape[1:]
-    rows = normed.shape[0]
+    units = weights.shape[1]
+    rows, width = normed.shape
     return pl.pallas_call(
         gradient_kernel,
         in_specs=[pl.BlockSpec(memory_space=pltpu.VMEM)] * 5,
@@ -250,13 +271,10 @@
     live_counts = tok * (4 + replica_table[:, 0]) // 6
     live = lax.dynamic_index_in_dim(live_counts, position, 0, keepdims=False)
 
-    pair = jnp.stack([weight_in[0], weight_out[0]]).reshape(2, 2, part, width)
-    theirs = jnp.where(core == 0, pair[:, 1], pair[:, 0])
-    mine = jnp.where(core == 0, pair[:, 0], pair[:, 1])
-    mine = jnp.where(core == source % 2, mine, shift(theirs, "core", 2, 1))
-    slot = jnp.arange(2).reshape(1, 2, 1, 1)
-    spread = jnp.where((slot == yl) & (yh == source // 2), mine[:, None], jnp.zeros((), bf16))
-    spread = spread.reshape(2, 2 * part, width)
+    flag = (position == source).astype(jnp.int32).reshape(1)
+    share_w = lax.psum_scatter(
+        stage(flag, weight_in[0], weight_out[0]), ("yh", "core"), scatter_dimension=0
+    )
 
     cot = cotangent[0].reshape(2, 2, half // 2, cols)
     cot = jnp.concatenate([cot[:, 0], cot[:, 1]], axis=2)
@@ -270,7 +288,8 @@
     local = jnp.bitwise_xor(ids - yh * 2 * vocab_block, core * vocab_block)
     low = local[:, :, 0].reshape(-1, 1)
     high = local[:, :, 1].reshape(-1, 1)
-    weights = lax.psum(spread, ("yh", "yl"))
+
+    info = jnp.stack([x, live, yl * half]).astype(jnp.int32)
 
     def slots(low, high, held, cot):
         cot = lax.all_to_all(cot, ("z", "yl"), 0, 0).reshape(8, half, 2 * cols)
@@ -281,7 +300,6 @@
         sent = jnp.concatenate([rows, jnp.broadcast_to(vectors, (8,) + vectors.shape)], axis=1)
         sent, cot = lax.optimization_barrier((sent, cot))
         got = lax.all_to_all(sent, ("yh", "yl"), 0, 0)
-        info = jnp.stack([x, live, yl * half]).astype(jnp.int32)
         got, sides = lax.optimization_barrier((got, gather_x(cot)))
         far = gather_far(*sides)
         got = got.reshape((4, 2) + got.shape[1:])
@@ -289,19 +307,28 @@
         emb = emb.reshape(half, 2 * cols)
         root = lax.dynamic_index_in_dim(got[:, :, half // 2 :], source // 2, 0, keepdims=False)
         root = root.reshape(2, -1, 2 * cols).astype(f32)
-        emb, far = lax.optimization_barrier((gather_z(emb), far))
-        upstream = assemble(merge_kernel, "merge", info, (cot, *sides, *far))
+        return (root[0], root[1], gather_z(emb), cot, *sides, *far)
+
+    def no_slots(low, high, held, cot):
+        lanes = 2 * cols
+        vector, blocks = jnp.zeros((width // lanes, lanes), f32), jnp.zeros((8, half, lanes), bf16)
+        return (vector, vector) + (blocks,) * 4 + (blocks[:4],) * 2
+
+    def features(gain, bias, emb, *cot):
+        upstream = assemble(merge_kernel, "merge", info, cot)
         sides, upstream = lax.optimization_barrier((gather_x(emb), upstream))
         blocks = (emb, *sides, *gather_far(*sides))
-        normed = assemble(norm_kernel, "norm", info, blocks, (root[0], root[1]))
+        normed = assemble(norm_kernel, "norm", info, blocks, (gain, bias))
         return normed, shift(normed, "core", 2, 1), upstream, shift(upstream, "core", 2, 1)
 
-    def nothing(low, high, held, cot):
+    def no_features(*blocks):
         return (jnp.zeros((half, width), bf16),) * 4
 
-    normed, normed_other, upstream, upstream_other = lax.cond(
-        source < replicas, slots, nothing, low, high, held, cot
-    )
+    some = source < replicas
+    blocks = lax.cond(some, slots, no_slots, low, high, held, cot)
+    *blocks, share_w = lax.optimization_barrier((*blocks, share_w))
+    weights = lax.all_gather(share_w, ("yh", "yl"))
+    normed, normed_other, upstream, upstream_other = lax.cond(some, features, no_features, *blocks)
     terms = gradients(normed, normed_other, upstream, upstream_other, weights)
     sums = lax.psum_scatter(terms, ("yh", "yl"), scatter_dimension=0)
     sums = sums.reshape(2, part, 2, width // 8)

time: 215 us -> 217 us (level)
  other arithmetic: 10.4 us -> 3.97 us
  Pallas kernels: 23.7 us -> 28.8 us
  between operations: 17.4 us -> 15 us
  waiting for transfers between devices: 82.2 us -> 84.6 us
  starting transfers between devices: 67.7 us -> 70 us
    ppermute x13 -> x12, starting transfers between devices: 52.4 us -> 45.2 us  [shift(): lax.ppermute(value, axis, [(i, (i + by) % size) for i in range(size)])]
    all_to_all x1, starting transfers between devices: 5.78 us -> 12 us  [slots(): cot = lax.all_to_all(cot, ('z', 'yl'), 0, 0).reshape(8, half, 2 * cols)]
    select_n x3 -> x0, other arithmetic: 4.95 us -> none  [the longest x1 1.98 us: on_device(): jnp.where((slot == yl) & (yh == source // 2), mine[:, None], jnp.zeros(()...]
    all_to_all x1, waiting for transfers between devices: 5.36 us -> 0.75 us  [gather_z(): lax.all_to_all(jnp.broadcast_to(block, (depth,) + block.shape), 'z', 0, 0)]
    ppermute x13 -> x12, waiting for transfers between devices: 25.4 us -> 29.5 us  [shift(): lax.ppermute(value, axis, [(i, (i + by) % size) for i in range(size)])]
    reduce_scatter x1, waiting for transfers between devices: 42.5 us -> 46.1 us  [on_device(): sums = lax.psum_scatter(terms, ('yh', 'yl'), scatter_dimension=0)]
    pallas_call x0 -> x1, Pallas kernels: none -> 3.63 us  [stage(): pl.pallas_call(stage_kernel, grid=(8,), in_specs=[pl.BlockSpec(memory_spa...]
    unnamed x12 -> x14, local copies, waits for them, and re-layouts: 0.03 us -> 3.61 us
  transfers between devices with their start and end apart: 18 -> 18, of which waited for: 11 -> 12; matrix products, arithmetic and copies ran while one was open for 3% -> 3% of each run, Pallas kernels for 6% -> 6%
where the time goes in v3:
time: 217 us; the launch traced here: 216 us
  waiting for transfers between devices  84.6 us (39%)
  starting transfers between devices  70 us (32%)
  Pallas kernels  28.8 us (13%)
  between operations  15 us (7%)
  local copies, waits for them, and re-layouts  11 us (5%)
  other arithmetic  3.97 us (2%)
  loops' own time  2.51 us (1%)
    reduce_scatter x1, waiting for transfers between devices, on_device(): sums = lax.psum_scatter(terms, ('yh', 'yl'), scatter_dimension=0)  46.1 us
    ppermute x12, starting transfers between devices, shift(): lax.ppermute(value, axis, [(i, (i + by) % size) for i in range(size)])  45.2 us
    ppermute x12, waiting for transfers between devices, shift(): lax.ppermute(value, axis, [(i, (i + by) % size) for i in range(size)])  29.5 us
    all_to_all x1, starting transfers between devices, slots(): cot = lax.all_to_all(cot, ('z', 'yl'), 0, 0).reshape(8, half, 2 * cols)  12 us
    pallas_call x1, Pallas kernels, gradients(): pl.pallas_call(gradient_kernel, in_specs=[pl.BlockSpec(memory_space=pltpu...  11.7 us
    pallas_call x2, Pallas kernels, assemble(): pl.pallas_call(kernel, in_specs=[pl.BlockSpec(memory_space=pltpu.SMEM)] +...  9.62 us
    all_to_all x1, starting transfers between devices, slots(): got = lax.all_to_all(sent, ('yh', 'yl'), 0, 0)  6.68 us
    all_to_all x1, waiting for transfers between devices, slots(): cot = lax.all_to_all(cot, ('z', 'yl'), 0, 0).reshape(8, half, 2 * cols)  6.21 us
  transfers between devices with their start and end apart: 18, of which 12 were waited for; matrix products, arithmetic and copies ran while one was open for 3% of the time, Pallas kernels for 6%

profile of v3, /device:TPU:1, one launch (start us, length us, event | category | flops | bytes accessed | tf_op | source)
XLA Modules:
  0.0 216.0 jit_solution(2555222214747754836)
XLA Ops:
  7.2 1.4 bitcast_select_fusion.2
  9.1 1.4 copy-done
  10.5 1.4 copy-done.1
  12.0 3.6 %stage.1 = bf16[8,192,1024]{2,1,0:T(8,128)(2,1)} custom-call(s32[1]{0:T(128)} %bitcast.12.flag_ref, bf16[192,4096]{1,0:T(8,128)(2,1)S(1)} %bitcast.50, bf16[192,4096]{1,0:T(8,128)(2,1)S(1)} %bitcast.51), custom_call_target="tpu_custom_call" | custom-call | tf_op jit(solution)/shard_map/stage/pallas_call | solution.py:167
  15.7 0.8 copy-done.3
  17.6 77.0 %conditional.2 = (f32[32,128]{1,0:T(8,128)S(1)}, f32[32,128]{1,0:T(8,128)S(1)}, bf16[8,288,128]{2,1,0:T(8,128)(2,1)}, bf16[8,288,128]{2,1,0:T(8,128)(2,1)}, bf16...) conditional(s32[]{:T(128)} %convert_element_type.8, () %tuple.35, ...), branch_computations={%region_1.2_spmd, %region_2.4_spmd} | conditional | flops 850717 | bytes 18120358 | solution.py:328
  17.8 0.9 broadcast_in_dim.11
  18.7 12.0 %all-to-all-start = ((bf16[16,144,128]{2,1,0:T(8,128)(2,1)}), bf16[16,144,128]{2,1,0:T(8,128)(2,1)}, u32[]{:S(2)}, u32[]{:S(2)}) async-start(bf16[16,144,128]{2,1,0:T(8,128)(2,1)} %bitcast.2), calls=%async_computation | async-start | bytes 1179648 | tf_op jit(solution)/shard_map/cond/branch_1_fun/all_to_all | solution.py:295
  30.7 2.9 %collective-permute-start.6 = (bf16[64,4224]{1,0:T(8,128)(2,1)S(1)}, bf16[64,4224]{1,0:T(8,128)(2,1)S(1)}, u32[]{:S(2)}, u32[]{:S(2)}) collective-permute-start(bf16[64,4224]{1,0:T(8,128)(2,1)S(1)} %get-tuple-element.64.own_ref), channel_id=1, source_target_pairs={{0,64},{64,0},{1,65},{65,1},{2,66},{66,2},{3,67},{67,3},{4,68},{68... | collective-permute-start | bytes 1622024 | tf_op jit(solution)/shard_map/cond/branch_1_fun/ppermute | solution.py:17
  35.9 3.9 %lookup.1 = bf16[1152,128]{1,0:T(8,128)(2,1)S(1)} custom-call(s32[1152,1]{1,0:T(8,128)S(1)} %reshape_squeeze.12.low_ref, s32[1152,1]{1,0:T(8,128)S(1)} %reshape_squeeze.13.high_ref, bf16[64,4224]{1,0:T(8,128)(2,1)S(1)} %get-tuple-element.64.own_ref, bf16[64,4224]{1,0:T(8,128)(2,1)S(1)} %collective-permute-done.6.other_ref), custom_call_target="tpu_custom_call" | custom-call | tf_op jit(solution)/shard_map/cond/branch_1_fun/lookup/pallas_call | solution.py:57
  39.9 0.8 pad_maximum_fusion
  40.6 6.2 %all-to-all-done = bf16[16,144,128]{2,1,0:T(8,128)(2,1)} async-done(((bf16[16,144,128]{2,1,0:T(8,128)(2,1)}), bf16[16,144,128]{2,1,0:T(8,128)(2,1)}, u32[]{:S(2)}, u32[]{:S(2)}) %all-to-all-start) | async-done | bytes 589856 | tf_op jit(solution)/shard_map/cond/branch_1_fun/all_to_all | solution.py:295
  46.8 6.7 %all-to-all-start.1 = ((bf16[8,176,128]{2,1,0:T(8,128)(2,1)}), bf16[8,176,128]{2,1,0:T(8,128)(2,1)S(1)}, u32[]{:S(2)}, u32[]{:S(2)}) async-start(bf16[8,176,128]{2,1,0:T(8,128)(2,1)} %pad_maximum_fusion), calls=%async_computation.1 | async-start | bytes 720896 | tf_op jit(solution)/shard_map/cond/branch_1_fun/all_to_all | solution.py:302
  53.5 3.1 %collective-permute-start.7 = (bf16[8,288,128]{2,1,0:T(8,128)(2,1)}, bf16[8,288,128]{2,1,0:T(8,128)(2,1)}, u32[]{:S(2)}, u32[]{:S(2)}) collective-permute-start(bf16[8,288,128]{2,1,0:T(8,128)(2,1)} %bitcast.3), channel_id=1, source_target_pairs={{0,2},{2,4},{4,6},{6,0},{1,3},{3,5},{5,7},{7,1},{8,10},{10,12},{12... | collective-permute-start | bytes 1769480 | tf_op jit(solution)/shard_map/cond/branch_1_fun/ppermute | solution.py:17
  56.6 3.4 %collective-permute-start.8 = (bf16[8,288,128]{2,1,0:T(8,128)(2,1)}, bf16[8,288,128]{2,1,0:T(8,128)(2,1)}, u32[]{:S(2)}, u32[]{:S(2)}) collective-permute-start(bf16[8,288,128]{2,1,0:T(8,128)(2,1)} %bitcast.3), channel_id=1, source_target_pairs={{0,6},{2,0},{4,2},{6,4},{1,7},{3,1},{5,3},{7,5},{8,14},{10,8},{12,... | collective-permute-start | bytes 1769480 | tf_op jit(solution)/shard_map/cond/branch_1_fun/ppermute | solution.py:17
  60.0 9.0 %collective-permute-done.7 = bf16[8,288,128]{2,1,0:T(8,128)(2,1)} collective-permute-done((bf16[8,288,128]{2,1,0:T(8,128)(2,1)}, bf16[8,288,128]{2,1,0:T(8,128)(2,1)}, u32[]{:S(2)}, u32[]{:S(2)}) %collective-permute-start.7) | collective-permute-done | bytes 589856 | tf_op jit(solution)/shard_map/cond/branch_1_fun/ppermute | solution.py:17
  69.0 1.6 collective-permute-done.8
  70.7 0.9 broadcast_in_dim.12
  71.5 6.0 %all-to-all-start.2 = ((bf16[8,288,128]{2,1,0:T(8,128)(2,1)}), bf16[8,288,128]{2,1,0:T(8,128)(2,1)}, u32[]{:S(2)}, u32[]{:S(2)}) async-start(bf16[8,288,128]{2,1,0:T(8,128)(2,1)} %broadcast_in_dim.12), calls=%async_computation.2 | async-start | bytes 1179648 | tf_op jit(solution)/shard_map/cond/branch_1_fun/all_to_all | solution.py:244
  78.1 1.0 slice.58
  79.1 4.6 %collective-permute-start.10 = (bf16[4,288,128]{2,1,0:T(8,128)(2,1)S(1)}, bf16[4,288,128]{2,1,0:T(8,128)(2,1)}, u32[]{:S(2)}, u32[]{:S(2)}) collective-permute-start(bf16[4,288,128]{2,1,0:T(8,128)(2,1)S(1)} %slice.58), channel_id=1, source_target_pairs={{0,6},{2,0},{4,2},{6,4},{1,7},{3,1},{5,3},{7,5},{8,14},{10,8},{12,... | collective-permute-start | bytes 884744 | tf_op jit(solution)/shard_map/cond/branch_1_fun/ppermute | solution.py:17
  83.7 1.0 slice.57
  84.7 1.9 collective-permute-start.9
  86.6 1.1 collective-permute-done.10
  87.7 6.1 %collective-permute-done.9 = bf16[4,288,128]{2,1,0:T(8,128)(2,1)} collective-permute-done((bf16[4,288,128]{2,1,0:T(8,128)(2,1)S(1)}, bf16[4,288,128]{2,1,0:T(8,128)(2,1)}, u32[]{:S(2)}, u32[]{:S(2)}) %collective-permute-start.9) | collective-permute-done | bytes 294944 | tf_op jit(solution)/shard_map/cond/branch_1_fun/ppermute | solution.py:17
  93.8 0.7 all-to-all-done.2
  94.7 0.7 dynamic_slice.11
  95.3 0.7 pad_add_fusion
  96.0 44.4 %conditional.3 = (bf16[288,4096]{1,0:T(8,128)(2,1)}, bf16[288,4096]{1,0:T(8,128)(2,1)}, bf16[288,4096]{1,0:T(8,128)(2,1)}, bf16[288,4096]{1,0:T(8,128)(2,1)}) conditional(s32[]{:T(128)} %convert_element_type.8, () %tuple.34, (bf16[8,288,128]{2,1,0:T(8,128)(2,1)}, s32[3]{0:T(128)S(1)}, bf16[8,288,128]{2,1,0:T(8,128)(2,1)}, ...), branch_computations={%region_5.6_spmd, %region_6.7_spmd} | conditional | bytes 27132176 | solution.py:331
  96.0 3.1 %collective-permute-start = (bf16[8,288,128]{2,1,0:T(8,128)(2,1)}, bf16[8,288,128]{2,1,0:T(8,128)(2,1)S(1)}, u32[]{:S(2)}, u32[]{:S(2)}) collective-permute-start(bf16[8,288,128]{2,1,0:T(8,128)(2,1)} %get-tuple-element.75.refs_0_), channel_id=1, source_target_pairs={{0,2},{2,4},{4,6},{6,0},{1,3},{3,5},{5,7},{7,1},{8,10},{10,12},{12... | collective-permute-start | bytes 1769480 | tf_op jit(solution)/shard_map/cond/branch_1_fun/ppermute | solution.py:17
  99.1 3.4 %collective-permute-start.1 = (bf16[8,288,128]{2,1,0:T(8,128)(2,1)}, bf16[8,288,128]{2,1,0:T(8,128)(2,1)S(1)}, u32[]{:S(2)}, u32[]{:S(2)}) collective-permute-start(bf16[8,288,128]{2,1,0:T(8,128)(2,1)} %get-tuple-element.75.refs_0_), channel_id=1, source_target_pairs={{0,6},{2,0},{4,2},{6,4},{1,7},{3,1},{5,3},{7,5},{8,14},{10,8},{12,... | collective-permute-start | bytes 1769480 | tf_op jit(solution)/shard_map/cond/branch_1_fun/ppermute | solution.py:17
  102.5 4.3 %merge.1 = bf16[288,4096]{1,0:T(8,128)(2,1)} custom-call(s32[3]{0:T(128)S(1)} %get-tuple-element.74.info_ref, bf16[8,288,128]{2,1,0:T(8,128)(2,1)} %get-tuple-element.76.refs_0_, bf16[8,288,128]{2,1,0:T(8,128)(2,1)} %get-tuple-element.77.refs_1_, bf16[8,288,128]{2,1,0:T(8,128)(2,1)} %get-tuple-element.78.refs_2_, ...), custom_call_target="tpu_custom_call" | custom-call | tf_op jit(solution)/shard_map/cond/branch_1_fun/merge/pallas_call | solution.py:146
  106.8 4.5 %collective-permute-done.refs_1_ = bf16[8,288,128]{2,1,0:T(8,128)(2,1)S(1)} collective-permute-done((bf16[8,288,128]{2,1,0:T(8,128)(2,1)}, bf16[8,288,128]{2,1,0:T(8,128)(2,1)S(1)}, u32[]{:S(2)}, u32[]{:S(2)}) %collective-permute-start) | collective-permute-done | bytes 589856 | tf_op jit(solution)/shard_map/cond/branch_1_fun/ppermute | solution.py:17
  111.3 1.7 collective-permute-done.1.refs_2_
  113.0 2.8 %collective-permute-start.2 = (bf16[4,288,128]{2,1,0:T(8,128)(2,1)S(1)}, bf16[4,288,128]{2,1,0:T(8,128)(2,1)S(1)}, u32[]{:S(2)}, u32[]{:S(2)}) collective-permute-start(bf16[4,288,128]{2,1,0:T(8,128)(2,1)S(1)} %slice.59), channel_id=1, source_target_pairs={{0,2},{2,4},{4,6},{6,0},{1,3},{3,5},{5,7},{7,1},{8,10},{10,12},{12... | collective-permute-start | bytes 884744 | tf_op jit(solution)/shard_map/cond/branch_1_fun/ppermute | solution.py:17
  115.9 3.7 %collective-permute-start.3 = (bf16[4,288,128]{2,1,0:T(8,128)(2,1)S(1)}, bf16[4,288,128]{2,1,0:T(8,128)(2,1)S(1)}, u32[]{:S(2)}, u32[]{:S(2)}) collective-permute-start(bf16[4,288,128]{2,1,0:T(8,128)(2,1)S(1)} %slice.60), channel_id=1, source_target_pairs={{0,6},{2,0},{4,2},{6,4},{1,7},{3,1},{5,3},{7,5},{8,14},{10,8},{12,... | collective-permute-start | bytes 884744 | tf_op jit(solution)/shard_map/cond/branch_1_fun/ppermute | solution.py:17
  119.6 6.4 %collective-permute-start.5 = (bf16[288,4096]{1,0:T(8,128)(2,1)}, bf16[288,4096]{1,0:T(8,128)(2,1)}, u32[]{:S(2)}, u32[]{:S(2)}) collective-permute-start(bf16[288,4096]{1,0:T(8,128)(2,1)} %merge.1), channel_id=1, source_target_pairs={{0,64},{64,0},{1,65},{65,1},{2,66},{66,2},{3,67},{67,3},{4,68},{68... | collective-permute-start | bytes 7077896 | tf_op jit(solution)/shard_map/cond/branch_1_fun/ppermute | solution.py:17
  126.0 5.3 %norm.1 = bf16[288,4096]{1,0:T(8,128)(2,1)} custom-call(s32[3]{0:T(128)S(1)} %get-tuple-element.74.info_ref, bf16[8,288,128]{2,1,0:T(8,128)(2,1)} %get-tuple-element.75.refs_0_, bf16[8,288,128]{2,1,0:T(8,128)(2,1)S(1)} %collective-permute-done.refs_1_, bf16[8,288,128]{2,1,0:T(8,128)(2,1)S(1)} %collective-permute-done.1.refs_2_, ...), custom_call_target="tpu_custom_call" | custom-call | tf_op jit(solution)/shard_map/cond/branch_1_fun/norm/pallas_call | solution.py:146
  131.4 4.6 %collective-permute-start.4 = (bf16[288,4096]{1,0:T(8,128)(2,1)}, bf16[288,4096]{1,0:T(8,128)(2,1)}, u32[]{:S(2)}, u32[]{:S(2)}) collective-permute-start(bf16[288,4096]{1,0:T(8,128)(2,1)} %norm.1), channel_id=1, source_target_pairs={{0,64},{64,0},{1,65},{65,1},{2,66},{66,2},{3,67},{67,3},{4,68},{68... | collective-permute-start | bytes 7077896 | tf_op jit(solution)/shard_map/cond/branch_1_fun/ppermute | solution.py:17
  136.0 4.5 %collective-permute-done.4 = bf16[288,4096]{1,0:T(8,128)(2,1)} collective-permute-done((bf16[288,4096]{1,0:T(8,128)(2,1)}, bf16[288,4096]{1,0:T(8,128)(2,1)}, u32[]{:S(2)}, u32[]{:S(2)}) %collective-permute-start.4) | collective-permute-done | bytes 2359328 | tf_op jit(solution)/shard_map/cond/branch_1_fun/ppermute | solution.py:17
  140.5 2.0 all-gather.3.cloned.1.call-done
  142.4 11.7 %gradients.1 = bf16[8,2,96,1024]{3,2,1,0:T(8,128)(2,1)} custom-call(bf16[288,4096]{1,0:T(8,128)(2,1)} %get-tuple-element.125.normed0, bf16[288,4096]{1,0:T(8,128)(2,1)} %get-tuple-element.126.normed1, bf16[288,4096]{1,0:T(8,128)(2,1)} %get-tuple-element.127.up0, bf16[288,4096]{1,0:T(8,128)(2,1)} %get-tuple-element.128.up1, bf16[8,192,1024]{2,1,0:T(8,128)(2,1)} %bitcast.53), custom_call_target="tpu_custom_call" | custom-call | tf_op jit(solution)/shard_map/gradients/pallas_call | solution.py:227
  154.2 46.1 %reduce-scatter.5.cloned.1.call-done = bf16[1,2,96,1024]{3,2,1,0:T(8,128)(2,1)} async-done(((bf16[8,2,96,1024]{3,2,1,0:T(8,128)(2,1)}), bf16[1,2,96,1024]{3,2,1,0:T(8,128)(2,1)}) %reduce-scatter.5.cloned.1.call-update) | async-done | bytes 393232 | tf_op jit(solution)/shard_map/reduce_scatter | solution.py:333
  200.3 1.3 reshape_reduce_scatter.3
  201.6 0.5 fusion.9
  202.2 5.3 %collective-permute-start.11 = (bf16[2,96,512]{2,1,0:T(8,128)(2,1)S(1)}, bf16[2,96,512]{2,1,0:T(8,128)(2,1)S(1)}, u32[]{:S(2)}, u32[]{:S(2)}) collective-permute-start(bf16[2,96,512]{2,1,0:T(8,128)(2,1)S(1)} %select_bitcast_fusion), channel_id=1, source_target_pairs={{0,64},{64,0},{1,65},{65,1},{2,66},{66,2},{3,67},{67,3},{4,68},{68... | collective-permute-start | bytes 589832 | tf_op jit(solution)/shard_map/ppermute | solution.py:17
  207.6 1.0 collective-permute-done.11
  208.7 0.8 fusion.5
  (50 shorter events, 1.8 us)
Async XLA Ops:
  7.2 87.4 %reduce-scatter.3.cloned.1.call-start = ((), (), s32[]{:S(2)}) async-start(), calls=%async_computation.5 | async-start | bytes 3538944 | tf_op jit(solution)/shard_map/reduce_scatter | solution.py:275
  9.1 1.4 copy-start
  10.5 1.4 copy-start.1
  15.6 0.9 copy-start.3
  15.6 1.0 copy-start.5
  15.6 1.1 copy-start.6
  15.6 2.0 copy-start.2
  15.6 2.0 copy-start.4
  15.6 126.8 %all-gather.3.cloned.1.call-start = ((), (), s32[]{:S(2)}) async-start(), calls=%async_computation.7 | async-start | bytes 3538944 | tf_op jit(solution)/shard_map/all_gather | solution.py:330
  18.7 28.2 %all-to-all-start = ((bf16[16,144,128]{2,1,0:T(8,128)(2,1)}), bf16[16,144,128]{2,1,0:T(8,128)(2,1)}, u32[]{:S(2)}, u32[]{:S(2)}) async-start(bf16[16,144,128]{2,1,0:T(8,128)(2,1)} %bitcast.2), calls=%async_computation | async-start | bytes 1179648 | tf_op jit(solution)/shard_map/cond/branch_1_fun/all_to_all | solution.py:295
  30.7 5.2 %collective-permute-start.6 = (bf16[64,4224]{1,0:T(8,128)(2,1)S(1)}, bf16[64,4224]{1,0:T(8,128)(2,1)S(1)}, u32[]{:S(2)}, u32[]{:S(2)}) collective-permute-start(bf16[64,4224]{1,0:T(8,128)(2,1)S(1)} %get-tuple-element.64.own_ref), channel_id=1, source_target_pairs={{0,64},{64,0},{1,65},{65,1},{2,66},{66,2},{3,67},{67,3},{4,68},{68... | collective-permute-start | bytes 1622024 | tf_op jit(solution)/shard_map/cond/branch_1_fun/ppermute | solution.py:17
  46.8 23.8 %all-to-all-start.1 = ((bf16[8,176,128]{2,1,0:T(8,128)(2,1)}), bf16[8,176,128]{2,1,0:T(8,128)(2,1)S(1)}, u32[]{:S(2)}, u32[]{:S(2)}) async-start(bf16[8,176,128]{2,1,0:T(8,128)(2,1)} %pad_maximum_fusion), calls=%async_computation.1 | async-start | bytes 720896 | tf_op jit(solution)/shard_map/cond/branch_1_fun/all_to_all | solution.py:302
  53.5 15.5 %collective-permute-start.7 = (bf16[8,288,128]{2,1,0:T(8,128)(2,1)}, bf16[8,288,128]{2,1,0:T(8,128)(2,1)}, u32[]{:S(2)}, u32[]{:S(2)}) collective-permute-start(bf16[8,288,128]{2,1,0:T(8,128)(2,1)} %bitcast.3), channel_id=1, source_target_pairs={{0,2},{2,4},{4,6},{6,0},{1,3},{3,5},{5,7},{7,1},{8,10},{10,12},{12... | collective-permute-start | bytes 1769480 | tf_op jit(solution)/shard_map/cond/branch_1_fun/ppermute | solution.py:17
  56.6 14.0 %collective-permute-start.8 = (bf16[8,288,128]{2,1,0:T(8,128)(2,1)}, bf16[8,288,128]{2,1,0:T(8,128)(2,1)}, u32[]{:S(2)}, u32[]{:S(2)}) collective-permute-start(bf16[8,288,128]{2,1,0:T(8,128)(2,1)} %bitcast.3), channel_id=1, source_target_pairs={{0,6},{2,0},{4,2},{6,4},{1,7},{3,1},{5,3},{7,5},{8,14},{10,8},{12,... | collective-permute-start | bytes 1769480 | tf_op jit(solution)/shard_map/cond/branch_1_fun/ppermute | solution.py:17
  71.5 23.0 %all-to-all-start.2 = ((bf16[8,288,128]{2,1,0:T(8,128)(2,1)}), bf16[8,288,128]{2,1,0:T(8,128)(2,1)}, u32[]{:S(2)}, u32[]{:S(2)}) async-start(bf16[8,288,128]{2,1,0:T(8,128)(2,1)} %broadcast_in_dim.12), calls=%async_computation.2 | async-start | bytes 1179648 | tf_op jit(solution)/shard_map/cond/branch_1_fun/all_to_all | solution.py:244
  79.1 8.6 %collective-permute-start.10 = (bf16[4,288,128]{2,1,0:T(8,128)(2,1)S(1)}, bf16[4,288,128]{2,1,0:T(8,128)(2,1)}, u32[]{:S(2)}, u32[]{:S(2)}) collective-permute-start(bf16[4,288,128]{2,1,0:T(8,128)(2,1)S(1)} %slice.58), channel_id=1, source_target_pairs={{0,6},{2,0},{4,2},{6,4},{1,7},{3,1},{5,3},{7,5},{8,14},{10,8},{12,... | collective-permute-start | bytes 884744 | tf_op jit(solution)/shard_map/cond/branch_1_fun/ppermute | solution.py:17
  84.7 9.2 %collective-permute-start.9 = (bf16[4,288,128]{2,1,0:T(8,128)(2,1)S(1)}, bf16[4,288,128]{2,1,0:T(8,128)(2,1)}, u32[]{:S(2)}, u32[]{:S(2)}) collective-permute-start(bf16[4,288,128]{2,1,0:T(8,128)(2,1)S(1)} %slice.57), channel_id=1, source_target_pairs={{0,2},{2,4},{4,6},{6,0},{1,3},{3,5},{5,7},{7,1},{8,10},{10,12},{12... | collective-permute-start | bytes 884744 | tf_op jit(solution)/shard_map/cond/branch_1_fun/ppermute | solution.py:17
  94.6 105.7 %reduce-scatter.5.cloned.1.call-start = ((), (), s32[]{:S(2)}) async-start(), calls=%async_computation.6 | async-start | bytes 3538944 | tf_op jit(solution)/shard_map/reduce_scatter | solution.py:333
  96.0 15.3 %collective-permute-start = (bf16[8,288,128]{2,1,0:T(8,128)(2,1)}, bf16[8,288,128]{2,1,0:T(8,128)(2,1)S(1)}, u32[]{:S(2)}, u32[]{:S(2)}) collective-permute-start(bf16[8,288,128]{2,1,0:T(8,128)(2,1)} %get-tuple-element.75.refs_0_), channel_id=1, source_target_pairs={{0,2},{2,4},{4,6},{6,0},{1,3},{3,5},{5,7},{7,1},{8,10},{10,12},{12... | collective-permute-start | bytes 1769480 | tf_op jit(solution)/shard_map/cond/branch_1_fun/ppermute | solution.py:17
  99.1 13.9 %collective-permute-start.1 = (bf16[8,288,128]{2,1,0:T(8,128)(2,1)}, bf16[8,288,128]{2,1,0:T(8,128)(2,1)S(1)}, u32[]{:S(2)}, u32[]{:S(2)}) collective-permute-start(bf16[8,288,128]{2,1,0:T(8,128)(2,1)} %get-tuple-element.75.refs_0_), channel_id=1, source_target_pairs={{0,6},{2,0},{4,2},{6,4},{1,7},{3,1},{5,3},{7,5},{8,14},{10,8},{12,... | collective-permute-start | bytes 1769480 | tf_op jit(solution)/shard_map/cond/branch_1_fun/ppermute | solution.py:17
  113.0 13.0 %collective-permute-start.2 = (bf16[4,288,128]{2,1,0:T(8,128)(2,1)S(1)}, bf16[4,288,128]{2,1,0:T(8,128)(2,1)S(1)}, u32[]{:S(2)}, u32[]{:S(2)}) collective-permute-start(bf16[4,288,128]{2,1,0:T(8,128)(2,1)S(1)} %slice.59), channel_id=1, source_target_pairs={{0,2},{2,4},{4,6},{6,0},{1,3},{3,5},{5,7},{7,1},{8,10},{10,12},{12... | collective-permute-start | bytes 884744 | tf_op jit(solution)/shard_map/cond/branch_1_fun/ppermute | solution.py:17
  115.9 10.1 %collective-permute-start.3 = (bf16[4,288,128]{2,1,0:T(8,128)(2,1)S(1)}, bf16[4,288,128]{2,1,0:T(8,128)(2,1)S(1)}, u32[]{:S(2)}, u32[]{:S(2)}) collective-permute-start(bf16[4,288,128]{2,1,0:T(8,128)(2,1)S(1)} %slice.60), channel_id=1, source_target_pairs={{0,6},{2,0},{4,2},{6,4},{1,7},{3,1},{5,3},{7,5},{8,14},{10,8},{12,... | collective-permute-start | bytes 884744 | tf_op jit(solution)/shard_map/cond/branch_1_fun/ppermute | solution.py:17
  119.6 16.4 %collective-permute-start.5 = (bf16[288,4096]{1,0:T(8,128)(2,1)}, bf16[288,4096]{1,0:T(8,128)(2,1)}, u32[]{:S(2)}, u32[]{:S(2)}) collective-permute-start(bf16[288,4096]{1,0:T(8,128)(2,1)} %merge.1), channel_id=1, source_target_pairs={{0,64},{64,0},{1,65},{65,1},{2,66},{66,2},{3,67},{67,3},{4,68},{68... | collective-permute-start | bytes 7077896 | tf_op jit(solution)/shard_map/cond/branch_1_fun/ppermute | solution.py:17
  131.4 9.1 %collective-permute-start.4 = (bf16[288,4096]{1,0:T(8,128)(2,1)}, bf16[288,4096]{1,0:T(8,128)(2,1)}, u32[]{:S(2)}, u32[]{:S(2)}) collective-permute-start(bf16[288,4096]{1,0:T(8,128)(2,1)} %norm.1), channel_id=1, source_target_pairs={{0,64},{64,0},{1,65},{65,1},{2,66},{66,2},{3,67},{67,3},{4,68},{68... | collective-permute-start | bytes 7077896 | tf_op jit(solution)/shard_map/cond/branch_1_fun/ppermute | solution.py:17
  202.2 6.4 %collective-permute-start.11 = (bf16[2,96,512]{2,1,0:T(8,128)(2,1)S(1)}, bf16[2,96,512]{2,1,0:T(8,128)(2,1)S(1)}, u32[]{:S(2)}, u32[]{:S(2)}) collective-permute-start(bf16[2,96,512]{2,1,0:T(8,128)(2,1)S(1)} %select_bitcast_fusion), channel_id=1, source_target_pairs={{0,64},{64,0},{1,65},{65,1},{2,66},{66,2},{3,67},{67,3},{4,68},{68... | collective-permute-start | bytes 589832 | tf_op jit(solution)/shard_map/ppermute | solution.py:17
Sparse Core Ops, SparseCore 0:
  15.8 65.3 reduce-scatter.2
  94.7 47.6 all-gather.2
  154.3 45.9 reduce-scatter.4

commit v4 on v3

--- a/solution.py
+++ b/solution.py
@@ -170,26 +170,47 @@
         in_specs=[pl.BlockSpec(memory_space=pltpu.SMEM), block, block],
         out_specs=pl.BlockSpec((1, units, width // 4), lambda i: (i, 0, 0)),
         out_shape=jax.ShapeDtypeStruct((8, units, width // 4), bf16),
-        compiler_params=pltpu.CompilerParams(vmem_limit_bytes=32 * MIB),
+        compiler_params=pltpu.CompilerParams(vmem_limit_bytes=60 * MIB),
         name="stage",
     )(flag, first, second)
 
 
-def gradient_kernel(normed0, normed1, up0, up1, weights, out_ref, acc, factors, ends):
-    units = weights.shape[1]
-    rows, width = normed0.shape
-    tokens = ((normed0, up0), (normed1, up1))
-    half, step = units // 2, width // 4
-    for i, refs in enumerate(tokens):
+def gradient_kernel(
+    normed0, normed1, up0, up1, weights, out, rows0, rows1, rows2, rows3, held, done, acc, factors,
+    come, go,
+):
+    units, step = weights.shape[1:]
+    rows = normed0.shape[0]
+    tokens = ((rows0, rows2), (rows1, rows3))
+    half = units // 2
+    main = 256
+
+    copies = []
+    for k in range(4):
+        columns = pl.ds(k * step, step)
+        pairs = [(weights.at[pl.ds(2 * k, 2)], held.at[pl.ds(2 * k, 2)])]
+        for source, target in ((normed0, rows0), (normed1, rows1), (up0, rows2), (up1, rows3)):
+            pairs.append((source.at[:, columns], target.at[:, columns]))
+        copies.append(
+            [pltpu.make_async_copy(a, b, come.at[k, n]) for n, (a, b) in enumerate(pairs)]
+        )
+        for copy in copies[k]:
+            copy.start()
+
+    for k in range(4):
+        for copy in copies[k]:
+            copy.wait()
         for j in range(2):
-            total = jnp.zeros((rows, units), f32)
-            for k in range(4):
-                both = [weights[2 * k + y, j * half:(j + 1) * half, :] for y in range(2)]
-                total += lax.dot_general(
-                    refs[j][:, k * step:(k + 1) * step], jnp.concatenate(both),
-                    (((1,), (1,)), ((), ())), preferred_element_type=f32,
+            both = jnp.concatenate(
+                [held[2 * k + y, j * half:(j + 1) * half, :] for y in range(2)]
+            )
+            for t, refs in enumerate(tokens):
+                here = (j, slice(t * rows, (t + 1) * rows))
+                term = lax.dot_general(
+                    refs[j][:, k * step:(k + 1) * step], both, (((1,), (1,)), ((), ())),
+                    preferred_element_type=f32,
                 )
-            acc[j, i * rows:(i + 1) * rows, :] = total
+                acc[here] = term if k == 0 else acc[here] + term
 
     value = acc[0]
     bent = jnp.tanh(SLOPE * (value + CUBE * value * value * value))
@@ -199,42 +220,50 @@
     factors[0] = jnp.transpose(acc[1] * slope).astype(bf16)
     factors[1] = jnp.transpose(0.5 * value * (1.0 + bent)).astype(bf16)
 
-    main = 256
-    rest = rows - main
-    for j in range(2):
-        for i, refs in enumerate(tokens):
-            ends[j, i * rest:(i + 1) * rest, :] = refs[j][main:, :]
-
-    out_width = out_ref.shape[-1]
-    for q in range(width // out_width):
-        columns = slice(q * out_width, (q + 1) * out_width)
+    leaving = []
+    for q in range(4):
+        columns = slice(q * step, (q + 1) * step)
         for j in range(2):
-            end = jnp.concatenate([factors[j, :, main:rows], factors[j, :, rows + main:]], axis=1)
-            total = jnp.dot(end, ends[j, :, columns], preferred_element_type=f32)
-            for i, refs in enumerate(tokens):
+            ends = [factors[j, :, main:rows], factors[j, :, rows + main:]]
+            total = jnp.dot(
+                jnp.concatenate(ends, axis=1),
+                jnp.concatenate([refs[j][main:, columns] for refs in tokens]),
+                preferred_element_type=f32,
+            )
+            for t, refs in enumerate(tokens):
                 total += jnp.dot(
-                    factors[j, :, i * rows:i * rows + main], refs[j][:main, columns],
+                    factors[j, :, t * rows:t * rows + main], refs[j][:main, columns],
                     preferred_element_type=f32,
                 )
             total = total.astype(bf16)
             for y in range(2):
-                out_ref[2 * q + y, j] = total[y * half:(y + 1) * half]
+                done[2 * q + y, j] = total[y * half:(y + 1) * half]
+        block = pl.ds(2 * q, 2)
+        leaving.append(pltpu.make_async_copy(done.at[block], out.at[block], go.at[q]))
+        leaving[q].start()
+    for copy in leaving:
+        copy.wait()
 
 
 def gradients(normed, normed_other, upstream, upstream_other, weights):
-    units = weights.shape[1]
+    units, step = weights.shape[1:]
     rows, width = normed.shape
+    shape = (8, 2, units // 2, step)
     return pl.pallas_call(
         gradient_kernel,
-        in_specs=[pl.BlockSpec(memory_space=pltpu.VMEM)] * 5,
-        out_specs=pl.BlockSpec(memory_space=pltpu.VMEM),
-        out_shape=jax.ShapeDtypeStruct((8, 2, units // 2, width // 4), bf16),
-        scratch_shapes=[
+        in_specs=[pl.BlockSpec(memory_space=pl.ANY)] * 5,
+        out_specs=pl.BlockSpec(memory_space=pl.ANY),
+        out_shape=jax.ShapeDtypeStruct(shape, bf16),
+        scratch_shapes=[pltpu.VMEM((rows, width), bf16)] * 4
+        + [
+            pltpu.VMEM(weights.shape, bf16),
+            pltpu.VMEM(shape, bf16),
             pltpu.VMEM((2, 2 * rows, units), f32),
             pltpu.VMEM((2, units, 2 * rows), bf16),
-            pltpu.VMEM((2, 2 * (rows - 256), width), bf16),
+            pltpu.SemaphoreType.DMA((4, 5)),
+            pltpu.SemaphoreType.DMA((4,)),
         ],
-        compiler_params=pltpu.CompilerParams(vmem_limit_bytes=48 * MIB),
+        compiler_params=pltpu.CompilerParams(vmem_limit_bytes=56 * MIB),
         name="gradients",
     )(normed, normed_other, upstream, upstream_other, weights)
 
@@ -272,8 +301,9 @@
     live = lax.dynamic_index_in_dim(live_counts, position, 0, keepdims=False)
 
     flag = (position == source).astype(jnp.int32).reshape(1)
+    staged = stage(flag, weight_in[0], weight_out[0])
     share_w = lax.psum_scatter(
-        stage(flag, weight_in[0], weight_out[0]), ("yh", "core"), scatter_dimension=0
+        staged.reshape(8 * units, width // 4), ("yh", "core"), scatter_dimension=0, tiled=True
     )
 
     cot = cotangent[0].reshape(2, 2, half // 2, cols)
@@ -327,12 +357,12 @@
     some = source < replicas
     blocks = lax.cond(some, slots, no_slots, low, high, held, cot)
     *blocks, share_w = lax.optimization_barrier((*blocks, share_w))
-    weights = lax.all_gather(share_w, ("yh", "yl"))
+    weights = lax.all_gather(share_w, ("yh", "yl"), tiled=True).reshape(8, units, width // 4)
     normed, normed_other, upstream, upstream_other = lax.cond(some, features, no_features, *blocks)
     terms = gradients(normed, normed_other, upstream, upstream_other, weights)
-    sums = lax.psum_scatter(terms, ("yh", "yl"), scatter_dimension=0)
-    sums = sums.reshape(2, part, 2, width // 8)
-    left, right = sums[:, :, 0], sums[:, :, 1]
+    terms = terms.reshape(16, part, width // 4)
+    sums = lax.psum_scatter(terms, ("yh", "yl"), scatter_dimension=0, tiled=True)
+    left, right = sums[:, :, : width // 8], sums[:, :, width // 8 :]
     theirs = shift(jnp.where(core == 0, right, left), "core", 2, 1)
     mine = jnp.where(core == 0, left, right)
     top = jnp.where(core == 0, mine, theirs)

time: 217 us -> 215 us (level)
  local copies, waits for them, and re-layouts: 11 us -> 6.32 us
    pallas_call x1, Pallas kernels: 3.63 us -> 6.46 us  [stage(): pl.pallas_call(stage_kernel, grid=(8,), in_specs=[pl.BlockSpec(memory_spa...]
    unnamed x14 -> x10, local copies, waits for them, and re-layouts: 3.61 us -> 0.8 us
    pallas_call x1, Pallas kernels: 11.7 us -> 9.26 us  [gradients(): pl.pallas_call(gradient_kernel, in_specs=[pl.BlockSpec(memory_space=pl.AN...]
where the time goes in v4:
time: 215 us; the launch traced here: 214 us
  waiting for transfers between devices  84.5 us (39%)
  starting transfers between devices  70.1 us (33%)
  Pallas kernels  29.2 us (14%)
  between operations  15.1 us (7%)
  local copies, waits for them, and re-layouts  6.32 us (3%)
  other arithmetic  6.02 us (3%)
  loops' own time  2.77 us (1%)
    reduce_scatter x1, waiting for transfers between devices, on_device(): lax.psum_scatter(terms, ('yh', 'yl'), scatter_dimension=0, tiled=True)  46.2 us
    ppermute x12, starting transfers between devices, shift(): lax.ppermute(value, axis, [(i, (i + by) % size) for i in range(size)])  45.3 us
    ppermute x12, waiting for transfers between devices, shift(): lax.ppermute(value, axis, [(i, (i + by) % size) for i in range(size)])  29.5 us
    all_to_all x1, starting transfers between devices, slots(): cot = lax.all_to_all(cot, ('z', 'yl'), 0, 0).reshape(8, half, 2 * cols)  12 us
    pallas_call x2, Pallas kernels, assemble(): pl.pallas_call(kernel, in_specs=[pl.BlockSpec(memory_space=pltpu.SMEM)] +...  9.64 us
    pallas_call x1, Pallas kernels, gradients(): pl.pallas_call(gradient_kernel, in_specs=[pl.BlockSpec(memory_space=pl.AN...  9.26 us
    all_to_all x1, starting transfers between devices, slots(): got = lax.all_to_all(sent, ('yh', 'yl'), 0, 0)  6.68 us
    pallas_call x1, Pallas kernels, stage(): pl.pallas_call(stage_kernel, grid=(8,), in_specs=[pl.BlockSpec(memory_spa...  6.46 us
  transfers between devices with their start and end apart: 18, of which 12 were waited for; matrix products, arithmetic and copies ran while one was open for 3% of the time, Pallas kernels for 6%

profile of v4, /device:TPU:1, one launch (start us, length us, event | category | flops | bytes accessed | tf_op | source)
XLA Modules:
  0.0 214.0 jit_solution(1577331580335425431)
XLA Ops:
  7.2 1.4 bitcast_select_fusion
  9.3 6.5 %stage.1 = bf16[8,192,1024]{2,1,0:T(8,128)(2,1)} custom-call(s32[1]{0:T(128)} %bitcast.12.flag_ref, bf16[192,4096]{1,0:T(8,128)(2,1)} %bitcast.48, bf16[192,4096]{1,0:T(8,128)(2,1)} %bitcast.49), custom_call_target="tpu_custom_call" | custom-call | tf_op jit(solution)/shard_map/stage/pallas_call | solution.py:167
  15.8 0.8 copy-done.1
  17.8 77.0 %conditional.2 = (f32[32,128]{1,0:T(8,128)S(1)}, f32[32,128]{1,0:T(8,128)S(1)}, bf16[8,288,128]{2,1,0:T(8,128)(2,1)}, bf16[8,288,128]{2,1,0:T(8,128)(2,1)}, bf16...) conditional(s32[]{:T(128)} %convert_element_type.8, () %tuple.35, ...), branch_computations={%region_1.2_spmd, %region_2.4_spmd} | conditional | flops 850717 | bytes 18120358 | solution.py:358
  18.0 0.9 broadcast_in_dim.11
  18.9 12.0 %all-to-all-start = ((bf16[16,144,128]{2,1,0:T(8,128)(2,1)}), bf16[16,144,128]{2,1,0:T(8,128)(2,1)}, u32[]{:S(2)}, u32[]{:S(2)}) async-start(bf16[16,144,128]{2,1,0:T(8,128)(2,1)} %bitcast.2), calls=%async_computation | async-start | bytes 1179648 | tf_op jit(solution)/shard_map/cond/branch_1_fun/all_to_all | solution.py:325
  30.9 2.9 %collective-permute-start.6 = (bf16[64,4224]{1,0:T(8,128)(2,1)S(1)}, bf16[64,4224]{1,0:T(8,128)(2,1)S(1)}, u32[]{:S(2)}, u32[]{:S(2)}) collective-permute-start(bf16[64,4224]{1,0:T(8,128)(2,1)S(1)} %get-tuple-element.64.own_ref), channel_id=1, source_target_pairs={{0,64},{64,0},{1,65},{65,1},{2,66},{66,2},{3,67},{67,3},{4,68},{68... | collective-permute-start | bytes 1622024 | tf_op jit(solution)/shard_map/cond/branch_1_fun/ppermute | solution.py:17
  35.8 0.3 reshape_squeeze.12.low_ref
  36.0 0.3 reshape_squeeze.13.high_ref
  36.3 3.9 %lookup.1 = bf16[1152,128]{1,0:T(8,128)(2,1)S(1)} custom-call(s32[1152,1]{1,0:T(8,128)S(1)} %reshape_squeeze.12.low_ref, s32[1152,1]{1,0:T(8,128)S(1)} %reshape_squeeze.13.high_ref, bf16[64,4224]{1,0:T(8,128)(2,1)S(1)} %get-tuple-element.64.own_ref, bf16[64,4224]{1,0:T(8,128)(2,1)S(1)} %collective-permute-done.6.other_ref), custom_call_target="tpu_custom_call" | custom-call | tf_op jit(solution)/shard_map/cond/branch_1_fun/lookup/pallas_call | solution.py:57
  40.3 0.8 pad_maximum_fusion
  41.0 6.0 %all-to-all-done = bf16[16,144,128]{2,1,0:T(8,128)(2,1)} async-done(((bf16[16,144,128]{2,1,0:T(8,128)(2,1)}), bf16[16,144,128]{2,1,0:T(8,128)(2,1)}, u32[]{:S(2)}, u32[]{:S(2)}) %all-to-all-start) | async-done | bytes 589856 | tf_op jit(solution)/shard_map/cond/branch_1_fun/all_to_all | solution.py:325
  47.0 6.7 %all-to-all-start.1 = ((bf16[8,176,128]{2,1,0:T(8,128)(2,1)}), bf16[8,176,128]{2,1,0:T(8,128)(2,1)S(1)}, u32[]{:S(2)}, u32[]{:S(2)}) async-start(bf16[8,176,128]{2,1,0:T(8,128)(2,1)} %pad_maximum_fusion), calls=%async_computation.1 | async-start | bytes 720896 | tf_op jit(solution)/shard_map/cond/branch_1_fun/all_to_all | solution.py:332
  53.7 3.1 %collective-permute-start.7 = (bf16[8,288,128]{2,1,0:T(8,128)(2,1)}, bf16[8,288,128]{2,1,0:T(8,128)(2,1)}, u32[]{:S(2)}, u32[]{:S(2)}) collective-permute-start(bf16[8,288,128]{2,1,0:T(8,128)(2,1)} %bitcast.3), channel_id=1, source_target_pairs={{0,2},{2,4},{4,6},{6,0},{1,3},{3,5},{5,7},{7,1},{8,10},{10,12},{12... | collective-permute-start | bytes 1769480 | tf_op jit(solution)/shard_map/cond/branch_1_fun/ppermute | solution.py:17
  56.8 3.4 %collective-permute-start.8 = (bf16[8,288,128]{2,1,0:T(8,128)(2,1)}, bf16[8,288,128]{2,1,0:T(8,128)(2,1)}, u32[]{:S(2)}, u32[]{:S(2)}) collective-permute-start(bf16[8,288,128]{2,1,0:T(8,128)(2,1)} %bitcast.3), channel_id=1, source_target_pairs={{0,6},{2,0},{4,2},{6,4},{1,7},{3,1},{5,3},{7,5},{8,14},{10,8},{12,... | collective-permute-start | bytes 1769480 | tf_op jit(solution)/shard_map/cond/branch_1_fun/ppermute | solution.py:17
  60.2 9.0 %collective-permute-done.7 = bf16[8,288,128]{2,1,0:T(8,128)(2,1)} collective-permute-done((bf16[8,288,128]{2,1,0:T(8,128)(2,1)}, bf16[8,288,128]{2,1,0:T(8,128)(2,1)}, u32[]{:S(2)}, u32[]{:S(2)}) %collective-permute-start.7) | collective-permute-done | bytes 589856 | tf_op jit(solution)/shard_map/cond/branch_1_fun/ppermute | solution.py:17
  69.2 1.6 collective-permute-done.8
  70.8 0.9 broadcast_in_dim.12
  71.7 6.0 %all-to-all-start.2 = ((bf16[8,288,128]{2,1,0:T(8,128)(2,1)}), bf16[8,288,128]{2,1,0:T(8,128)(2,1)}, u32[]{:S(2)}, u32[]{:S(2)}) async-start(bf16[8,288,128]{2,1,0:T(8,128)(2,1)} %broadcast_in_dim.12), calls=%async_computation.2 | async-start | bytes 1179648 | tf_op jit(solution)/shard_map/cond/branch_1_fun/all_to_all | solution.py:273
  78.4 1.0 slice.58
  79.4 4.6 %collective-permute-start.10 = (bf16[4,288,128]{2,1,0:T(8,128)(2,1)S(1)}, bf16[4,288,128]{2,1,0:T(8,128)(2,1)}, u32[]{:S(2)}, u32[]{:S(2)}) collective-permute-start(bf16[4,288,128]{2,1,0:T(8,128)(2,1)S(1)} %slice.58), channel_id=1, source_target_pairs={{0,6},{2,0},{4,2},{6,4},{1,7},{3,1},{5,3},{7,5},{8,14},{10,8},{12,... | collective-permute-start | bytes 884744 | tf_op jit(solution)/shard_map/cond/branch_1_fun/ppermute | solution.py:17
  84.0 1.0 slice.57
  84.9 1.9 collective-permute-start.9
  86.9 1.1 collective-permute-done.10
  88.0 6.1 %collective-permute-done.9 = bf16[4,288,128]{2,1,0:T(8,128)(2,1)} collective-permute-done((bf16[4,288,128]{2,1,0:T(8,128)(2,1)S(1)}, bf16[4,288,128]{2,1,0:T(8,128)(2,1)}, u32[]{:S(2)}, u32[]{:S(2)}) %collective-permute-start.9) | collective-permute-done | bytes 294944 | tf_op jit(solution)/shard_map/cond/branch_1_fun/ppermute | solution.py:17
  94.1 0.7 all-to-all-done.2
  94.9 0.6 dynamic_slice.11
  95.5 0.7 pad_add_fusion
  96.2 44.5 %conditional.3 = (bf16[288,4096]{1,0:T(8,128)(2,1)}, bf16[288,4096]{1,0:T(8,128)(2,1)}, bf16[288,4096]{1,0:T(8,128)(2,1)}, bf16[288,4096]{1,0:T(8,128)(2,1)}) conditional(s32[]{:T(128)} %convert_element_type.8, () %tuple.34, (bf16[8,288,128]{2,1,0:T(8,128)(2,1)}, s32[3]{0:T(128)S(1)}, bf16[8,288,128]{2,1,0:T(8,128)(2,1)}, ...), branch_computations={%region_5.6_spmd, %region_6.7_spmd} | conditional | bytes 27132176 | solution.py:361
  96.2 3.1 %collective-permute-start = (bf16[8,288,128]{2,1,0:T(8,128)(2,1)}, bf16[8,288,128]{2,1,0:T(8,128)(2,1)S(1)}, u32[]{:S(2)}, u32[]{:S(2)}) collective-permute-start(bf16[8,288,128]{2,1,0:T(8,128)(2,1)} %get-tuple-element.75.refs_0_), channel_id=1, source_target_pairs={{0,2},{2,4},{4,6},{6,0},{1,3},{3,5},{5,7},{7,1},{8,10},{10,12},{12... | collective-permute-start | bytes 1769480 | tf_op jit(solution)/shard_map/cond/branch_1_fun/ppermute | solution.py:17
  99.3 3.4 %collective-permute-start.1 = (bf16[8,288,128]{2,1,0:T(8,128)(2,1)}, bf16[8,288,128]{2,1,0:T(8,128)(2,1)S(1)}, u32[]{:S(2)}, u32[]{:S(2)}) collective-permute-start(bf16[8,288,128]{2,1,0:T(8,128)(2,1)} %get-tuple-element.75.refs_0_), channel_id=1, source_target_pairs={{0,6},{2,0},{4,2},{6,4},{1,7},{3,1},{5,3},{7,5},{8,14},{10,8},{12,... | collective-permute-start | bytes 1769480 | tf_op jit(solution)/shard_map/cond/branch_1_fun/ppermute | solution.py:17
  102.7 4.3 %merge.1 = bf16[288,4096]{1,0:T(8,128)(2,1)} custom-call(s32[3]{0:T(128)S(1)} %get-tuple-element.74.info_ref, bf16[8,288,128]{2,1,0:T(8,128)(2,1)} %get-tuple-element.76.refs_0_, bf16[8,288,128]{2,1,0:T(8,128)(2,1)} %get-tuple-element.77.refs_1_, bf16[8,288,128]{2,1,0:T(8,128)(2,1)} %get-tuple-element.78.refs_2_, ...), custom_call_target="tpu_custom_call" | custom-call | tf_op jit(solution)/shard_map/cond/branch_1_fun/merge/pallas_call | solution.py:146
  107.0 4.5 %collective-permute-done.refs_1_ = bf16[8,288,128]{2,1,0:T(8,128)(2,1)S(1)} collective-permute-done((bf16[8,288,128]{2,1,0:T(8,128)(2,1)}, bf16[8,288,128]{2,1,0:T(8,128)(2,1)S(1)}, u32[]{:S(2)}, u32[]{:S(2)}) %collective-permute-start) | collective-permute-done | bytes 589856 | tf_op jit(solution)/shard_map/cond/branch_1_fun/ppermute | solution.py:17
  111.5 1.7 collective-permute-done.1.refs_2_
  113.2 2.8 %collective-permute-start.2 = (bf16[4,288,128]{2,1,0:T(8,128)(2,1)S(1)}, bf16[4,288,128]{2,1,0:T(8,128)(2,1)S(1)}, u32[]{:S(2)}, u32[]{:S(2)}) collective-permute-start(bf16[4,288,128]{2,1,0:T(8,128)(2,1)S(1)} %slice.59), channel_id=1, source_target_pairs={{0,2},{2,4},{4,6},{6,0},{1,3},{3,5},{5,7},{7,1},{8,10},{10,12},{12... | collective-permute-start | bytes 884744 | tf_op jit(solution)/shard_map/cond/branch_1_fun/ppermute | solution.py:17
  116.1 3.7 %collective-permute-start.3 = (bf16[4,288,128]{2,1,0:T(8,128)(2,1)S(1)}, bf16[4,288,128]{2,1,0:T(8,128)(2,1)S(1)}, u32[]{:S(2)}, u32[]{:S(2)}) collective-permute-start(bf16[4,288,128]{2,1,0:T(8,128)(2,1)S(1)} %slice.60), channel_id=1, source_target_pairs={{0,6},{2,0},{4,2},{6,4},{1,7},{3,1},{5,3},{7,5},{8,14},{10,8},{12,... | collective-permute-start | bytes 884744 | tf_op jit(solution)/shard_map/cond/branch_1_fun/ppermute | solution.py:17
  119.7 6.4 %collective-permute-start.5 = (bf16[288,4096]{1,0:T(8,128)(2,1)}, bf16[288,4096]{1,0:T(8,128)(2,1)}, u32[]{:S(2)}, u32[]{:S(2)}) collective-permute-start(bf16[288,4096]{1,0:T(8,128)(2,1)} %merge.1), channel_id=1, source_target_pairs={{0,64},{64,0},{1,65},{65,1},{2,66},{66,2},{3,67},{67,3},{4,68},{68... | collective-permute-start | bytes 7077896 | tf_op jit(solution)/shard_map/cond/branch_1_fun/ppermute | solution.py:17
  126.2 5.3 %norm.1 = bf16[288,4096]{1,0:T(8,128)(2,1)} custom-call(s32[3]{0:T(128)S(1)} %get-tuple-element.74.info_ref, bf16[8,288,128]{2,1,0:T(8,128)(2,1)} %get-tuple-element.75.refs_0_, bf16[8,288,128]{2,1,0:T(8,128)(2,1)S(1)} %collective-permute-done.refs_1_, bf16[8,288,128]{2,1,0:T(8,128)(2,1)S(1)} %collective-permute-done.1.refs_2_, ...), custom_call_target="tpu_custom_call" | custom-call | tf_op jit(solution)/shard_map/cond/branch_1_fun/norm/pallas_call | solution.py:146
  131.6 4.6 %collective-permute-start.4 = (bf16[288,4096]{1,0:T(8,128)(2,1)}, bf16[288,4096]{1,0:T(8,128)(2,1)}, u32[]{:S(2)}, u32[]{:S(2)}) collective-permute-start(bf16[288,4096]{1,0:T(8,128)(2,1)} %norm.1), channel_id=1, source_target_pairs={{0,64},{64,0},{1,65},{65,1},{2,66},{66,2},{3,67},{67,3},{4,68},{68... | collective-permute-start | bytes 7077896 | tf_op jit(solution)/shard_map/cond/branch_1_fun/ppermute | solution.py:17
  136.2 4.5 %collective-permute-done.4 = bf16[288,4096]{1,0:T(8,128)(2,1)} collective-permute-done((bf16[288,4096]{1,0:T(8,128)(2,1)}, bf16[288,4096]{1,0:T(8,128)(2,1)}, u32[]{:S(2)}, u32[]{:S(2)}) %collective-permute-start.4) | collective-permute-done | bytes 2359328 | tf_op jit(solution)/shard_map/cond/branch_1_fun/ppermute | solution.py:17
  140.7 2.1 all-gather.2.cloned.1.call-done
  142.7 9.3 %gradients.1 = bf16[8,2,96,1024]{3,2,1,0:T(8,128)(2,1)} custom-call(bf16[288,4096]{1,0:T(8,128)(2,1)} %get-tuple-element.125.normed0, bf16[288,4096]{1,0:T(8,128)(2,1)} %get-tuple-element.126.normed1, bf16[288,4096]{1,0:T(8,128)(2,1)} %get-tuple-element.127.up0, bf16[288,4096]{1,0:T(8,128)(2,1)} %get-tuple-element.128.up1, bf16[8,192,1024]{2,1,0:T(8,128)(2,1)} %bitcast.47), custom_call_target="tpu_custom_call" | custom-call | tf_op jit(solution)/shard_map/gradients/pallas_call | solution.py:252
  152.0 46.2 %reduce-scatter.5.cloned.1.call-done = bf16[2,96,1024]{2,1,0:T(8,128)(2,1)} async-done(((bf16[16,96,1024]{2,1,0:T(8,128)(2,1)}), bf16[2,96,1024]{2,1,0:T(8,128)(2,1)}) %reduce-scatter.5.cloned.1.call-update) | async-done | bytes 393232 | tf_op jit(solution)/shard_map/reduce_scatter | solution.py:364
  198.2 1.0 broadcast_select_fusion.2
  199.2 5.4 %collective-permute-start.11 = (bf16[2,96,512]{2,1,0:T(8,128)(2,1)S(1)}, bf16[2,96,512]{2,1,0:T(8,128)(2,1)S(1)}, u32[]{:S(2)}, u32[]{:S(2)}) collective-permute-start(bf16[2,96,512]{2,1,0:T(8,128)(2,1)S(1)} %broadcast_select_fusion.2), channel_id=1, source_target_pairs={{0,64},{64,0},{1,65},{65,1},{2,66},{66,2},{3,67},{67,3},{4,68},{68... | collective-permute-start | bytes 589832 | tf_op jit(solution)/shard_map/ppermute | solution.py:17
  204.6 1.0 collective-permute-done.11
  205.7 1.1 broadcast_select_fusion
  206.7 0.8 fusion.5
  (43 shorter events, 1.1 us)
Async XLA Ops:
  7.2 87.6 %reduce-scatter.3.cloned.1.call-start = ((), (), s32[]{:S(2)}) async-start(), calls=%async_computation.5 | async-start | bytes 3538944 | tf_op jit(solution)/shard_map/reduce_scatter | solution.py:305
  15.7 0.9 copy-start.1
  15.7 1.0 copy-start.3
  15.7 1.1 copy-start.4
  15.7 2.0 copy-start
  15.7 2.1 copy-start.2
  15.8 126.9 %all-gather.2.cloned.1.call-start = ((), (), s32[]{:S(2)}) async-start(), calls=%async_computation.6 | async-start | bytes 3538944 | tf_op jit(solution)/shard_map/all_gather | solution.py:360
  18.9 28.2 %all-to-all-start = ((bf16[16,144,128]{2,1,0:T(8,128)(2,1)}), bf16[16,144,128]{2,1,0:T(8,128)(2,1)}, u32[]{:S(2)}, u32[]{:S(2)}) async-start(bf16[16,144,128]{2,1,0:T(8,128)(2,1)} %bitcast.2), calls=%async_computation | async-start | bytes 1179648 | tf_op jit(solution)/shard_map/cond/branch_1_fun/all_to_all | solution.py:325
  30.9 5.4 %collective-permute-start.6 = (bf16[64,4224]{1,0:T(8,128)(2,1)S(1)}, bf16[64,4224]{1,0:T(8,128)(2,1)S(1)}, u32[]{:S(2)}, u32[]{:S(2)}) collective-permute-start(bf16[64,4224]{1,0:T(8,128)(2,1)S(1)} %get-tuple-element.64.own_ref), channel_id=1, source_target_pairs={{0,64},{64,0},{1,65},{65,1},{2,66},{66,2},{3,67},{67,3},{4,68},{68... | collective-permute-start | bytes 1622024 | tf_op jit(solution)/shard_map/cond/branch_1_fun/ppermute | solution.py:17
  47.0 23.8 %all-to-all-start.1 = ((bf16[8,176,128]{2,1,0:T(8,128)(2,1)}), bf16[8,176,128]{2,1,0:T(8,128)(2,1)S(1)}, u32[]{:S(2)}, u32[]{:S(2)}) async-start(bf16[8,176,128]{2,1,0:T(8,128)(2,1)} %pad_maximum_fusion), calls=%async_computation.1 | async-start | bytes 720896 | tf_op jit(solution)/shard_map/cond/branch_1_fun/all_to_all | solution.py:332
  53.7 15.5 %collective-permute-start.7 = (bf16[8,288,128]{2,1,0:T(8,128)(2,1)}, bf16[8,288,128]{2,1,0:T(8,128)(2,1)}, u32[]{:S(2)}, u32[]{:S(2)}) collective-permute-start(bf16[8,288,128]{2,1,0:T(8,128)(2,1)} %bitcast.3), channel_id=1, source_target_pairs={{0,2},{2,4},{4,6},{6,0},{1,3},{3,5},{5,7},{7,1},{8,10},{10,12},{12... | collective-permute-start | bytes 1769480 | tf_op jit(solution)/shard_map/cond/branch_1_fun/ppermute | solution.py:17
  56.8 14.0 %collective-permute-start.8 = (bf16[8,288,128]{2,1,0:T(8,128)(2,1)}, bf16[8,288,128]{2,1,0:T(8,128)(2,1)}, u32[]{:S(2)}, u32[]{:S(2)}) collective-permute-start(bf16[8,288,128]{2,1,0:T(8,128)(2,1)} %bitcast.3), channel_id=1, source_target_pairs={{0,6},{2,0},{4,2},{6,4},{1,7},{3,1},{5,3},{7,5},{8,14},{10,8},{12,... | collective-permute-start | bytes 1769480 | tf_op jit(solution)/shard_map/cond/branch_1_fun/ppermute | solution.py:17
  71.7 23.1 %all-to-all-start.2 = ((bf16[8,288,128]{2,1,0:T(8,128)(2,1)}), bf16[8,288,128]{2,1,0:T(8,128)(2,1)}, u32[]{:S(2)}, u32[]{:S(2)}) async-start(bf16[8,288,128]{2,1,0:T(8,128)(2,1)} %broadcast_in_dim.12), calls=%async_computation.2 | async-start | bytes 1179648 | tf_op jit(solution)/shard_map/cond/branch_1_fun/all_to_all | solution.py:273
  79.4 8.6 %collective-permute-start.10 = (bf16[4,288,128]{2,1,0:T(8,128)(2,1)S(1)}, bf16[4,288,128]{2,1,0:T(8,128)(2,1)}, u32[]{:S(2)}, u32[]{:S(2)}) collective-permute-start(bf16[4,288,128]{2,1,0:T(8,128)(2,1)S(1)} %slice.58), channel_id=1, source_target_pairs={{0,6},{2,0},{4,2},{6,4},{1,7},{3,1},{5,3},{7,5},{8,14},{10,8},{12,... | collective-permute-start | bytes 884744 | tf_op jit(solution)/shard_map/cond/branch_1_fun/ppermute | solution.py:17
  84.9 9.2 %collective-permute-start.9 = (bf16[4,288,128]{2,1,0:T(8,128)(2,1)S(1)}, bf16[4,288,128]{2,1,0:T(8,128)(2,1)}, u32[]{:S(2)}, u32[]{:S(2)}) collective-permute-start(bf16[4,288,128]{2,1,0:T(8,128)(2,1)S(1)} %slice.57), channel_id=1, source_target_pairs={{0,2},{2,4},{4,6},{6,0},{1,3},{3,5},{5,7},{7,1},{8,10},{10,12},{12... | collective-permute-start | bytes 884744 | tf_op jit(solution)/shard_map/cond/branch_1_fun/ppermute | solution.py:17
  94.8 103.4 %reduce-scatter.5.cloned.1.call-start = ((), (), s32[]{:S(2)}) async-start(), calls=%async_computation.7 | async-start | bytes 3538944 | tf_op jit(solution)/shard_map/reduce_scatter | solution.py:364
  96.2 15.3 %collective-permute-start = (bf16[8,288,128]{2,1,0:T(8,128)(2,1)}, bf16[8,288,128]{2,1,0:T(8,128)(2,1)S(1)}, u32[]{:S(2)}, u32[]{:S(2)}) collective-permute-start(bf16[8,288,128]{2,1,0:T(8,128)(2,1)} %get-tuple-element.75.refs_0_), channel_id=1, source_target_pairs={{0,2},{2,4},{4,6},{6,0},{1,3},{3,5},{5,7},{7,1},{8,10},{10,12},{12... | collective-permute-start | bytes 1769480 | tf_op jit(solution)/shard_map/cond/branch_1_fun/ppermute | solution.py:17
  99.3 13.9 %collective-permute-start.1 = (bf16[8,288,128]{2,1,0:T(8,128)(2,1)}, bf16[8,288,128]{2,1,0:T(8,128)(2,1)S(1)}, u32[]{:S(2)}, u32[]{:S(2)}) collective-permute-start(bf16[8,288,128]{2,1,0:T(8,128)(2,1)} %get-tuple-element.75.refs_0_), channel_id=1, source_target_pairs={{0,6},{2,0},{4,2},{6,4},{1,7},{3,1},{5,3},{7,5},{8,14},{10,8},{12,... | collective-permute-start | bytes 1769480 | tf_op jit(solution)/shard_map/cond/branch_1_fun/ppermute | solution.py:17
  113.2 13.0 %collective-permute-start.2 = (bf16[4,288,128]{2,1,0:T(8,128)(2,1)S(1)}, bf16[4,288,128]{2,1,0:T(8,128)(2,1)S(1)}, u32[]{:S(2)}, u32[]{:S(2)}) collective-permute-start(bf16[4,288,128]{2,1,0:T(8,128)(2,1)S(1)} %slice.59), channel_id=1, source_target_pairs={{0,2},{2,4},{4,6},{6,0},{1,3},{3,5},{5,7},{7,1},{8,10},{10,12},{12... | collective-permute-start | bytes 884744 | tf_op jit(solution)/shard_map/cond/branch_1_fun/ppermute | solution.py:17
  116.1 10.1 %collective-permute-start.3 = (bf16[4,288,128]{2,1,0:T(8,128)(2,1)S(1)}, bf16[4,288,128]{2,1,0:T(8,128)(2,1)S(1)}, u32[]{:S(2)}, u32[]{:S(2)}) collective-permute-start(bf16[4,288,128]{2,1,0:T(8,128)(2,1)S(1)} %slice.60), channel_id=1, source_target_pairs={{0,6},{2,0},{4,2},{6,4},{1,7},{3,1},{5,3},{7,5},{8,14},{10,8},{12,... | collective-permute-start | bytes 884744 | tf_op jit(solution)/shard_map/cond/branch_1_fun/ppermute | solution.py:17
  119.7 16.4 %collective-permute-start.5 = (bf16[288,4096]{1,0:T(8,128)(2,1)}, bf16[288,4096]{1,0:T(8,128)(2,1)}, u32[]{:S(2)}, u32[]{:S(2)}) collective-permute-start(bf16[288,4096]{1,0:T(8,128)(2,1)} %merge.1), channel_id=1, source_target_pairs={{0,64},{64,0},{1,65},{65,1},{2,66},{66,2},{3,67},{67,3},{4,68},{68... | collective-permute-start | bytes 7077896 | tf_op jit(solution)/shard_map/cond/branch_1_fun/ppermute | solution.py:17
  131.6 9.1 %collective-permute-start.4 = (bf16[288,4096]{1,0:T(8,128)(2,1)}, bf16[288,4096]{1,0:T(8,128)(2,1)}, u32[]{:S(2)}, u32[]{:S(2)}) collective-permute-start(bf16[288,4096]{1,0:T(8,128)(2,1)} %norm.1), channel_id=1, source_target_pairs={{0,64},{64,0},{1,65},{65,1},{2,66},{66,2},{3,67},{67,3},{4,68},{68... | collective-permute-start | bytes 7077896 | tf_op jit(solution)/shard_map/cond/branch_1_fun/ppermute | solution.py:17
  199.2 6.4 %collective-permute-start.11 = (bf16[2,96,512]{2,1,0:T(8,128)(2,1)S(1)}, bf16[2,96,512]{2,1,0:T(8,128)(2,1)S(1)}, u32[]{:S(2)}, u32[]{:S(2)}) collective-permute-start(bf16[2,96,512]{2,1,0:T(8,128)(2,1)S(1)} %broadcast_select_fusion.2), channel_id=1, source_target_pairs={{0,64},{64,0},{1,65},{65,1},{2,66},{66,2},{3,67},{67,3},{4,68},{68... | collective-permute-start | bytes 589832 | tf_op jit(solution)/shard_map/ppermute | solution.py:17
Sparse Core Ops, SparseCore 0:
  15.9 65.6 reduce-scatter.2
  95.0 47.7 all-gather.1
  152.1 46.0 reduce-scatter.4

commit v5 on v4

--- a/solution.py
+++ b/solution.py
@@ -154,32 +154,12 @@
     )(info, *blocks, *extra)
 
 
-def stage_kernel(flag_ref, first_ref, second_ref, out_ref):
-    rows = first_ref.shape[0]
-    for j, ref in enumerate((first_ref, second_ref)):
-        kept = jnp.where(flag_ref[0] == 1, ref[...].astype(f32), 0.0)
-        out_ref[0, j * rows:(j + 1) * rows, :] = kept.astype(bf16)
-
-
-def stage(flag, first, second):
-    units, width = first.shape
-    block = pl.BlockSpec((units // 2, width // 4), lambda i: (i % 2, i // 2))
-    return pl.pallas_call(
-        stage_kernel,
-        grid=(8,),
-        in_specs=[pl.BlockSpec(memory_space=pltpu.SMEM), block, block],
-        out_specs=pl.BlockSpec((1, units, width // 4), lambda i: (i, 0, 0)),
-        out_shape=jax.ShapeDtypeStruct((8, units, width // 4), bf16),
-        compiler_params=pltpu.CompilerParams(vmem_limit_bytes=60 * MIB),
-        name="stage",
-    )(flag, first, second)
-
-
 def gradient_kernel(
     normed0, normed1, up0, up1, weights, out, rows0, rows1, rows2, rows3, held, done, acc, factors,
     come, go,
 ):
-    units, step = weights.shape[1:]
+    units, width = weights.shape[1:]
+    step = width // 4
     rows = normed0.shape[0]
     tokens = ((rows0, rows2), (rows1, rows3))
     half = units // 2
@@ -188,7 +168,7 @@
     copies = []
     for k in range(4):
         columns = pl.ds(k * step, step)
-        pairs = [(weights.at[pl.ds(2 * k, 2)], held.at[pl.ds(2 * k, 2)])]
+        pairs = [(weights.at[:, :, columns], held.at[:, :, columns])]
         for source, target in ((normed0, rows0), (normed1, rows1), (up0, rows2), (up1, rows3)):
             pairs.append((source.at[:, columns], target.at[:, columns]))
         copies.append(
@@ -201,14 +181,11 @@
         for copy in copies[k]:
             copy.wait()
         for j in range(2):
-            both = jnp.concatenate(
-                [held[2 * k + y, j * half:(j + 1) * half, :] for y in range(2)]
-            )
             for t, refs in enumerate(tokens):
                 here = (j, slice(t * rows, (t + 1) * rows))
                 term = lax.dot_general(
-                    refs[j][:, k * step:(k + 1) * step], both, (((1,), (1,)), ((), ())),
-                    preferred_element_type=f32,
+                    refs[j][:, k * step:(k + 1) * step], held[j, :, k * step:(k + 1) * step],
+                    (((1,), (1,)), ((), ())), preferred_element_type=f32,
                 )
                 acc[here] = term if k == 0 else acc[here] + term
 
@@ -246,8 +223,8 @@
 
 
 def gradients(normed, normed_other, upstream, upstream_other, weights):
-    units, step = weights.shape[1:]
-    rows, width = normed.shape
+    units, width = weights.shape[1:]
+    rows, step = normed.shape[0], width // 4
     shape = (8, 2, units // 2, step)
     return pl.pallas_call(
         gradient_kernel,
@@ -300,65 +277,59 @@
     live_counts = tok * (4 + replica_table[:, 0]) // 6
     live = lax.dynamic_index_in_dim(live_counts, position, 0, keepdims=False)
 
-    flag = (position == source).astype(jnp.int32).reshape(1)
-    staged = stage(flag, weight_in[0], weight_out[0])
-    share_w = lax.psum_scatter(
-        staged.reshape(8 * units, width // 4), ("yh", "core"), scatter_dimension=0, tiled=True
-    )
+    pair = jnp.stack([weight_in[0], weight_out[0]]).reshape(2, 2, part, width)
+    theirs = jnp.where(core == 0, pair[:, 1], pair[:, 0])
+    mine = jnp.where(core == 0, pair[:, 0], pair[:, 1])
+    mine = jnp.where(core == source % 2, mine, shift(theirs, "core", 2, 1))
+    slot = jnp.arange(2).reshape(1, 2, 1, 1)
+    spread = jnp.where((slot == yl) & (yh == source // 2), mine[:, None], jnp.zeros((), bf16))
+    spread = spread.reshape(2, 2 * part, width)
 
     cot = cotangent[0].reshape(2, 2, half // 2, cols)
     cot = jnp.concatenate([cot[:, 0], cot[:, 1]], axis=2)
-    cot = jnp.broadcast_to(cot, (8,) + cot.shape).reshape((16,) + cot.shape[1:])
+    cot = lax.all_to_all(cot, "yl", 0, 0).reshape(half, 2 * cols)
+    spread, cot = lax.optimization_barrier((spread, cot))
 
     vectors = jnp.concatenate([ln_gain.reshape(-1, 2 * cols), ln_bias.reshape(-1, 2 * cols)])
     share = vectors.shape[0] // 2
-    held = jnp.concatenate([embedding.T, vectors], axis=1)
+    vectors = lax.dynamic_slice_in_dim(vectors, yl * share, share, 0)
+    table = embedding.T
     ids = token_ids.reshape(4, 2, 2, 2, half // 2)
     ids = jnp.where(core == 0, ids[:, 0], ids[:, 1])
     local = jnp.bitwise_xor(ids - yh * 2 * vocab_block, core * vocab_block)
     low = local[:, :, 0].reshape(-1, 1)
     high = local[:, :, 1].reshape(-1, 1)
-
-    info = jnp.stack([x, live, yl * half]).astype(jnp.int32)
-
-    def slots(low, high, held, cot):
-        cot = lax.all_to_all(cot, ("z", "yl"), 0, 0).reshape(8, half, 2 * cols)
-        swapped = shift(held, "core", 2, 1)
-        rows = lookup(low, high, held, swapped, vocab_block // 8).reshape(8, half // 2, 2 * cols)
-        vectors = jnp.where(core == source % 2, held[:, vocab_block:], swapped[:, vocab_block:])
-        vectors = lax.dynamic_slice_in_dim(vectors, yl * share, share, 0)
+    weights = lax.psum(spread, ("yh", "yl"))
+
+    def slots(low, high, table, vectors, cot):
+        cot = gather_z(cot)
+        swapped = shift(table, "core", 2, 1)
+        rows = lookup(low, high, table, swapped, vocab_block // 8).reshape(8, half // 2, 2 * cols)
         sent = jnp.concatenate([rows, jnp.broadcast_to(vectors, (8,) + vectors.shape)], axis=1)
         sent, cot = lax.optimization_barrier((sent, cot))
         got = lax.all_to_all(sent, ("yh", "yl"), 0, 0)
+        info = jnp.stack([x, live, yl * half]).astype(jnp.int32)
         got, sides = lax.optimization_barrier((got, gather_x(cot)))
         far = gather_far(*sides)
         got = got.reshape((4, 2) + got.shape[1:])
         emb = jnp.sum(got[:, :, : half // 2].astype(f32), axis=0).astype(bf16)
         emb = emb.reshape(half, 2 * cols)
         root = lax.dynamic_index_in_dim(got[:, :, half // 2 :], source // 2, 0, keepdims=False)
+        root = jnp.where(core == source % 2, root, shift(root, "core", 2, 1))
         root = root.reshape(2, -1, 2 * cols).astype(f32)
-        return (root[0], root[1], gather_z(emb), cot, *sides, *far)
-
-    def no_slots(low, high, held, cot):
-        lanes = 2 * cols
-        vector, blocks = jnp.zeros((width // lanes, lanes), f32), jnp.zeros((8, half, lanes), bf16)
-        return (vector, vector) + (blocks,) * 4 + (blocks[:4],) * 2
-
-    def features(gain, bias, emb, *cot):
-        upstream = assemble(merge_kernel, "merge", info, cot)
+        emb, far = lax.optimization_barrier((gather_z(emb), far))
+        upstream = assemble(merge_kernel, "merge", info, (cot, *sides, *far))
         sides, upstream = lax.optimization_barrier((gather_x(emb), upstream))
         blocks = (emb, *sides, *gather_far(*sides))
-        normed = assemble(norm_kernel, "norm", info, blocks, (gain, bias))
+        normed = assemble(norm_kernel, "norm", info, blocks, (root[0], root[1]))
         return normed, shift(normed, "core", 2, 1), upstream, shift(upstream, "core", 2, 1)
 
-    def no_features(*blocks):
+    def nothing(low, high, table, vectors, cot):
         return (jnp.zeros((half, width), bf16),) * 4
 
-    some = source < replicas
-    blocks = lax.cond(some, slots, no_slots, low, high, held, cot)
-    *blocks, share_w = lax.optimization_barrier((*blocks, share_w))
-    weights = lax.all_gather(share_w, ("yh", "yl"), tiled=True).reshape(8, units, width // 4)
-    normed, normed_other, upstream, upstream_other = lax.cond(some, features, no_features, *blocks)
+    normed, normed_other, upstream, upstream_other = lax.cond(
+        source < replicas, slots, nothing, low, high, table, vectors, cot
+    )
     terms = gradients(normed, normed_other, upstream, upstream_other, weights)
     terms = terms.reshape(16, part, width // 4)
     sums = lax.psum_scatter(terms, ("yh", "yl"), scatter_dimension=0, tiled=True)

time: 215 us -> 221 us (1.028)
  Pallas kernels: 29.2 us -> 21.2 us
  other arithmetic: 6.02 us -> 13.7 us
  waiting for transfers between devices: 84.5 us -> 88 us
  local copies, waits for them, and re-layouts: 6.32 us -> 9.05 us
    all_to_all x1 -> x2, waiting for transfers between devices: 0.7 us -> 15.4 us  [gather_z(): lax.all_to_all(jnp.broadcast_to(block, (depth,) + block.shape), 'z', 0, 0)]
    all_to_all x1, starting transfers between devices: 12 us -> 3.31 us  [on_device(): cot = lax.all_to_all(cot, 'yl', 0, 0).reshape(half, 2 * cols)]
    pallas_call x1 -> x0, Pallas kernels: 6.46 us -> none  [stage(): pl.pallas_call(stage_kernel, grid=(8,), in_specs=[pl.BlockSpec(memory_spa...]
    reduce_scatter x1, waiting for transfers between devices: 46.2 us -> 39.9 us  [on_device(): lax.psum_scatter(terms, ('yh', 'yl'), scatter_dimension=0, tiled=True)]
    all_to_all x1, waiting for transfers between devices: 6.02 us -> 0.01 us  [on_device(): cot = lax.all_to_all(cot, 'yl', 0, 0).reshape(half, 2 * cols)]
    select_n x1 -> x3, other arithmetic: 0.01 us -> 4.96 us  [the longest x1 1.98 us: on_device(): jnp.where((slot == yl) & (yh == source // 2), mine[:, None], jnp.zeros(()...]
    ppermute x12 -> x14, starting transfers between devices: 45.3 us -> 49 us  [shift(): lax.ppermute(value, axis, [(i, (i + by) % size) for i in range(size)])]
    cond x0 -> x12, local copies, waits for them, and re-layouts: none -> 3.39 us
  transfers between devices with their start and end apart: 18 -> 20, of which waited for: 12 -> 12; matrix products, arithmetic and copies ran while one was open for 3% -> 6% of each run, Pallas kernels for 6% -> 5%
where the time goes in v5:
time: 221 us; the launch traced here: 220 us
  waiting for transfers between devices  88 us (40%)
  starting transfers between devices  68 us (31%)
  Pallas kernels  21.2 us (10%)
  between operations  17.1 us (8%)
  other arithmetic  13.7 us (6%)
  local copies, waits for them, and re-layouts  9.05 us (4%)
  loops' own time  2.54 us (1%)
    ppermute x14, starting transfers between devices, shift(): lax.ppermute(value, axis, [(i, (i + by) % size) for i in range(size)])  49 us
    reduce_scatter x1, waiting for transfers between devices, on_device(): lax.psum_scatter(terms, ('yh', 'yl'), scatter_dimension=0, tiled=True)  39.9 us
    ppermute x14, waiting for transfers between devices, shift(): lax.ppermute(value, axis, [(i, (i + by) % size) for i in range(size)])  32.7 us
    all_to_all x2, waiting for transfers between devices, gather_z(): lax.all_to_all(jnp.broadcast_to(block, (depth,) + block.shape), 'z', 0, 0)  15.4 us
    pallas_call x1, Pallas kernels, gradients(): pl.pallas_call(gradient_kernel, in_specs=[pl.BlockSpec(memory_space=pl.AN...  9.28 us
    all_to_all x2, starting transfers between devices, gather_z(): lax.all_to_all(jnp.broadcast_to(block, (depth,) + block.shape), 'z', 0, 0)  8.2 us
    pallas_call x2, Pallas kernels, assemble(): pl.pallas_call(kernel, in_specs=[pl.BlockSpec(memory_space=pltpu.SMEM)] +...  8.05 us
    all_to_all x1, starting transfers between devices, slots(): got = lax.all_to_all(sent, ('yh', 'yl'), 0, 0)  7.38 us
  transfers between devices with their start and end apart: 20, of which 12 were waited for; matrix products, arithmetic and copies ran while one was open for 6% of the time, Pallas kernels for 5%

profile of v5, /device:TPU:1, one launch (start us, length us, event | category | flops | bytes accessed | tf_op | source)
XLA Modules:
  0.0 219.6 jit_solution(3078320502943397300)
XLA Ops:
  7.2 2.2 pad_maximum_fusion.1
  9.4 1.4 fusion.3
  10.7 8.8 %collective-permute-start.12 = (bf16[2,96,4096]{2,1,0:T(8,128)(2,1)}, bf16[2,96,4096]{2,1,0:T(8,128)(2,1)}, u32[]{:S(2)}, u32[]{:S(2)}) collective-permute-start(bf16[2,96,4096]{2,1,0:T(8,128)(2,1)} %fusion.3), channel_id=1, source_target_pairs={{0,64},{64,0},{1,65},{65,1},{2,66},{66,2},{3,67},{67,3},{4,68},{68... | collective-permute-start | bytes 4718600 | tf_op jit(solution)/shard_map/ppermute | solution.py:17
  20.9 3.3 %all-to-all-start.3 = ((bf16[2,144,128]{2,1,0:T(8,128)(2,1)}), bf16[2,144,128]{2,1,0:T(8,128)(2,1)S(1)}, u32[]{:S(2)}, u32[]{:S(2)}) async-start(bf16[2,144,128]{2,1,0:T(8,128)(2,1)} %pad_maximum_fusion.3), calls=%async_computation.3 | async-start | bytes 147456 | tf_op jit(solution)/shard_map/all_to_all | solution.py:290
  27.4 1.6 fusion.5
  29.0 2.0 bitcast_select_fusion.1
  32.1 122.1 %conditional.1 = (bf16[288,4096]{1,0:T(8,128)(2,1)}, bf16[288,4096]{1,0:T(8,128)(2,1)}, bf16[288,4096]{1,0:T(8,128)(2,1)}, bf16[288,4096]{1,0:T(8,128)(2,1)}) conditional(s32[]{:T(128)} %convert_element_type.8, () %tuple.68, (s32[]{:T(128)}, s32[8,2]{0,1:T(2,128)S(1)}, s32[]{:T(128)}, s32[]{:T(128)}, s32[]{:T(128)}, /*index=5*/s32[]{:T(128)}, ...), branch_computations={%region_1.2_spmd, %region_2.4_spmd} | conditional | flops 854905 | bytes 51536116 | solution.py:330
  32.1 0.9 broadcast_in_dim.31
  33.0 4.7 %all-to-all-start = ((bf16[8,288,128]{2,1,0:T(8,128)(2,1)}), bf16[8,288,128]{2,1,0:T(8,128)(2,1)S(1)}, u32[]{:S(2)}, u32[]{:S(2)}) async-start(bf16[8,288,128]{2,1,0:T(8,128)(2,1)} %broadcast_in_dim.31), calls=%async_computation | async-start | bytes 1179648 | tf_op jit(solution)/shard_map/cond/branch_1_fun/all_to_all | solution.py:250
  37.6 1.9 collective-permute-start
  40.3 1.1 collective-permute-done.other_ref
  41.4 3.9 %lookup.1 = bf16[1152,128]{1,0:T(8,128)(2,1)S(1)} custom-call(s32[1152,1]{1,0:T(8,128)S(1)} %reshape_squeeze.12.low_ref, s32[1152,1]{1,0:T(8,128)S(1)} %reshape_squeeze.13.high_ref, bf16[64,4096]{1,0:T(8,128)(2,1)S(1)} %get-tuple-element.106.own_ref, bf16[64,4096]{1,0:T(8,128)(2,1)S(1)} %collective-permute-done.other_ref), custom_call_target="tpu_custom_call" | custom-call | tf_op jit(solution)/shard_map/cond/branch_1_fun/lookup/pallas_call | solution.py:57
  45.3 0.8 pad_maximum_fusion
  46.1 10.3 %all-to-all-done.refs_0_ = bf16[8,288,128]{2,1,0:T(8,128)(2,1)S(1)} async-done(((bf16[8,288,128]{2,1,0:T(8,128)(2,1)}), bf16[8,288,128]{2,1,0:T(8,128)(2,1)S(1)}, u32[]{:S(2)}, u32[]{:S(2)}) %all-to-all-start) | async-done | bytes 589856 | tf_op jit(solution)/shard_map/cond/branch_1_fun/all_to_all | solution.py:250
  56.4 7.4 %all-to-all-start.1 = ((bf16[8,176,128]{2,1,0:T(8,128)(2,1)}), bf16[8,176,128]{2,1,0:T(8,128)(2,1)S(1)}, u32[]{:S(2)}, u32[]{:S(2)}) async-start(bf16[8,176,128]{2,1,0:T(8,128)(2,1)} %pad_maximum_fusion), calls=%async_computation.1 | async-start | bytes 720896 | tf_op jit(solution)/shard_map/cond/branch_1_fun/all_to_all | solution.py:310
  63.8 4.4 %collective-permute-start.2 = (bf16[8,288,128]{2,1,0:T(8,128)(2,1)S(1)}, bf16[8,288,128]{2,1,0:T(8,128)(2,1)S(1)}, u32[]{:S(2)}, u32[]{:S(2)}) collective-permute-start(bf16[8,288,128]{2,1,0:T(8,128)(2,1)S(1)} %all-to-all-done.refs_0_), channel_id=1, source_target_pairs={{0,6},{2,0},{4,2},{6,4},{1,7},{3,1},{5,3},{7,5},{8,14},{10,8},{12,... | collective-permute-start | bytes 1769480 | tf_op jit(solution)/shard_map/cond/branch_1_fun/ppermute | solution.py:17
  68.1 1.9 collective-permute-start.1
  70.1 10.0 %collective-permute-done.2.refs_2_ = bf16[8,288,128]{2,1,0:T(8,128)(2,1)S(1)} collective-permute-done((bf16[8,288,128]{2,1,0:T(8,128)(2,1)S(1)}, bf16[8,288,128]{2,1,0:T(8,128)(2,1)S(1)}, u32[]{:S(2)}, u32[]{:S(2)}) %collective-permute-start.2) | collective-permute-done | bytes 589856 | tf_op jit(solution)/shard_map/cond/branch_1_fun/ppermute | solution.py:17
  80.1 5.1 %collective-permute-done.1.refs_1_ = bf16[8,288,128]{2,1,0:T(8,128)(2,1)S(1)} collective-permute-done((bf16[8,288,128]{2,1,0:T(8,128)(2,1)S(1)}, bf16[8,288,128]{2,1,0:T(8,128)(2,1)S(1)}, u32[]{:S(2)}, u32[]{:S(2)}) %collective-permute-start.1) | collective-permute-done | bytes 589856 | tf_op jit(solution)/shard_map/cond/branch_1_fun/ppermute | solution.py:17
  85.3 0.9 broadcast_in_dim.32
  86.2 3.5 %all-to-all-start.2 = ((bf16[8,288,128]{2,1,0:T(8,128)(2,1)}), bf16[8,288,128]{2,1,0:T(8,128)(2,1)S(1)}, u32[]{:S(2)}, u32[]{:S(2)}) async-start(bf16[8,288,128]{2,1,0:T(8,128)(2,1)} %broadcast_in_dim.32), calls=%async_computation.2 | async-start | bytes 1179648 | tf_op jit(solution)/shard_map/cond/branch_1_fun/all_to_all | solution.py:250
  89.8 1.9 collective-permute-start.4
  91.7 3.4 %collective-permute-start.3 = (bf16[4,288,128]{2,1,0:T(8,128)(2,1)S(1)}, bf16[4,288,128]{2,1,0:T(8,128)(2,1)S(1)}, u32[]{:S(2)}, u32[]{:S(2)}) collective-permute-start(bf16[4,288,128]{2,1,0:T(8,128)(2,1)S(1)} %slice.57), channel_id=1, source_target_pairs={{0,2},{2,4},{4,6},{6,0},{1,3},{3,5},{5,7},{7,1},{8,10},{10,12},{12... | collective-permute-start | bytes 884744 | tf_op jit(solution)/shard_map/cond/branch_1_fun/ppermute | solution.py:17
  95.1 3.3 %collective-permute-done.4.refs_4_ = bf16[4,288,128]{2,1,0:T(8,128)(2,1)S(1)} collective-permute-done((bf16[4,288,128]{2,1,0:T(8,128)(2,1)S(1)}, bf16[4,288,128]{2,1,0:T(8,128)(2,1)S(1)}, u32[]{:S(2)}, u32[]{:S(2)}) %collective-permute-start.4) | collective-permute-done | bytes 294944 | tf_op jit(solution)/shard_map/cond/branch_1_fun/ppermute | solution.py:17
  99.2 2.4 %collective-permute-done.3.refs_3_ = bf16[4,288,128]{2,1,0:T(8,128)(2,1)S(1)} collective-permute-done((bf16[4,288,128]{2,1,0:T(8,128)(2,1)S(1)}, bf16[4,288,128]{2,1,0:T(8,128)(2,1)S(1)}, u32[]{:S(2)}, u32[]{:S(2)}) %collective-permute-start.3) | collective-permute-done | bytes 294944 | tf_op jit(solution)/shard_map/cond/branch_1_fun/ppermute | solution.py:17
  102.3 5.1 %all-to-all-done.2.refs_0_ = bf16[8,288,128]{2,1,0:T(8,128)(2,1)S(1)} async-done(((bf16[8,288,128]{2,1,0:T(8,128)(2,1)}), bf16[8,288,128]{2,1,0:T(8,128)(2,1)S(1)}, u32[]{:S(2)}, u32[]{:S(2)}) %all-to-all-start.2) | async-done | bytes 589856 | tf_op jit(solution)/shard_map/cond/branch_1_fun/all_to_all | solution.py:250
  107.4 1.9 collective-permute-start.6
  109.3 3.4 %collective-permute-start.5 = (bf16[8,288,128]{2,1,0:T(8,128)(2,1)S(1)}, bf16[8,288,128]{2,1,0:T(8,128)(2,1)S(1)}, u32[]{:S(2)}, u32[]{:S(2)}) collective-permute-start(bf16[8,288,128]{2,1,0:T(8,128)(2,1)S(1)} %all-to-all-done.2.refs_0_), channel_id=1, source_target_pairs={{0,2},{2,4},{4,6},{6,0},{1,3},{3,5},{5,7},{7,1},{8,10},{10,12},{12... | collective-permute-start | bytes 1769480 | tf_op jit(solution)/shard_map/cond/branch_1_fun/ppermute | solution.py:17
  115.6 0.8 slice.87
  117.0 4.6 %collective-permute-start.9 = (bf16[2,32,128]{2,1,0:T(8,128)(2,1)}, bf16[2,32,128]{2,1,0:T(8,128)(2,1)}, u32[]{:S(2)}, u32[]{:S(2)}) collective-permute-start(bf16[2,32,128]{2,1,0:T(8,128)(2,1)} %dynamic-slice_bitcast_fusion), channel_id=1, source_target_pairs={{0,64},{64,0},{1,65},{65,1},{2,66},{66,2},{3,67},{67,3},{4,68},{68... | collective-permute-start | bytes 49160 | tf_op jit(solution)/shard_map/cond/branch_1_fun/ppermute | solution.py:17
  122.3 1.0 copy-done.1
  123.3 1.0 copy-done.3
  124.2 3.2 %merge.1 = bf16[288,4096]{1,0:T(8,128)(2,1)} custom-call(s32[3]{0:T(128)S(1)} %pad_add_fusion.info_ref, bf16[8,288,128]{2,1,0:T(8,128)(2,1)S(1)} %all-to-all-done.refs_0_, bf16[8,288,128]{2,1,0:T(8,128)(2,1)S(1)} %collective-permute-done.1.refs_1_, bf16[8,288,128]{2,1,0:T(8,128)(2,1)S(1)} %collective-permute-done.2.refs_2_, ...), custom_call_target="tpu_custom_call" | custom-call | tf_op jit(solution)/shard_map/cond/branch_1_fun/merge/pallas_call | solution.py:146
  127.5 2.8 %collective-permute-start.8 = (bf16[4,288,128]{2,1,0:T(8,128)(2,1)S(1)}, bf16[4,288,128]{2,1,0:T(8,128)(2,1)S(1)}, u32[]{:S(2)}, u32[]{:S(2)}) collective-permute-start(bf16[4,288,128]{2,1,0:T(8,128)(2,1)S(1)} %slice.60), channel_id=1, source_target_pairs={{0,6},{2,0},{4,2},{6,4},{1,7},{3,1},{5,3},{7,5},{8,14},{10,8},{12,... | collective-permute-start | bytes 884744 | tf_op jit(solution)/shard_map/cond/branch_1_fun/ppermute | solution.py:17
  130.4 2.4 %collective-permute-start.7 = (bf16[4,288,128]{2,1,0:T(8,128)(2,1)S(1)}, bf16[4,288,128]{2,1,0:T(8,128)(2,1)S(1)}, u32[]{:S(2)}, u32[]{:S(2)}) collective-permute-start(bf16[4,288,128]{2,1,0:T(8,128)(2,1)S(1)} %slice.59), channel_id=1, source_target_pairs={{0,2},{2,4},{4,6},{6,0},{1,3},{3,5},{5,7},{7,1},{8,10},{10,12},{12... | collective-permute-start | bytes 884744 | tf_op jit(solution)/shard_map/cond/branch_1_fun/ppermute | solution.py:17
  132.8 0.8 select_convert_fusion
  133.6 3.1 %collective-permute-start.11 = (bf16[288,4096]{1,0:T(8,128)(2,1)}, bf16[288,4096]{1,0:T(8,128)(2,1)}, u32[]{:S(2)}, u32[]{:S(2)}) collective-permute-start(bf16[288,4096]{1,0:T(8,128)(2,1)} %merge.1), channel_id=1, source_target_pairs={{0,64},{64,0},{1,65},{65,1},{2,66},{66,2},{3,67},{67,3},{4,68},{68... | collective-permute-start | bytes 7077896 | tf_op jit(solution)/shard_map/cond/branch_1_fun/ppermute | solution.py:17
  137.3 4.5 %collective-permute-done.7.refs_3_ = bf16[4,288,128]{2,1,0:T(8,128)(2,1)S(1)} collective-permute-done((bf16[4,288,128]{2,1,0:T(8,128)(2,1)S(1)}, bf16[4,288,128]{2,1,0:T(8,128)(2,1)S(1)}, u32[]{:S(2)}, u32[]{:S(2)}) %collective-permute-start.7) | collective-permute-done | bytes 294944 | tf_op jit(solution)/shard_map/cond/branch_1_fun/ppermute | solution.py:17
  141.8 4.8 %norm.1 = bf16[288,4096]{1,0:T(8,128)(2,1)} custom-call(s32[3]{0:T(128)S(1)} %pad_add_fusion.info_ref, bf16[8,288,128]{2,1,0:T(8,128)(2,1)S(1)} %all-to-all-done.2.refs_0_, bf16[8,288,128]{2,1,0:T(8,128)(2,1)S(1)} %collective-permute-done.5.refs_1_, bf16[8,288,128]{2,1,0:T(8,128)(2,1)S(1)} %collective-permute-done.6.refs_2_, ...), custom_call_target="tpu_custom_call" | custom-call | tf_op jit(solution)/shard_map/cond/branch_1_fun/norm/pallas_call | solution.py:146
  146.6 3.0 %collective-permute-start.10 = (bf16[288,4096]{1,0:T(8,128)(2,1)}, bf16[288,4096]{1,0:T(8,128)(2,1)}, u32[]{:S(2)}, u32[]{:S(2)}) collective-permute-start(bf16[288,4096]{1,0:T(8,128)(2,1)} %norm.1), channel_id=1, source_target_pairs={{0,64},{64,0},{1,65},{65,1},{2,66},{66,2},{3,67},{67,3},{4,68},{68... | collective-permute-start | bytes 7077896 | tf_op jit(solution)/shard_map/cond/branch_1_fun/ppermute | solution.py:17
  149.6 4.5 %collective-permute-done.10 = bf16[288,4096]{1,0:T(8,128)(2,1)} collective-permute-done((bf16[288,4096]{1,0:T(8,128)(2,1)}, bf16[288,4096]{1,0:T(8,128)(2,1)}, u32[]{:S(2)}, u32[]{:S(2)}) %collective-permute-start.10) | collective-permute-done | bytes 2359328 | tf_op jit(solution)/shard_map/cond/branch_1_fun/ppermute | solution.py:17
  154.1 9.3 %gradients.1 = bf16[8,2,96,1024]{3,2,1,0:T(8,128)(2,1)} custom-call(bf16[288,4096]{1,0:T(8,128)(2,1)} %get-tuple-element.130.normed0, bf16[288,4096]{1,0:T(8,128)(2,1)} %get-tuple-element.131.normed1, bf16[288,4096]{1,0:T(8,128)(2,1)} %get-tuple-element.132.up0, bf16[288,4096]{1,0:T(8,128)(2,1)} %get-tuple-element.133.up1, ...), custom_call_target="tpu_custom_call" | custom-call | tf_op jit(solution)/shard_map/gradients/pallas_call | solution.py:229
  163.4 39.9 %reduce-scatter.2.cloned.1.call-done = bf16[2,96,1024]{2,1,0:T(8,128)(2,1)} async-done(((bf16[16,96,1024]{2,1,0:T(8,128)(2,1)}), bf16[2,96,1024]{2,1,0:T(8,128)(2,1)}) %reduce-scatter.2.cloned.1.call-update) | async-done | bytes 393232 | tf_op jit(solution)/shard_map/reduce_scatter | solution.py:335
  203.3 1.0 broadcast_select_fusion.2
  204.3 5.5 %collective-permute-start.13 = (bf16[2,96,512]{2,1,0:T(8,128)(2,1)S(1)}, bf16[2,96,512]{2,1,0:T(8,128)(2,1)S(1)}, u32[]{:S(2)}, u32[]{:S(2)}) collective-permute-start(bf16[2,96,512]{2,1,0:T(8,128)(2,1)S(1)} %broadcast_select_fusion.2), channel_id=1, source_target_pairs={{0,64},{64,0},{1,65},{65,1},{2,66},{66,2},{3,67},{67,3},{4,68},{68... | collective-permute-start | bytes 589832 | tf_op jit(solution)/shard_map/ppermute | solution.py:17
  209.8 1.0 collective-permute-done.13
  210.9 1.1 broadcast_select_fusion
  211.9 0.8 fusion.8
  (65 shorter events, 7.4 us)
Async XLA Ops:
  9.3 10.2 %copy-start.7 = (bf16[1,576,64]{1,2,0:T(8,128)(2,1)S(1)}, bf16[1,576,64]{1,2,0:T(8,128)(2,1)}, u32[]{:S(2)}) copy-start(bf16[1,576,64]{1,2,0:T(8,128)(2,1)} %param.17) | copy-start | bytes 221188
  9.4 14.9 %copy-start.11 = (s32[8,2]{0,1:T(2,128)S(1)}, s32[8,2]{0,1:T(2,128)}, u32[]{:S(2)}) copy-start(s32[8,2]{0,1:T(2,128)} %param.11) | copy-start | bytes 196
  10.7 16.6 %collective-permute-start.12 = (bf16[2,96,4096]{2,1,0:T(8,128)(2,1)}, bf16[2,96,4096]{2,1,0:T(8,128)(2,1)}, u32[]{:S(2)}, u32[]{:S(2)}) collective-permute-start(bf16[2,96,4096]{2,1,0:T(8,128)(2,1)} %fusion.3), channel_id=1, source_target_pairs={{0,64},{64,0},{1,65},{65,1},{2,66},{66,2},{3,67},{67,3},{4,68},{68... | collective-permute-start | bytes 4718600 | tf_op jit(solution)/shard_map/ppermute | solution.py:17
  20.9 10.1 %all-to-all-start.3 = ((bf16[2,144,128]{2,1,0:T(8,128)(2,1)}), bf16[2,144,128]{2,1,0:T(8,128)(2,1)S(1)}, u32[]{:S(2)}, u32[]{:S(2)}) async-start(bf16[2,144,128]{2,1,0:T(8,128)(2,1)} %pad_maximum_fusion.3), calls=%async_computation.3 | async-start | bytes 147456 | tf_op jit(solution)/shard_map/all_to_all | solution.py:290
  24.2 129.9 %all-reduce.2.cloned.1.call-start = ((), (), s32[]{:S(2)}) async-start(), calls=%async_computation.5 | async-start | bytes 6291456 | tf_op jit(solution)/shard_map/psum | solution.py:302
  31.0 0.7 copy-start.9
  31.0 0.8 copy-start.10
  31.0 1.1 copy-start.5
  31.0 1.1 copy-start.8
  31.0 172.3 %reduce-scatter.2.cloned.1.call-start = ((), (), s32[]{:S(2)}) async-start(), calls=%async_computation.6 | async-start | bytes 3538944 | tf_op jit(solution)/shard_map/reduce_scatter | solution.py:335
  33.0 23.4 %all-to-all-start = ((bf16[8,288,128]{2,1,0:T(8,128)(2,1)}), bf16[8,288,128]{2,1,0:T(8,128)(2,1)S(1)}, u32[]{:S(2)}, u32[]{:S(2)}) async-start(bf16[8,288,128]{2,1,0:T(8,128)(2,1)} %broadcast_in_dim.31), calls=%async_computation | async-start | bytes 1179648 | tf_op jit(solution)/shard_map/cond/branch_1_fun/all_to_all | solution.py:250
  37.6 3.8 %collective-permute-start = (bf16[64,4096]{1,0:T(8,128)(2,1)S(1)}, bf16[64,4096]{1,0:T(8,128)(2,1)S(1)}, u32[]{:S(2)}, u32[]{:S(2)}) collective-permute-start(bf16[64,4096]{1,0:T(8,128)(2,1)S(1)} %get-tuple-element.106.own_ref), channel_id=1, source_target_pairs={{0,64},{64,0},{1,65},{65,1},{2,66},{66,2},{3,67},{67,3},{4,68},{68... | collective-permute-start | bytes 1572872 | tf_op jit(solution)/shard_map/cond/branch_1_fun/ppermute | solution.py:17
  56.4 28.9 %all-to-all-start.1 = ((bf16[8,176,128]{2,1,0:T(8,128)(2,1)}), bf16[8,176,128]{2,1,0:T(8,128)(2,1)S(1)}, u32[]{:S(2)}, u32[]{:S(2)}) async-start(bf16[8,176,128]{2,1,0:T(8,128)(2,1)} %pad_maximum_fusion), calls=%async_computation.1 | async-start | bytes 720896 | tf_op jit(solution)/shard_map/cond/branch_1_fun/all_to_all | solution.py:310
  63.8 16.4 %collective-permute-start.2 = (bf16[8,288,128]{2,1,0:T(8,128)(2,1)S(1)}, bf16[8,288,128]{2,1,0:T(8,128)(2,1)S(1)}, u32[]{:S(2)}, u32[]{:S(2)}) collective-permute-start(bf16[8,288,128]{2,1,0:T(8,128)(2,1)S(1)} %all-to-all-done.refs_0_), channel_id=1, source_target_pairs={{0,6},{2,0},{4,2},{6,4},{1,7},{3,1},{5,3},{7,5},{8,14},{10,8},{12,... | collective-permute-start | bytes 1769480 | tf_op jit(solution)/shard_map/cond/branch_1_fun/ppermute | solution.py:17
  68.1 17.1 %collective-permute-start.1 = (bf16[8,288,128]{2,1,0:T(8,128)(2,1)S(1)}, bf16[8,288,128]{2,1,0:T(8,128)(2,1)S(1)}, u32[]{:S(2)}, u32[]{:S(2)}) collective-permute-start(bf16[8,288,128]{2,1,0:T(8,128)(2,1)S(1)} %all-to-all-done.refs_0_), channel_id=1, source_target_pairs={{0,2},{2,4},{4,6},{6,0},{1,3},{3,5},{5,7},{7,1},{8,10},{10,12},{12... | collective-permute-start | bytes 1769480 | tf_op jit(solution)/shard_map/cond/branch_1_fun/ppermute | solution.py:17
  85.2 1.0 copy-start.4
  86.2 21.2 %all-to-all-start.2 = ((bf16[8,288,128]{2,1,0:T(8,128)(2,1)}), bf16[8,288,128]{2,1,0:T(8,128)(2,1)S(1)}, u32[]{:S(2)}, u32[]{:S(2)}) async-start(bf16[8,288,128]{2,1,0:T(8,128)(2,1)} %broadcast_in_dim.32), calls=%async_computation.2 | async-start | bytes 1179648 | tf_op jit(solution)/shard_map/cond/branch_1_fun/all_to_all | solution.py:250
  89.8 8.6 %collective-permute-start.4 = (bf16[4,288,128]{2,1,0:T(8,128)(2,1)S(1)}, bf16[4,288,128]{2,1,0:T(8,128)(2,1)S(1)}, u32[]{:S(2)}, u32[]{:S(2)}) collective-permute-start(bf16[4,288,128]{2,1,0:T(8,128)(2,1)S(1)} %slice.58), channel_id=1, source_target_pairs={{0,6},{2,0},{4,2},{6,4},{1,7},{3,1},{5,3},{7,5},{8,14},{10,8},{12,... | collective-permute-start | bytes 884744 | tf_op jit(solution)/shard_map/cond/branch_1_fun/ppermute | solution.py:17
  91.7 9.8 %collective-permute-start.3 = (bf16[4,288,128]{2,1,0:T(8,128)(2,1)S(1)}, bf16[4,288,128]{2,1,0:T(8,128)(2,1)S(1)}, u32[]{:S(2)}, u32[]{:S(2)}) collective-permute-start(bf16[4,288,128]{2,1,0:T(8,128)(2,1)S(1)} %slice.57), channel_id=1, source_target_pairs={{0,2},{2,4},{4,6},{6,0},{1,3},{3,5},{5,7},{7,1},{8,10},{10,12},{12... | collective-permute-start | bytes 884744 | tf_op jit(solution)/shard_map/cond/branch_1_fun/ppermute | solution.py:17
  98.4 0.7 copy-start
  101.6 0.7 copy-start.2
  107.4 20.1 %collective-permute-start.6 = (bf16[8,288,128]{2,1,0:T(8,128)(2,1)S(1)}, bf16[8,288,128]{2,1,0:T(8,128)(2,1)S(1)}, u32[]{:S(2)}, u32[]{:S(2)}) collective-permute-start(bf16[8,288,128]{2,1,0:T(8,128)(2,1)S(1)} %all-to-all-done.2.refs_0_), channel_id=1, source_target_pairs={{0,6},{2,0},{4,2},{6,4},{1,7},{3,1},{5,3},{7,5},{8,14},{10,8},{12,... | collective-permute-start | bytes 1769480 | tf_op jit(solution)/shard_map/cond/branch_1_fun/ppermute | solution.py:17
  109.3 18.2 %collective-permute-start.5 = (bf16[8,288,128]{2,1,0:T(8,128)(2,1)S(1)}, bf16[8,288,128]{2,1,0:T(8,128)(2,1)S(1)}, u32[]{:S(2)}, u32[]{:S(2)}) collective-permute-start(bf16[8,288,128]{2,1,0:T(8,128)(2,1)S(1)} %all-to-all-done.2.refs_0_), channel_id=1, source_target_pairs={{0,2},{2,4},{4,6},{6,0},{1,3},{3,5},{5,7},{7,1},{8,10},{10,12},{12... | collective-permute-start | bytes 1769480 | tf_op jit(solution)/shard_map/cond/branch_1_fun/ppermute | solution.py:17
  116.4 5.2 %copy-start.6 = (bf16[4,2,32,128]{3,2,1,0:T(8,128)(2,1)}, bf16[4,2,32,128]{3,2,1,0:T(8,128)(2,1)S(1)}, u32[]{:S(2)}) copy-start(bf16[4,2,32,128]{3,2,1,0:T(8,128)(2,1)S(1)} %slice.87) | copy-start | bytes 196612 | tf_op jit(solution)/shard_map/cond
  117.0 15.8 %collective-permute-start.9 = (bf16[2,32,128]{2,1,0:T(8,128)(2,1)}, bf16[2,32,128]{2,1,0:T(8,128)(2,1)}, u32[]{:S(2)}, u32[]{:S(2)}) collective-permute-start(bf16[2,32,128]{2,1,0:T(8,128)(2,1)} %dynamic-slice_bitcast_fusion), channel_id=1, source_target_pairs={{0,64},{64,0},{1,65},{65,1},{2,66},{66,2},{3,67},{67,3},{4,68},{68... | collective-permute-start | bytes 49160 | tf_op jit(solution)/shard_map/cond/branch_1_fun/ppermute | solution.py:17
  122.3 1.0 copy-start.1
  123.3 1.0 copy-start.3
  127.5 9.8 %collective-permute-start.8 = (bf16[4,288,128]{2,1,0:T(8,128)(2,1)S(1)}, bf16[4,288,128]{2,1,0:T(8,128)(2,1)S(1)}, u32[]{:S(2)}, u32[]{:S(2)}) collective-permute-start(bf16[4,288,128]{2,1,0:T(8,128)(2,1)S(1)} %slice.60), channel_id=1, source_target_pairs={{0,6},{2,0},{4,2},{6,4},{1,7},{3,1},{5,3},{7,5},{8,14},{10,8},{12,... | collective-permute-start | bytes 884744 | tf_op jit(solution)/shard_map/cond/branch_1_fun/ppermute | solution.py:17
  130.4 11.4 %collective-permute-start.7 = (bf16[4,288,128]{2,1,0:T(8,128)(2,1)S(1)}, bf16[4,288,128]{2,1,0:T(8,128)(2,1)S(1)}, u32[]{:S(2)}, u32[]{:S(2)}) collective-permute-start(bf16[4,288,128]{2,1,0:T(8,128)(2,1)S(1)} %slice.59), channel_id=1, source_target_pairs={{0,2},{2,4},{4,6},{6,0},{1,3},{3,5},{5,7},{7,1},{8,10},{10,12},{12... | collective-permute-start | bytes 884744 | tf_op jit(solution)/shard_map/cond/branch_1_fun/ppermute | solution.py:17
  133.6 16.0 %collective-permute-start.11 = (bf16[288,4096]{1,0:T(8,128)(2,1)}, bf16[288,4096]{1,0:T(8,128)(2,1)}, u32[]{:S(2)}, u32[]{:S(2)}) collective-permute-start(bf16[288,4096]{1,0:T(8,128)(2,1)} %merge.1), channel_id=1, source_target_pairs={{0,64},{64,0},{1,65},{65,1},{2,66},{66,2},{3,67},{67,3},{4,68},{68... | collective-permute-start | bytes 7077896 | tf_op jit(solution)/shard_map/cond/branch_1_fun/ppermute | solution.py:17
  146.6 7.5 %collective-permute-start.10 = (bf16[288,4096]{1,0:T(8,128)(2,1)}, bf16[288,4096]{1,0:T(8,128)(2,1)}, u32[]{:S(2)}, u32[]{:S(2)}) collective-permute-start(bf16[288,4096]{1,0:T(8,128)(2,1)} %norm.1), channel_id=1, source_target_pairs={{0,64},{64,0},{1,65},{65,1},{2,66},{66,2},{3,67},{67,3},{4,68},{68... | collective-permute-start | bytes 7077896 | tf_op jit(solution)/shard_map/cond/branch_1_fun/ppermute | solution.py:17
  204.3 6.5 %collective-permute-start.13 = (bf16[2,96,512]{2,1,0:T(8,128)(2,1)S(1)}, bf16[2,96,512]{2,1,0:T(8,128)(2,1)S(1)}, u32[]{:S(2)}, u32[]{:S(2)}) collective-permute-start(bf16[2,96,512]{2,1,0:T(8,128)(2,1)S(1)} %broadcast_select_fusion.2), channel_id=1, source_target_pairs={{0,64},{64,0},{1,65},{65,1},{2,66},{66,2},{3,67},{67,3},{4,68},{68... | collective-permute-start | bytes 589832 | tf_op jit(solution)/shard_map/ppermute | solution.py:17
Sparse Core Ops, SparseCore 0:
  31.1 102.3 all-reduce.1
  163.5 39.7 reduce-scatter.1

commit v6 on v4

--- a/solution.py
+++ b/solution.py
@@ -154,22 +154,45 @@
     )(info, *blocks, *extra)
 
 
-def stage_kernel(flag_ref, first_ref, second_ref, out_ref):
-    rows = first_ref.shape[0]
-    for j, ref in enumerate((first_ref, second_ref)):
-        kept = jnp.where(flag_ref[0] == 1, ref[...].astype(f32), 0.0)
-        out_ref[0, j * rows:(j + 1) * rows, :] = kept.astype(bf16)
+def stage_kernel(flag_ref, first, second, out, come, leave, come_sem, leave_sem):
+    units, width = first.shape
+    half, step = units // 2, width // 4
+    copies = []
+    for k in range(4):
+        columns = pl.ds(k * step, step)
+        for j, source in enumerate((first, second)):
+            copies.append(
+                pltpu.make_async_copy(source.at[:, columns], come.at[k, j], come_sem.at[k, j])
+            )
+            copies[-1].start()
+    leaving = []
+    for k in range(4):
+        for j in range(2):
+            copies[2 * k + j].wait()
+            for c in range(2):
+                kept = come[k, j, c * half:(c + 1) * half, :].astype(f32)
+                kept = jnp.where(flag_ref[0] == 1, kept, 0.0)
+                leave[2 * k + c, j * half:(j + 1) * half, :] = kept.astype(bf16)
+        block = pl.ds(2 * k, 2)
+        leaving.append(pltpu.make_async_copy(leave.at[block], out.at[block], leave_sem.at[k]))
+        leaving[k].start()
+    for copy in leaving:
+        copy.wait()
 
 
 def stage(flag, first, second):
     units, width = first.shape
-    block = pl.BlockSpec((units // 2, width // 4), lambda i: (i % 2, i // 2))
     return pl.pallas_call(
         stage_kernel,
-        grid=(8,),
-        in_specs=[pl.BlockSpec(memory_space=pltpu.SMEM), block, block],
-        out_specs=pl.BlockSpec((1, units, width // 4), lambda i: (i, 0, 0)),
+        in_specs=[pl.BlockSpec(memory_space=pltpu.SMEM)] + [pl.BlockSpec(memory_space=pl.ANY)] * 2,
+        out_specs=pl.BlockSpec(memory_space=pl.ANY),
         out_shape=jax.ShapeDtypeStruct((8, units, width // 4), bf16),
+        scratch_shapes=[
+            pltpu.VMEM((4, 2, units, width // 4), bf16),
+            pltpu.VMEM((8, units, width // 4), bf16),
+            pltpu.SemaphoreType.DMA((4, 2)),
+            pltpu.SemaphoreType.DMA((4,)),
+        ],
         compiler_params=pltpu.CompilerParams(vmem_limit_bytes=60 * MIB),
         name="stage",
     )(flag, first, second)

time: 215 us -> 212 us (0.986)
  Pallas kernels: 29.2 us -> 25.8 us
    pallas_call x1, Pallas kernels: 6.46 us -> 2.99 us  [stage(): pl.pallas_call(stage_kernel, in_specs=[pl.BlockSpec(memory_space=pltpu.SM...]
where the time goes in v6:
time: 212 us; the launch traced here: 211 us
  waiting for transfers between devices  84.5 us (40%)
  starting transfers between devices  70.1 us (33%)
  Pallas kernels  25.8 us (12%)
  between operations  15.1 us (7%)
  local copies, waits for them, and re-layouts  6.31 us (3%)
  other arithmetic  6.02 us (3%)
  loops' own time  2.77 us (1%)
    reduce_scatter x1, waiting for transfers between devices, on_device(): lax.psum_scatter(terms, ('yh', 'yl'), scatter_dimension=0, tiled=True)  46.2 us
    ppermute x12, starting transfers between devices, shift(): lax.ppermute(value, axis, [(i, (i + by) % size) for i in range(size)])  45.3 us
    ppermute x12, waiting for transfers between devices, shift(): lax.ppermute(value, axis, [(i, (i + by) % size) for i in range(size)])  29.5 us
    all_to_all x1, starting transfers between devices, slots(): cot = lax.all_to_all(cot, ('z', 'yl'), 0, 0).reshape(8, half, 2 * cols)  12 us
    pallas_call x2, Pallas kernels, assemble(): pl.pallas_call(kernel, in_specs=[pl.BlockSpec(memory_space=pltpu.SMEM)] +...  9.64 us
    pallas_call x1, Pallas kernels, gradients(): pl.pallas_call(gradient_kernel, in_specs=[pl.BlockSpec(memory_space=pl.AN...  9.26 us
    all_to_all x1, starting transfers between devices, slots(): got = lax.all_to_all(sent, ('yh', 'yl'), 0, 0)  6.68 us
    all_to_all x1, waiting for transfers between devices, slots(): cot = lax.all_to_all(cot, ('z', 'yl'), 0, 0).reshape(8, half, 2 * cols)  6.02 us
  transfers between devices with their start and end apart: 18, of which 12 were waited for; matrix products, arithmetic and copies ran while one was open for 3% of the time, Pallas kernels for 6%

profile of v6, /device:TPU:1, one launch (start us, length us, event | category | flops | bytes accessed | tf_op | source)
XLA Modules:
  0.0 210.7 jit_solution(15688614153784160851)
XLA Ops:
  7.2 1.4 bitcast_select_fusion
  9.3 3.0 %stage.1 = bf16[8,192,1024]{2,1,0:T(8,128)(2,1)} custom-call(s32[1]{0:T(128)} %bitcast.12.flag_ref, bf16[192,4096]{1,0:T(8,128)(2,1)} %bitcast.48, bf16[192,4096]{1,0:T(8,128)(2,1)} %bitcast.49), custom_call_target="tpu_custom_call" | custom-call | tf_op jit(solution)/shard_map/stage/pallas_call | solution.py:185
  12.4 0.8 copy-done.1
  14.4 77.0 %conditional.2 = (f32[32,128]{1,0:T(8,128)S(1)}, f32[32,128]{1,0:T(8,128)S(1)}, bf16[8,288,128]{2,1,0:T(8,128)(2,1)}, bf16[8,288,128]{2,1,0:T(8,128)(2,1)}, bf16...) conditional(s32[]{:T(128)} %convert_element_type.8, () %tuple.35, ...), branch_computations={%region_1.2_spmd, %region_2.4_spmd} | conditional | flops 850717 | bytes 18120358 | solution.py:381
  14.5 0.9 broadcast_in_dim.11
  15.4 12.0 %all-to-all-start = ((bf16[16,144,128]{2,1,0:T(8,128)(2,1)}), bf16[16,144,128]{2,1,0:T(8,128)(2,1)}, u32[]{:S(2)}, u32[]{:S(2)}) async-start(bf16[16,144,128]{2,1,0:T(8,128)(2,1)} %bitcast.2), calls=%async_computation | async-start | bytes 1179648 | tf_op jit(solution)/shard_map/cond/branch_1_fun/all_to_all | solution.py:348
  27.4 2.9 %collective-permute-start.6 = (bf16[64,4224]{1,0:T(8,128)(2,1)S(1)}, bf16[64,4224]{1,0:T(8,128)(2,1)S(1)}, u32[]{:S(2)}, u32[]{:S(2)}) collective-permute-start(bf16[64,4224]{1,0:T(8,128)(2,1)S(1)} %get-tuple-element.64.own_ref), channel_id=1, source_target_pairs={{0,64},{64,0},{1,65},{65,1},{2,66},{66,2},{3,67},{67,3},{4,68},{68... | collective-permute-start | bytes 1622024 | tf_op jit(solution)/shard_map/cond/branch_1_fun/ppermute | solution.py:17
  32.3 0.3 reshape_squeeze.12.low_ref
  32.6 0.3 reshape_squeeze.13.high_ref
  32.9 3.9 %lookup.1 = bf16[1152,128]{1,0:T(8,128)(2,1)S(1)} custom-call(s32[1152,1]{1,0:T(8,128)S(1)} %reshape_squeeze.12.low_ref, s32[1152,1]{1,0:T(8,128)S(1)} %reshape_squeeze.13.high_ref, bf16[64,4224]{1,0:T(8,128)(2,1)S(1)} %get-tuple-element.64.own_ref, bf16[64,4224]{1,0:T(8,128)(2,1)S(1)} %collective-permute-done.6.other_ref), custom_call_target="tpu_custom_call" | custom-call | tf_op jit(solution)/shard_map/cond/branch_1_fun/lookup/pallas_call | solution.py:57
  36.8 0.8 pad_maximum_fusion
  37.6 6.0 %all-to-all-done = bf16[16,144,128]{2,1,0:T(8,128)(2,1)} async-done(((bf16[16,144,128]{2,1,0:T(8,128)(2,1)}), bf16[16,144,128]{2,1,0:T(8,128)(2,1)}, u32[]{:S(2)}, u32[]{:S(2)}) %all-to-all-start) | async-done | bytes 589856 | tf_op jit(solution)/shard_map/cond/branch_1_fun/all_to_all | solution.py:348
  43.6 6.7 %all-to-all-start.1 = ((bf16[8,176,128]{2,1,0:T(8,128)(2,1)}), bf16[8,176,128]{2,1,0:T(8,128)(2,1)S(1)}, u32[]{:S(2)}, u32[]{:S(2)}) async-start(bf16[8,176,128]{2,1,0:T(8,128)(2,1)} %pad_maximum_fusion), calls=%async_computation.1 | async-start | bytes 720896 | tf_op jit(solution)/shard_map/cond/branch_1_fun/all_to_all | solution.py:355
  50.3 3.1 %collective-permute-start.7 = (bf16[8,288,128]{2,1,0:T(8,128)(2,1)}, bf16[8,288,128]{2,1,0:T(8,128)(2,1)}, u32[]{:S(2)}, u32[]{:S(2)}) collective-permute-start(bf16[8,288,128]{2,1,0:T(8,128)(2,1)} %bitcast.3), channel_id=1, source_target_pairs={{0,2},{2,4},{4,6},{6,0},{1,3},{3,5},{5,7},{7,1},{8,10},{10,12},{12... | collective-permute-start | bytes 1769480 | tf_op jit(solution)/shard_map/cond/branch_1_fun/ppermute | solution.py:17
  53.4 3.4 %collective-permute-start.8 = (bf16[8,288,128]{2,1,0:T(8,128)(2,1)}, bf16[8,288,128]{2,1,0:T(8,128)(2,1)}, u32[]{:S(2)}, u32[]{:S(2)}) collective-permute-start(bf16[8,288,128]{2,1,0:T(8,128)(2,1)} %bitcast.3), channel_id=1, source_target_pairs={{0,6},{2,0},{4,2},{6,4},{1,7},{3,1},{5,3},{7,5},{8,14},{10,8},{12,... | collective-permute-start | bytes 1769480 | tf_op jit(solution)/shard_map/cond/branch_1_fun/ppermute | solution.py:17
  56.8 9.0 %collective-permute-done.7 = bf16[8,288,128]{2,1,0:T(8,128)(2,1)} collective-permute-done((bf16[8,288,128]{2,1,0:T(8,128)(2,1)}, bf16[8,288,128]{2,1,0:T(8,128)(2,1)}, u32[]{:S(2)}, u32[]{:S(2)}) %collective-permute-start.7) | collective-permute-done | bytes 589856 | tf_op jit(solution)/shard_map/cond/branch_1_fun/ppermute | solution.py:17
  65.7 1.6 collective-permute-done.8
  67.4 0.9 broadcast_in_dim.12
  68.3 6.0 %all-to-all-start.2 = ((bf16[8,288,128]{2,1,0:T(8,128)(2,1)}), bf16[8,288,128]{2,1,0:T(8,128)(2,1)}, u32[]{:S(2)}, u32[]{:S(2)}) async-start(bf16[8,288,128]{2,1,0:T(8,128)(2,1)} %broadcast_in_dim.12), calls=%async_computation.2 | async-start | bytes 1179648 | tf_op jit(solution)/shard_map/cond/branch_1_fun/all_to_all | solution.py:296
  74.9 1.0 slice.58
  75.9 4.6 %collective-permute-start.10 = (bf16[4,288,128]{2,1,0:T(8,128)(2,1)S(1)}, bf16[4,288,128]{2,1,0:T(8,128)(2,1)}, u32[]{:S(2)}, u32[]{:S(2)}) collective-permute-start(bf16[4,288,128]{2,1,0:T(8,128)(2,1)S(1)} %slice.58), channel_id=1, source_target_pairs={{0,6},{2,0},{4,2},{6,4},{1,7},{3,1},{5,3},{7,5},{8,14},{10,8},{12,... | collective-permute-start | bytes 884744 | tf_op jit(solution)/shard_map/cond/branch_1_fun/ppermute | solution.py:17
  80.5 1.0 slice.57
  81.5 1.9 collective-permute-start.9
  83.5 1.1 collective-permute-done.10
  84.5 6.1 %collective-permute-done.9 = bf16[4,288,128]{2,1,0:T(8,128)(2,1)} collective-permute-done((bf16[4,288,128]{2,1,0:T(8,128)(2,1)S(1)}, bf16[4,288,128]{2,1,0:T(8,128)(2,1)}, u32[]{:S(2)}, u32[]{:S(2)}) %collective-permute-start.9) | collective-permute-done | bytes 294944 | tf_op jit(solution)/shard_map/cond/branch_1_fun/ppermute | solution.py:17
  90.7 0.7 all-to-all-done.2
  91.4 0.6 dynamic_slice.11
  92.0 0.7 pad_add_fusion
  92.7 44.5 %conditional.3 = (bf16[288,4096]{1,0:T(8,128)(2,1)}, bf16[288,4096]{1,0:T(8,128)(2,1)}, bf16[288,4096]{1,0:T(8,128)(2,1)}, bf16[288,4096]{1,0:T(8,128)(2,1)}) conditional(s32[]{:T(128)} %convert_element_type.8, () %tuple.34, (bf16[8,288,128]{2,1,0:T(8,128)(2,1)}, s32[3]{0:T(128)S(1)}, bf16[8,288,128]{2,1,0:T(8,128)(2,1)}, ...), branch_computations={%region_5.6_spmd, %region_6.7_spmd} | conditional | bytes 27132176 | solution.py:384
  92.7 3.1 %collective-permute-start = (bf16[8,288,128]{2,1,0:T(8,128)(2,1)}, bf16[8,288,128]{2,1,0:T(8,128)(2,1)S(1)}, u32[]{:S(2)}, u32[]{:S(2)}) collective-permute-start(bf16[8,288,128]{2,1,0:T(8,128)(2,1)} %get-tuple-element.75.refs_0_), channel_id=1, source_target_pairs={{0,2},{2,4},{4,6},{6,0},{1,3},{3,5},{5,7},{7,1},{8,10},{10,12},{12... | collective-permute-start | bytes 1769480 | tf_op jit(solution)/shard_map/cond/branch_1_fun/ppermute | solution.py:17
  95.8 3.4 %collective-permute-start.1 = (bf16[8,288,128]{2,1,0:T(8,128)(2,1)}, bf16[8,288,128]{2,1,0:T(8,128)(2,1)S(1)}, u32[]{:S(2)}, u32[]{:S(2)}) collective-permute-start(bf16[8,288,128]{2,1,0:T(8,128)(2,1)} %get-tuple-element.75.refs_0_), channel_id=1, source_target_pairs={{0,6},{2,0},{4,2},{6,4},{1,7},{3,1},{5,3},{7,5},{8,14},{10,8},{12,... | collective-permute-start | bytes 1769480 | tf_op jit(solution)/shard_map/cond/branch_1_fun/ppermute | solution.py:17
  99.2 4.3 %merge.1 = bf16[288,4096]{1,0:T(8,128)(2,1)} custom-call(s32[3]{0:T(128)S(1)} %get-tuple-element.74.info_ref, bf16[8,288,128]{2,1,0:T(8,128)(2,1)} %get-tuple-element.76.refs_0_, bf16[8,288,128]{2,1,0:T(8,128)(2,1)} %get-tuple-element.77.refs_1_, bf16[8,288,128]{2,1,0:T(8,128)(2,1)} %get-tuple-element.78.refs_2_, ...), custom_call_target="tpu_custom_call" | custom-call | tf_op jit(solution)/shard_map/cond/branch_1_fun/merge/pallas_call | solution.py:146
  103.5 4.5 %collective-permute-done.refs_1_ = bf16[8,288,128]{2,1,0:T(8,128)(2,1)S(1)} collective-permute-done((bf16[8,288,128]{2,1,0:T(8,128)(2,1)}, bf16[8,288,128]{2,1,0:T(8,128)(2,1)S(1)}, u32[]{:S(2)}, u32[]{:S(2)}) %collective-permute-start) | collective-permute-done | bytes 589856 | tf_op jit(solution)/shard_map/cond/branch_1_fun/ppermute | solution.py:17
  108.0 1.7 collective-permute-done.1.refs_2_
  109.7 2.8 %collective-permute-start.2 = (bf16[4,288,128]{2,1,0:T(8,128)(2,1)S(1)}, bf16[4,288,128]{2,1,0:T(8,128)(2,1)S(1)}, u32[]{:S(2)}, u32[]{:S(2)}) collective-permute-start(bf16[4,288,128]{2,1,0:T(8,128)(2,1)S(1)} %slice.59), channel_id=1, source_target_pairs={{0,2},{2,4},{4,6},{6,0},{1,3},{3,5},{5,7},{7,1},{8,10},{10,12},{12... | collective-permute-start | bytes 884744 | tf_op jit(solution)/shard_map/cond/branch_1_fun/ppermute | solution.py:17
  112.6 3.7 %collective-permute-start.3 = (bf16[4,288,128]{2,1,0:T(8,128)(2,1)S(1)}, bf16[4,288,128]{2,1,0:T(8,128)(2,1)S(1)}, u32[]{:S(2)}, u32[]{:S(2)}) collective-permute-start(bf16[4,288,128]{2,1,0:T(8,128)(2,1)S(1)} %slice.60), channel_id=1, source_target_pairs={{0,6},{2,0},{4,2},{6,4},{1,7},{3,1},{5,3},{7,5},{8,14},{10,8},{12,... | collective-permute-start | bytes 884744 | tf_op jit(solution)/shard_map/cond/branch_1_fun/ppermute | solution.py:17
  116.3 6.4 %collective-permute-start.5 = (bf16[288,4096]{1,0:T(8,128)(2,1)}, bf16[288,4096]{1,0:T(8,128)(2,1)}, u32[]{:S(2)}, u32[]{:S(2)}) collective-permute-start(bf16[288,4096]{1,0:T(8,128)(2,1)} %merge.1), channel_id=1, source_target_pairs={{0,64},{64,0},{1,65},{65,1},{2,66},{66,2},{3,67},{67,3},{4,68},{68... | collective-permute-start | bytes 7077896 | tf_op jit(solution)/shard_map/cond/branch_1_fun/ppermute | solution.py:17
  122.8 5.3 %norm.1 = bf16[288,4096]{1,0:T(8,128)(2,1)} custom-call(s32[3]{0:T(128)S(1)} %get-tuple-element.74.info_ref, bf16[8,288,128]{2,1,0:T(8,128)(2,1)} %get-tuple-element.75.refs_0_, bf16[8,288,128]{2,1,0:T(8,128)(2,1)S(1)} %collective-permute-done.refs_1_, bf16[8,288,128]{2,1,0:T(8,128)(2,1)S(1)} %collective-permute-done.1.refs_2_, ...), custom_call_target="tpu_custom_call" | custom-call | tf_op jit(solution)/shard_map/cond/branch_1_fun/norm/pallas_call | solution.py:146
  128.1 4.6 %collective-permute-start.4 = (bf16[288,4096]{1,0:T(8,128)(2,1)}, bf16[288,4096]{1,0:T(8,128)(2,1)}, u32[]{:S(2)}, u32[]{:S(2)}) collective-permute-start(bf16[288,4096]{1,0:T(8,128)(2,1)} %norm.1), channel_id=1, source_target_pairs={{0,64},{64,0},{1,65},{65,1},{2,66},{66,2},{3,67},{67,3},{4,68},{68... | collective-permute-start | bytes 7077896 | tf_op jit(solution)/shard_map/cond/branch_1_fun/ppermute | solution.py:17
  132.7 4.5 %collective-permute-done.4 = bf16[288,4096]{1,0:T(8,128)(2,1)} collective-permute-done((bf16[288,4096]{1,0:T(8,128)(2,1)}, bf16[288,4096]{1,0:T(8,128)(2,1)}, u32[]{:S(2)}, u32[]{:S(2)}) %collective-permute-start.4) | collective-permute-done | bytes 2359328 | tf_op jit(solution)/shard_map/cond/branch_1_fun/ppermute | solution.py:17
  137.2 2.1 all-gather.2.cloned.1.call-done
  139.2 9.3 %gradients.1 = bf16[8,2,96,1024]{3,2,1,0:T(8,128)(2,1)} custom-call(bf16[288,4096]{1,0:T(8,128)(2,1)} %get-tuple-element.125.normed0, bf16[288,4096]{1,0:T(8,128)(2,1)} %get-tuple-element.126.normed1, bf16[288,4096]{1,0:T(8,128)(2,1)} %get-tuple-element.127.up0, bf16[288,4096]{1,0:T(8,128)(2,1)} %get-tuple-element.128.up1, bf16[8,192,1024]{2,1,0:T(8,128)(2,1)} %bitcast.47), custom_call_target="tpu_custom_call" | custom-call | tf_op jit(solution)/shard_map/gradients/pallas_call | solution.py:275
  148.5 46.2 %reduce-scatter.5.cloned.1.call-done = bf16[2,96,1024]{2,1,0:T(8,128)(2,1)} async-done(((bf16[16,96,1024]{2,1,0:T(8,128)(2,1)}), bf16[2,96,1024]{2,1,0:T(8,128)(2,1)}) %reduce-scatter.5.cloned.1.call-update) | async-done | bytes 393232 | tf_op jit(solution)/shard_map/reduce_scatter | solution.py:387
  194.7 1.0 broadcast_select_fusion.2
  195.8 5.4 %collective-permute-start.11 = (bf16[2,96,512]{2,1,0:T(8,128)(2,1)S(1)}, bf16[2,96,512]{2,1,0:T(8,128)(2,1)S(1)}, u32[]{:S(2)}, u32[]{:S(2)}) collective-permute-start(bf16[2,96,512]{2,1,0:T(8,128)(2,1)S(1)} %broadcast_select_fusion.2), channel_id=1, source_target_pairs={{0,64},{64,0},{1,65},{65,1},{2,66},{66,2},{3,67},{67,3},{4,68},{68... | collective-permute-start | bytes 589832 | tf_op jit(solution)/shard_map/ppermute | solution.py:17
  201.2 1.0 collective-permute-done.11
  202.3 1.1 broadcast_select_fusion
  203.4 0.8 fusion.5
  (43 shorter events, 1.1 us)
Async XLA Ops:
  7.2 84.2 %reduce-scatter.3.cloned.1.call-start = ((), (), s32[]{:S(2)}) async-start(), calls=%async_computation.5 | async-start | bytes 3538944 | tf_op jit(solution)/shard_map/reduce_scatter | solution.py:328
  12.3 0.9 copy-start.1
  12.3 1.0 copy-start.3
  12.3 1.1 copy-start.4
  12.3 2.0 copy-start
  12.3 2.0 copy-start.2
  12.3 126.9 %all-gather.2.cloned.1.call-start = ((), (), s32[]{:S(2)}) async-start(), calls=%async_computation.6 | async-start | bytes 3538944 | tf_op jit(solution)/shard_map/all_gather | solution.py:383
  15.4 28.2 %all-to-all-start = ((bf16[16,144,128]{2,1,0:T(8,128)(2,1)}), bf16[16,144,128]{2,1,0:T(8,128)(2,1)}, u32[]{:S(2)}, u32[]{:S(2)}) async-start(bf16[16,144,128]{2,1,0:T(8,128)(2,1)} %bitcast.2), calls=%async_computation | async-start | bytes 1179648 | tf_op jit(solution)/shard_map/cond/branch_1_fun/all_to_all | solution.py:348
  27.4 5.4 %collective-permute-start.6 = (bf16[64,4224]{1,0:T(8,128)(2,1)S(1)}, bf16[64,4224]{1,0:T(8,128)(2,1)S(1)}, u32[]{:S(2)}, u32[]{:S(2)}) collective-permute-start(bf16[64,4224]{1,0:T(8,128)(2,1)S(1)} %get-tuple-element.64.own_ref), channel_id=1, source_target_pairs={{0,64},{64,0},{1,65},{65,1},{2,66},{66,2},{3,67},{67,3},{4,68},{68... | collective-permute-start | bytes 1622024 | tf_op jit(solution)/shard_map/cond/branch_1_fun/ppermute | solution.py:17
  43.6 23.8 %all-to-all-start.1 = ((bf16[8,176,128]{2,1,0:T(8,128)(2,1)}), bf16[8,176,128]{2,1,0:T(8,128)(2,1)S(1)}, u32[]{:S(2)}, u32[]{:S(2)}) async-start(bf16[8,176,128]{2,1,0:T(8,128)(2,1)} %pad_maximum_fusion), calls=%async_computation.1 | async-start | bytes 720896 | tf_op jit(solution)/shard_map/cond/branch_1_fun/all_to_all | solution.py:355
  50.3 15.5 %collective-permute-start.7 = (bf16[8,288,128]{2,1,0:T(8,128)(2,1)}, bf16[8,288,128]{2,1,0:T(8,128)(2,1)}, u32[]{:S(2)}, u32[]{:S(2)}) collective-permute-start(bf16[8,288,128]{2,1,0:T(8,128)(2,1)} %bitcast.3), channel_id=1, source_target_pairs={{0,2},{2,4},{4,6},{6,0},{1,3},{3,5},{5,7},{7,1},{8,10},{10,12},{12... | collective-permute-start | bytes 1769480 | tf_op jit(solution)/shard_map/cond/branch_1_fun/ppermute | solution.py:17
  53.4 14.0 %collective-permute-start.8 = (bf16[8,288,128]{2,1,0:T(8,128)(2,1)}, bf16[8,288,128]{2,1,0:T(8,128)(2,1)}, u32[]{:S(2)}, u32[]{:S(2)}) collective-permute-start(bf16[8,288,128]{2,1,0:T(8,128)(2,1)} %bitcast.3), channel_id=1, source_target_pairs={{0,6},{2,0},{4,2},{6,4},{1,7},{3,1},{5,3},{7,5},{8,14},{10,8},{12,... | collective-permute-start | bytes 1769480 | tf_op jit(solution)/shard_map/cond/branch_1_fun/ppermute | solution.py:17
  68.3 23.1 %all-to-all-start.2 = ((bf16[8,288,128]{2,1,0:T(8,128)(2,1)}), bf16[8,288,128]{2,1,0:T(8,128)(2,1)}, u32[]{:S(2)}, u32[]{:S(2)}) async-start(bf16[8,288,128]{2,1,0:T(8,128)(2,1)} %broadcast_in_dim.12), calls=%async_computation.2 | async-start | bytes 1179648 | tf_op jit(solution)/shard_map/cond/branch_1_fun/all_to_all | solution.py:296
  75.9 8.6 %collective-permute-start.10 = (bf16[4,288,128]{2,1,0:T(8,128)(2,1)S(1)}, bf16[4,288,128]{2,1,0:T(8,128)(2,1)}, u32[]{:S(2)}, u32[]{:S(2)}) collective-permute-start(bf16[4,288,128]{2,1,0:T(8,128)(2,1)S(1)} %slice.58), channel_id=1, source_target_pairs={{0,6},{2,0},{4,2},{6,4},{1,7},{3,1},{5,3},{7,5},{8,14},{10,8},{12,... | collective-permute-start | bytes 884744 | tf_op jit(solution)/shard_map/cond/branch_1_fun/ppermute | solution.py:17
  81.5 9.2 %collective-permute-start.9 = (bf16[4,288,128]{2,1,0:T(8,128)(2,1)S(1)}, bf16[4,288,128]{2,1,0:T(8,128)(2,1)}, u32[]{:S(2)}, u32[]{:S(2)}) collective-permute-start(bf16[4,288,128]{2,1,0:T(8,128)(2,1)S(1)} %slice.57), channel_id=1, source_target_pairs={{0,2},{2,4},{4,6},{6,0},{1,3},{3,5},{5,7},{7,1},{8,10},{10,12},{12... | collective-permute-start | bytes 884744 | tf_op jit(solution)/shard_map/cond/branch_1_fun/ppermute | solution.py:17
  91.4 103.4 %reduce-scatter.5.cloned.1.call-start = ((), (), s32[]{:S(2)}) async-start(), calls=%async_computation.7 | async-start | bytes 3538944 | tf_op jit(solution)/shard_map/reduce_scatter | solution.py:387
  92.7 15.3 %collective-permute-start = (bf16[8,288,128]{2,1,0:T(8,128)(2,1)}, bf16[8,288,128]{2,1,0:T(8,128)(2,1)S(1)}, u32[]{:S(2)}, u32[]{:S(2)}) collective-permute-start(bf16[8,288,128]{2,1,0:T(8,128)(2,1)} %get-tuple-element.75.refs_0_), channel_id=1, source_target_pairs={{0,2},{2,4},{4,6},{6,0},{1,3},{3,5},{5,7},{7,1},{8,10},{10,12},{12... | collective-permute-start | bytes 1769480 | tf_op jit(solution)/shard_map/cond/branch_1_fun/ppermute | solution.py:17
  95.8 13.9 %collective-permute-start.1 = (bf16[8,288,128]{2,1,0:T(8,128)(2,1)}, bf16[8,288,128]{2,1,0:T(8,128)(2,1)S(1)}, u32[]{:S(2)}, u32[]{:S(2)}) collective-permute-start(bf16[8,288,128]{2,1,0:T(8,128)(2,1)} %get-tuple-element.75.refs_0_), channel_id=1, source_target_pairs={{0,6},{2,0},{4,2},{6,4},{1,7},{3,1},{5,3},{7,5},{8,14},{10,8},{12,... | collective-permute-start | bytes 1769480 | tf_op jit(solution)/shard_map/cond/branch_1_fun/ppermute | solution.py:17
  109.7 13.0 %collective-permute-start.2 = (bf16[4,288,128]{2,1,0:T(8,128)(2,1)S(1)}, bf16[4,288,128]{2,1,0:T(8,128)(2,1)S(1)}, u32[]{:S(2)}, u32[]{:S(2)}) collective-permute-start(bf16[4,288,128]{2,1,0:T(8,128)(2,1)S(1)} %slice.59), channel_id=1, source_target_pairs={{0,2},{2,4},{4,6},{6,0},{1,3},{3,5},{5,7},{7,1},{8,10},{10,12},{12... | collective-permute-start | bytes 884744 | tf_op jit(solution)/shard_map/cond/branch_1_fun/ppermute | solution.py:17
  112.6 10.1 %collective-permute-start.3 = (bf16[4,288,128]{2,1,0:T(8,128)(2,1)S(1)}, bf16[4,288,128]{2,1,0:T(8,128)(2,1)S(1)}, u32[]{:S(2)}, u32[]{:S(2)}) collective-permute-start(bf16[4,288,128]{2,1,0:T(8,128)(2,1)S(1)} %slice.60), channel_id=1, source_target_pairs={{0,6},{2,0},{4,2},{6,4},{1,7},{3,1},{5,3},{7,5},{8,14},{10,8},{12,... | collective-permute-start | bytes 884744 | tf_op jit(solution)/shard_map/cond/branch_1_fun/ppermute | solution.py:17
  116.3 16.4 %collective-permute-start.5 = (bf16[288,4096]{1,0:T(8,128)(2,1)}, bf16[288,4096]{1,0:T(8,128)(2,1)}, u32[]{:S(2)}, u32[]{:S(2)}) collective-permute-start(bf16[288,4096]{1,0:T(8,128)(2,1)} %merge.1), channel_id=1, source_target_pairs={{0,64},{64,0},{1,65},{65,1},{2,66},{66,2},{3,67},{67,3},{4,68},{68... | collective-permute-start | bytes 7077896 | tf_op jit(solution)/shard_map/cond/branch_1_fun/ppermute | solution.py:17
  128.1 9.1 %collective-permute-start.4 = (bf16[288,4096]{1,0:T(8,128)(2,1)}, bf16[288,4096]{1,0:T(8,128)(2,1)}, u32[]{:S(2)}, u32[]{:S(2)}) collective-permute-start(bf16[288,4096]{1,0:T(8,128)(2,1)} %norm.1), channel_id=1, source_target_pairs={{0,64},{64,0},{1,65},{65,1},{2,66},{66,2},{3,67},{67,3},{4,68},{68... | collective-permute-start | bytes 7077896 | tf_op jit(solution)/shard_map/cond/branch_1_fun/ppermute | solution.py:17
  195.8 6.5 %collective-permute-start.11 = (bf16[2,96,512]{2,1,0:T(8,128)(2,1)S(1)}, bf16[2,96,512]{2,1,0:T(8,128)(2,1)S(1)}, u32[]{:S(2)}, u32[]{:S(2)}) collective-permute-start(bf16[2,96,512]{2,1,0:T(8,128)(2,1)S(1)} %broadcast_select_fusion.2), channel_id=1, source_target_pairs={{0,64},{64,0},{1,65},{65,1},{2,66},{66,2},{3,67},{67,3},{4,68},{68... | collective-permute-start | bytes 589832 | tf_op jit(solution)/shard_map/ppermute | solution.py:17
Sparse Core Ops, SparseCore 0:
  12.5 65.3 reduce-scatter.2
  91.5 47.7 all-gather.1
  148.7 46.0 reduce-scatter.4

commit v7 on v6

--- a/solution.py
+++ b/solution.py
@@ -154,9 +154,13 @@
     )(info, *blocks, *extra)
 
 
-def stage_kernel(flag_ref, first, second, out, come, leave, come_sem, leave_sem):
+def stage_kernel(table_ref, position_ref, first, second, out, come, leave, come_sem, leave_sem):
     units, width = first.shape
     half, step = units // 2, width // 4
+    replicas = table_ref.shape[1]
+    chosen = jnp.int32(replicas)
+    for p in reversed(range(replicas)):
+        chosen = jnp.where(table_ref[1, p] == 1, p, chosen)
     copies = []
     for k in range(4):
         columns = pl.ds(k * step, step)
@@ -171,7 +175,7 @@
             copies[2 * k + j].wait()
             for c in range(2):
                 kept = come[k, j, c * half:(c + 1) * half, :].astype(f32)
-                kept = jnp.where(flag_ref[0] == 1, kept, 0.0)
+                kept = jnp.where(chosen == position_ref[0], kept, 0.0)
                 leave[2 * k + c, j * half:(j + 1) * half, :] = kept.astype(bf16)
         block = pl.ds(2 * k, 2)
         leaving.append(pltpu.make_async_copy(leave.at[block], out.at[block], leave_sem.at[k]))
@@ -180,11 +184,12 @@
         copy.wait()
 
 
-def stage(flag, first, second):
+def stage(table, position, first, second):
     units, width = first.shape
     return pl.pallas_call(
         stage_kernel,
-        in_specs=[pl.BlockSpec(memory_space=pltpu.SMEM)] + [pl.BlockSpec(memory_space=pl.ANY)] * 2,
+        in_specs=[pl.BlockSpec(memory_space=pltpu.SMEM)] * 2
+        + [pl.BlockSpec(memory_space=pl.ANY)] * 2,
         out_specs=pl.BlockSpec(memory_space=pl.ANY),
         out_shape=jax.ShapeDtypeStruct((8, units, width // 4), bf16),
         scratch_shapes=[
@@ -195,7 +200,7 @@
         ],
         compiler_params=pltpu.CompilerParams(vmem_limit_bytes=60 * MIB),
         name="stage",
-    )(flag, first, second)
+    )(table, position, first, second)
 
 
 def gradient_kernel(
@@ -323,8 +328,7 @@
     live_counts = tok * (4 + replica_table[:, 0]) // 6
     live = lax.dynamic_index_in_dim(live_counts, position, 0, keepdims=False)
 
-    flag = (position == source).astype(jnp.int32).reshape(1)
-    staged = stage(flag, weight_in[0], weight_out[0])
+    staged = stage(replica_table.T, position.reshape(1), weight_in[0], weight_out[0])
     share_w = lax.psum_scatter(
         staged.reshape(8 * units, width // 4), ("yh", "core"), scatter_dimension=0, tiled=True
     )

time: 212 us -> 211 us (level)
  transfers between devices with their start and end apart: 18 -> 18, of which waited for: 12 -> 12; matrix products, arithmetic and copies ran while one was open for 3% -> 4% of each run, Pallas kernels for 6% -> 6%
where the time goes in v7:
time: 211 us; the launch traced here: 210 us
  waiting for transfers between devices  84.5 us (40%)
  starting transfers between devices  70.4 us (33%)
  Pallas kernels  26.5 us (13%)
  between operations  14.5 us (7%)
  local copies, waits for them, and re-layouts  6.3 us (3%)
  other arithmetic  5.17 us (2%)
  loops' own time  2.51 us (1%)
    reduce_scatter x1, waiting for transfers between devices, on_device(): lax.psum_scatter(terms, ('yh', 'yl'), scatter_dimension=0, tiled=True)  46.1 us
    ppermute x12, starting transfers between devices, shift(): lax.ppermute(value, axis, [(i, (i + by) % size) for i in range(size)])  45.4 us
    ppermute x12, waiting for transfers between devices, shift(): lax.ppermute(value, axis, [(i, (i + by) % size) for i in range(size)])  29.3 us
    all_to_all x1, starting transfers between devices, slots(): cot = lax.all_to_all(cot, ('z', 'yl'), 0, 0).reshape(8, half, 2 * cols)  12 us
    pallas_call x2, Pallas kernels, assemble(): pl.pallas_call(kernel, in_specs=[pl.BlockSpec(memory_space=pltpu.SMEM)] +...  9.63 us
    pallas_call x1, Pallas kernels, gradients(): pl.pallas_call(gradient_kernel, in_specs=[pl.BlockSpec(memory_space=pl.AN...  9.27 us
    all_to_all x1, starting transfers between devices, slots(): got = lax.all_to_all(sent, ('yh', 'yl'), 0, 0)  6.51 us
    all_to_all x1, starting transfers between devices, gather_z(): lax.all_to_all(jnp.broadcast_to(block, (depth,) + block.shape), 'z', 0, 0)  6.36 us
  transfers between devices with their start and end apart: 18, of which 12 were waited for; matrix products, arithmetic and copies ran while one was open for 4% of the time, Pallas kernels for 6%

profile of v7, /device:TPU:1, one launch (start us, length us, event | category | flops | bytes accessed | tf_op | source)
XLA Modules:
  0.0 209.8 jit_solution(16593118170494896583)
XLA Ops:
  7.2 3.7 %stage.1 = bf16[8,192,1024]{2,1,0:T(8,128)(2,1)} custom-call(s32[2,8]{1,0:T(2,128)} %bitcast.59, s32[1]{0:T(128)} %bitcast.13.position_ref, bf16[192,4096]{1,0:T(8,128)(2,1)} %bitcast.49, bf16[192,4096]{1,0:T(8,128)(2,1)} %bitcast.50), custom_call_target="tpu_custom_call" | custom-call | tf_op jit(solution)/shard_map/stage/pallas_call | solution.py:189
  11.1 0.7 copy-done.1
  12.1 0.6 bitcast_select_fusion
  13.6 77.0 %conditional.2 = (f32[32,128]{1,0:T(8,128)S(1)}, f32[32,128]{1,0:T(8,128)S(1)}, bf16[8,288,128]{2,1,0:T(8,128)(2,1)}, bf16[8,288,128]{2,1,0:T(8,128)(2,1)}, bf16...) conditional(s32[]{:T(128)} %convert_element_type.10, () %tuple.35, ...), branch_computations={%region_1.2_spmd, %region_2.4_spmd} | conditional | flops 850717 | bytes 18120358 | solution.py:385
  13.7 0.9 broadcast_in_dim.11
  14.6 12.0 %all-to-all-start = ((bf16[16,144,128]{2,1,0:T(8,128)(2,1)}), bf16[16,144,128]{2,1,0:T(8,128)(2,1)}, u32[]{:S(2)}, u32[]{:S(2)}) async-start(bf16[16,144,128]{2,1,0:T(8,128)(2,1)} %bitcast.2), calls=%async_computation | async-start | bytes 1179648 | tf_op jit(solution)/shard_map/cond/branch_1_fun/all_to_all | solution.py:352
  26.6 2.9 %collective-permute-start.6 = (bf16[64,4224]{1,0:T(8,128)(2,1)S(1)}, bf16[64,4224]{1,0:T(8,128)(2,1)S(1)}, u32[]{:S(2)}, u32[]{:S(2)}) collective-permute-start(bf16[64,4224]{1,0:T(8,128)(2,1)S(1)} %get-tuple-element.64.own_ref), channel_id=1, source_target_pairs={{0,64},{64,0},{1,65},{65,1},{2,66},{66,2},{3,67},{67,3},{4,68},{68... | collective-permute-start | bytes 1622024 | tf_op jit(solution)/shard_map/cond/branch_1_fun/ppermute | solution.py:17
  31.3 0.3 reshape_squeeze.12.low_ref
  31.6 0.3 reshape_squeeze.13.high_ref
  31.9 3.9 %lookup.1 = bf16[1152,128]{1,0:T(8,128)(2,1)S(1)} custom-call(s32[1152,1]{1,0:T(8,128)S(1)} %reshape_squeeze.12.low_ref, s32[1152,1]{1,0:T(8,128)S(1)} %reshape_squeeze.13.high_ref, bf16[64,4224]{1,0:T(8,128)(2,1)S(1)} %get-tuple-element.64.own_ref, bf16[64,4224]{1,0:T(8,128)(2,1)S(1)} %collective-permute-done.6.other_ref), custom_call_target="tpu_custom_call" | custom-call | tf_op jit(solution)/shard_map/cond/branch_1_fun/lookup/pallas_call | solution.py:57
  35.8 0.7 pad_maximum_fusion
  36.6 6.2 %all-to-all-done = bf16[16,144,128]{2,1,0:T(8,128)(2,1)} async-done(((bf16[16,144,128]{2,1,0:T(8,128)(2,1)}), bf16[16,144,128]{2,1,0:T(8,128)(2,1)}, u32[]{:S(2)}, u32[]{:S(2)}) %all-to-all-start) | async-done | bytes 589856 | tf_op jit(solution)/shard_map/cond/branch_1_fun/all_to_all | solution.py:352
  42.8 6.5 %all-to-all-start.1 = ((bf16[8,176,128]{2,1,0:T(8,128)(2,1)}), bf16[8,176,128]{2,1,0:T(8,128)(2,1)S(1)}, u32[]{:S(2)}, u32[]{:S(2)}) async-start(bf16[8,176,128]{2,1,0:T(8,128)(2,1)} %pad_maximum_fusion), calls=%async_computation.1 | async-start | bytes 720896 | tf_op jit(solution)/shard_map/cond/branch_1_fun/all_to_all | solution.py:359
  49.3 3.1 %collective-permute-start.7 = (bf16[8,288,128]{2,1,0:T(8,128)(2,1)}, bf16[8,288,128]{2,1,0:T(8,128)(2,1)}, u32[]{:S(2)}, u32[]{:S(2)}) collective-permute-start(bf16[8,288,128]{2,1,0:T(8,128)(2,1)} %bitcast.3), channel_id=1, source_target_pairs={{0,2},{2,4},{4,6},{6,0},{1,3},{3,5},{5,7},{7,1},{8,10},{10,12},{12... | collective-permute-start | bytes 1769480 | tf_op jit(solution)/shard_map/cond/branch_1_fun/ppermute | solution.py:17
  52.4 3.4 %collective-permute-start.8 = (bf16[8,288,128]{2,1,0:T(8,128)(2,1)}, bf16[8,288,128]{2,1,0:T(8,128)(2,1)}, u32[]{:S(2)}, u32[]{:S(2)}) collective-permute-start(bf16[8,288,128]{2,1,0:T(8,128)(2,1)} %bitcast.3), channel_id=1, source_target_pairs={{0,6},{2,0},{4,2},{6,4},{1,7},{3,1},{5,3},{7,5},{8,14},{10,8},{12,... | collective-permute-start | bytes 1769480 | tf_op jit(solution)/shard_map/cond/branch_1_fun/ppermute | solution.py:17
  55.8 8.8 %collective-permute-done.7 = bf16[8,288,128]{2,1,0:T(8,128)(2,1)} collective-permute-done((bf16[8,288,128]{2,1,0:T(8,128)(2,1)}, bf16[8,288,128]{2,1,0:T(8,128)(2,1)}, u32[]{:S(2)}, u32[]{:S(2)}) %collective-permute-start.7) | collective-permute-done | bytes 589856 | tf_op jit(solution)/shard_map/cond/branch_1_fun/ppermute | solution.py:17
  64.5 1.6 collective-permute-done.8
  66.2 0.9 broadcast_in_dim.12
  67.1 6.4 %all-to-all-start.2 = ((bf16[8,288,128]{2,1,0:T(8,128)(2,1)}), bf16[8,288,128]{2,1,0:T(8,128)(2,1)}, u32[]{:S(2)}, u32[]{:S(2)}) async-start(bf16[8,288,128]{2,1,0:T(8,128)(2,1)} %broadcast_in_dim.12), calls=%async_computation.2 | async-start | bytes 1179648 | tf_op jit(solution)/shard_map/cond/branch_1_fun/all_to_all | solution.py:301
  74.0 1.0 slice.58
  75.0 4.6 %collective-permute-start.10 = (bf16[4,288,128]{2,1,0:T(8,128)(2,1)S(1)}, bf16[4,288,128]{2,1,0:T(8,128)(2,1)}, u32[]{:S(2)}, u32[]{:S(2)}) collective-permute-start(bf16[4,288,128]{2,1,0:T(8,128)(2,1)S(1)} %slice.58), channel_id=1, source_target_pairs={{0,6},{2,0},{4,2},{6,4},{1,7},{3,1},{5,3},{7,5},{8,14},{10,8},{12,... | collective-permute-start | bytes 884744 | tf_op jit(solution)/shard_map/cond/branch_1_fun/ppermute | solution.py:17
  79.6 1.0 slice.57
  80.6 1.9 collective-permute-start.9
  82.6 1.1 collective-permute-done.10
  83.7 6.1 %collective-permute-done.9 = bf16[4,288,128]{2,1,0:T(8,128)(2,1)} collective-permute-done((bf16[4,288,128]{2,1,0:T(8,128)(2,1)S(1)}, bf16[4,288,128]{2,1,0:T(8,128)(2,1)}, u32[]{:S(2)}, u32[]{:S(2)}) %collective-permute-start.9) | collective-permute-done | bytes 294944 | tf_op jit(solution)/shard_map/cond/branch_1_fun/ppermute | solution.py:17
  89.8 0.7 all-to-all-done.2
  90.6 0.6 dynamic_slice.11
  91.2 0.7 pad_add_fusion
  91.9 44.5 %conditional.3 = (bf16[288,4096]{1,0:T(8,128)(2,1)}, bf16[288,4096]{1,0:T(8,128)(2,1)}, bf16[288,4096]{1,0:T(8,128)(2,1)}, bf16[288,4096]{1,0:T(8,128)(2,1)}) conditional(s32[]{:T(128)} %convert_element_type.10, () %tuple.34, (bf16[8,288,128]{2,1,0:T(8,128)(2,1)}, s32[3]{0:T(128)S(1)}, bf16[8,288,128]{2,1,0:T(8,128)(2,1)}, ...), branch_computations={%region_5.6_spmd, %region_6.7_spmd} | conditional | bytes 27132176 | solution.py:388
  91.9 3.1 %collective-permute-start = (bf16[8,288,128]{2,1,0:T(8,128)(2,1)}, bf16[8,288,128]{2,1,0:T(8,128)(2,1)S(1)}, u32[]{:S(2)}, u32[]{:S(2)}) collective-permute-start(bf16[8,288,128]{2,1,0:T(8,128)(2,1)} %get-tuple-element.75.refs_0_), channel_id=1, source_target_pairs={{0,2},{2,4},{4,6},{6,0},{1,3},{3,5},{5,7},{7,1},{8,10},{10,12},{12... | collective-permute-start | bytes 1769480 | tf_op jit(solution)/shard_map/cond/branch_1_fun/ppermute | solution.py:17
  95.0 3.4 %collective-permute-start.1 = (bf16[8,288,128]{2,1,0:T(8,128)(2,1)}, bf16[8,288,128]{2,1,0:T(8,128)(2,1)S(1)}, u32[]{:S(2)}, u32[]{:S(2)}) collective-permute-start(bf16[8,288,128]{2,1,0:T(8,128)(2,1)} %get-tuple-element.75.refs_0_), channel_id=1, source_target_pairs={{0,6},{2,0},{4,2},{6,4},{1,7},{3,1},{5,3},{7,5},{8,14},{10,8},{12,... | collective-permute-start | bytes 1769480 | tf_op jit(solution)/shard_map/cond/branch_1_fun/ppermute | solution.py:17
  98.4 4.3 %merge.1 = bf16[288,4096]{1,0:T(8,128)(2,1)} custom-call(s32[3]{0:T(128)S(1)} %get-tuple-element.74.info_ref, bf16[8,288,128]{2,1,0:T(8,128)(2,1)} %get-tuple-element.76.refs_0_, bf16[8,288,128]{2,1,0:T(8,128)(2,1)} %get-tuple-element.77.refs_1_, bf16[8,288,128]{2,1,0:T(8,128)(2,1)} %get-tuple-element.78.refs_2_, ...), custom_call_target="tpu_custom_call" | custom-call | tf_op jit(solution)/shard_map/cond/branch_1_fun/merge/pallas_call | solution.py:146
  102.7 4.5 %collective-permute-done.refs_1_ = bf16[8,288,128]{2,1,0:T(8,128)(2,1)S(1)} collective-permute-done((bf16[8,288,128]{2,1,0:T(8,128)(2,1)}, bf16[8,288,128]{2,1,0:T(8,128)(2,1)S(1)}, u32[]{:S(2)}, u32[]{:S(2)}) %collective-permute-start) | collective-permute-done | bytes 589856 | tf_op jit(solution)/shard_map/cond/branch_1_fun/ppermute | solution.py:17
  107.2 1.7 collective-permute-done.1.refs_2_
  108.9 2.8 %collective-permute-start.2 = (bf16[4,288,128]{2,1,0:T(8,128)(2,1)S(1)}, bf16[4,288,128]{2,1,0:T(8,128)(2,1)S(1)}, u32[]{:S(2)}, u32[]{:S(2)}) collective-permute-start(bf16[4,288,128]{2,1,0:T(8,128)(2,1)S(1)} %slice.59), channel_id=1, source_target_pairs={{0,2},{2,4},{4,6},{6,0},{1,3},{3,5},{5,7},{7,1},{8,10},{10,12},{12... | collective-permute-start | bytes 884744 | tf_op jit(solution)/shard_map/cond/branch_1_fun/ppermute | solution.py:17
  111.8 3.7 %collective-permute-start.3 = (bf16[4,288,128]{2,1,0:T(8,128)(2,1)S(1)}, bf16[4,288,128]{2,1,0:T(8,128)(2,1)S(1)}, u32[]{:S(2)}, u32[]{:S(2)}) collective-permute-start(bf16[4,288,128]{2,1,0:T(8,128)(2,1)S(1)} %slice.60), channel_id=1, source_target_pairs={{0,6},{2,0},{4,2},{6,4},{1,7},{3,1},{5,3},{7,5},{8,14},{10,8},{12,... | collective-permute-start | bytes 884744 | tf_op jit(solution)/shard_map/cond/branch_1_fun/ppermute | solution.py:17
  115.5 6.4 %collective-permute-start.5 = (bf16[288,4096]{1,0:T(8,128)(2,1)}, bf16[288,4096]{1,0:T(8,128)(2,1)}, u32[]{:S(2)}, u32[]{:S(2)}) collective-permute-start(bf16[288,4096]{1,0:T(8,128)(2,1)} %merge.1), channel_id=1, source_target_pairs={{0,64},{64,0},{1,65},{65,1},{2,66},{66,2},{3,67},{67,3},{4,68},{68... | collective-permute-start | bytes 7077896 | tf_op jit(solution)/shard_map/cond/branch_1_fun/ppermute | solution.py:17
  121.9 5.3 %norm.1 = bf16[288,4096]{1,0:T(8,128)(2,1)} custom-call(s32[3]{0:T(128)S(1)} %get-tuple-element.74.info_ref, bf16[8,288,128]{2,1,0:T(8,128)(2,1)} %get-tuple-element.75.refs_0_, bf16[8,288,128]{2,1,0:T(8,128)(2,1)S(1)} %collective-permute-done.refs_1_, bf16[8,288,128]{2,1,0:T(8,128)(2,1)S(1)} %collective-permute-done.1.refs_2_, ...), custom_call_target="tpu_custom_call" | custom-call | tf_op jit(solution)/shard_map/cond/branch_1_fun/norm/pallas_call | solution.py:146
  127.3 4.6 %collective-permute-start.4 = (bf16[288,4096]{1,0:T(8,128)(2,1)}, bf16[288,4096]{1,0:T(8,128)(2,1)}, u32[]{:S(2)}, u32[]{:S(2)}) collective-permute-start(bf16[288,4096]{1,0:T(8,128)(2,1)} %norm.1), channel_id=1, source_target_pairs={{0,64},{64,0},{1,65},{65,1},{2,66},{66,2},{3,67},{67,3},{4,68},{68... | collective-permute-start | bytes 7077896 | tf_op jit(solution)/shard_map/cond/branch_1_fun/ppermute | solution.py:17
  131.9 4.5 %collective-permute-done.4 = bf16[288,4096]{1,0:T(8,128)(2,1)} collective-permute-done((bf16[288,4096]{1,0:T(8,128)(2,1)}, bf16[288,4096]{1,0:T(8,128)(2,1)}, u32[]{:S(2)}, u32[]{:S(2)}) %collective-permute-start.4) | collective-permute-done | bytes 2359328 | tf_op jit(solution)/shard_map/cond/branch_1_fun/ppermute | solution.py:17
  136.4 2.0 all-gather.2.cloned.1.call-done
  138.4 9.3 %gradients.1 = bf16[8,2,96,1024]{3,2,1,0:T(8,128)(2,1)} custom-call(bf16[288,4096]{1,0:T(8,128)(2,1)} %get-tuple-element.125.normed0, bf16[288,4096]{1,0:T(8,128)(2,1)} %get-tuple-element.126.normed1, bf16[288,4096]{1,0:T(8,128)(2,1)} %get-tuple-element.127.up0, bf16[288,4096]{1,0:T(8,128)(2,1)} %get-tuple-element.128.up1, bf16[8,192,1024]{2,1,0:T(8,128)(2,1)} %bitcast.48), custom_call_target="tpu_custom_call" | custom-call | tf_op jit(solution)/shard_map/gradients/pallas_call | solution.py:280
  147.7 46.1 %reduce-scatter.5.cloned.1.call-done = bf16[2,96,1024]{2,1,0:T(8,128)(2,1)} async-done(((bf16[16,96,1024]{2,1,0:T(8,128)(2,1)}), bf16[2,96,1024]{2,1,0:T(8,128)(2,1)}) %reduce-scatter.5.cloned.1.call-update) | async-done | bytes 393232 | tf_op jit(solution)/shard_map/reduce_scatter | solution.py:391
  193.8 1.0 broadcast_select_fusion.2
  194.9 5.5 %collective-permute-start.11 = (bf16[2,96,512]{2,1,0:T(8,128)(2,1)S(1)}, bf16[2,96,512]{2,1,0:T(8,128)(2,1)S(1)}, u32[]{:S(2)}, u32[]{:S(2)}) collective-permute-start(bf16[2,96,512]{2,1,0:T(8,128)(2,1)S(1)} %broadcast_select_fusion.2), channel_id=1, source_target_pairs={{0,64},{64,0},{1,65},{65,1},{2,66},{66,2},{3,67},{67,3},{4,68},{68... | collective-permute-start | bytes 589832 | tf_op jit(solution)/shard_map/ppermute | solution.py:17
  200.4 1.0 collective-permute-done.11
  201.4 1.1 broadcast_select_fusion
  202.5 0.8 fusion.5
  (45 shorter events, 1.1 us)
Async XLA Ops:
  7.2 83.4 %reduce-scatter.3.cloned.1.call-start = ((), (), s32[]{:S(2)}) async-start(), calls=%async_computation.5 | async-start | bytes 3538944 | tf_op jit(solution)/shard_map/reduce_scatter | solution.py:332
  10.9 0.9 copy-start.1
  10.9 1.0 copy-start.3
  10.9 1.1 copy-start.4
  10.9 1.1 copy-start.5
  11.0 2.5 %copy-start = (bf16[4096,64]{0,1:T(8,128)(2,1)S(1)}, bf16[4096,64]{0,1:T(8,128)(2,1)}, u32[]{:S(2)}) copy-start(bf16[4096,64]{0,1:T(8,128)(2,1)} %param.14) | copy-start | bytes 1572868
  11.0 2.6 %copy-start.2 = (s32[8,576]{1,0:T(8,128)S(1)}, s32[8,576]{1,0:T(8,128)}, u32[]{:S(2)}) copy-start(s32[8,576]{1,0:T(8,128)} %param.12) | copy-start | bytes 55300
  11.0 127.4 %all-gather.2.cloned.1.call-start = ((), (), s32[]{:S(2)}) async-start(), calls=%async_computation.6 | async-start | bytes 3538944 | tf_op jit(solution)/shard_map/all_gather | solution.py:387
  14.6 28.2 %all-to-all-start = ((bf16[16,144,128]{2,1,0:T(8,128)(2,1)}), bf16[16,144,128]{2,1,0:T(8,128)(2,1)}, u32[]{:S(2)}, u32[]{:S(2)}) async-start(bf16[16,144,128]{2,1,0:T(8,128)(2,1)} %bitcast.2), calls=%async_computation | async-start | bytes 1179648 | tf_op jit(solution)/shard_map/cond/branch_1_fun/all_to_all | solution.py:352
  26.6 5.2 %collective-permute-start.6 = (bf16[64,4224]{1,0:T(8,128)(2,1)S(1)}, bf16[64,4224]{1,0:T(8,128)(2,1)S(1)}, u32[]{:S(2)}, u32[]{:S(2)}) collective-permute-start(bf16[64,4224]{1,0:T(8,128)(2,1)S(1)} %get-tuple-element.64.own_ref), channel_id=1, source_target_pairs={{0,64},{64,0},{1,65},{65,1},{2,66},{66,2},{3,67},{67,3},{4,68},{68... | collective-permute-start | bytes 1622024 | tf_op jit(solution)/shard_map/cond/branch_1_fun/ppermute | solution.py:17
  42.8 23.4 %all-to-all-start.1 = ((bf16[8,176,128]{2,1,0:T(8,128)(2,1)}), bf16[8,176,128]{2,1,0:T(8,128)(2,1)S(1)}, u32[]{:S(2)}, u32[]{:S(2)}) async-start(bf16[8,176,128]{2,1,0:T(8,128)(2,1)} %pad_maximum_fusion), calls=%async_computation.1 | async-start | bytes 720896 | tf_op jit(solution)/shard_map/cond/branch_1_fun/all_to_all | solution.py:359
  49.3 15.3 %collective-permute-start.7 = (bf16[8,288,128]{2,1,0:T(8,128)(2,1)}, bf16[8,288,128]{2,1,0:T(8,128)(2,1)}, u32[]{:S(2)}, u32[]{:S(2)}) collective-permute-start(bf16[8,288,128]{2,1,0:T(8,128)(2,1)} %bitcast.3), channel_id=1, source_target_pairs={{0,2},{2,4},{4,6},{6,0},{1,3},{3,5},{5,7},{7,1},{8,10},{10,12},{12... | collective-permute-start | bytes 1769480 | tf_op jit(solution)/shard_map/cond/branch_1_fun/ppermute | solution.py:17
  52.4 13.8 %collective-permute-start.8 = (bf16[8,288,128]{2,1,0:T(8,128)(2,1)}, bf16[8,288,128]{2,1,0:T(8,128)(2,1)}, u32[]{:S(2)}, u32[]{:S(2)}) collective-permute-start(bf16[8,288,128]{2,1,0:T(8,128)(2,1)} %bitcast.3), channel_id=1, source_target_pairs={{0,6},{2,0},{4,2},{6,4},{1,7},{3,1},{5,3},{7,5},{8,14},{10,8},{12,... | collective-permute-start | bytes 1769480 | tf_op jit(solution)/shard_map/cond/branch_1_fun/ppermute | solution.py:17
  67.1 23.4 %all-to-all-start.2 = ((bf16[8,288,128]{2,1,0:T(8,128)(2,1)}), bf16[8,288,128]{2,1,0:T(8,128)(2,1)}, u32[]{:S(2)}, u32[]{:S(2)}) async-start(bf16[8,288,128]{2,1,0:T(8,128)(2,1)} %broadcast_in_dim.12), calls=%async_computation.2 | async-start | bytes 1179648 | tf_op jit(solution)/shard_map/cond/branch_1_fun/all_to_all | solution.py:301
  75.0 8.6 %collective-permute-start.10 = (bf16[4,288,128]{2,1,0:T(8,128)(2,1)S(1)}, bf16[4,288,128]{2,1,0:T(8,128)(2,1)}, u32[]{:S(2)}, u32[]{:S(2)}) collective-permute-start(bf16[4,288,128]{2,1,0:T(8,128)(2,1)S(1)} %slice.58), channel_id=1, source_target_pairs={{0,6},{2,0},{4,2},{6,4},{1,7},{3,1},{5,3},{7,5},{8,14},{10,8},{12,... | collective-permute-start | bytes 884744 | tf_op jit(solution)/shard_map/cond/branch_1_fun/ppermute | solution.py:17
  80.6 9.2 %collective-permute-start.9 = (bf16[4,288,128]{2,1,0:T(8,128)(2,1)S(1)}, bf16[4,288,128]{2,1,0:T(8,128)(2,1)}, u32[]{:S(2)}, u32[]{:S(2)}) collective-permute-start(bf16[4,288,128]{2,1,0:T(8,128)(2,1)S(1)} %slice.57), channel_id=1, source_target_pairs={{0,2},{2,4},{4,6},{6,0},{1,3},{3,5},{5,7},{7,1},{8,10},{10,12},{12... | collective-permute-start | bytes 884744 | tf_op jit(solution)/shard_map/cond/branch_1_fun/ppermute | solution.py:17
  90.6 103.3 %reduce-scatter.5.cloned.1.call-start = ((), (), s32[]{:S(2)}) async-start(), calls=%async_computation.7 | async-start | bytes 3538944 | tf_op jit(solution)/shard_map/reduce_scatter | solution.py:391
  91.9 15.3 %collective-permute-start = (bf16[8,288,128]{2,1,0:T(8,128)(2,1)}, bf16[8,288,128]{2,1,0:T(8,128)(2,1)S(1)}, u32[]{:S(2)}, u32[]{:S(2)}) collective-permute-start(bf16[8,288,128]{2,1,0:T(8,128)(2,1)} %get-tuple-element.75.refs_0_), channel_id=1, source_target_pairs={{0,2},{2,4},{4,6},{6,0},{1,3},{3,5},{5,7},{7,1},{8,10},{10,12},{12... | collective-permute-start | bytes 1769480 | tf_op jit(solution)/shard_map/cond/branch_1_fun/ppermute | solution.py:17
  95.0 13.9 %collective-permute-start.1 = (bf16[8,288,128]{2,1,0:T(8,128)(2,1)}, bf16[8,288,128]{2,1,0:T(8,128)(2,1)S(1)}, u32[]{:S(2)}, u32[]{:S(2)}) collective-permute-start(bf16[8,288,128]{2,1,0:T(8,128)(2,1)} %get-tuple-element.75.refs_0_), channel_id=1, source_target_pairs={{0,6},{2,0},{4,2},{6,4},{1,7},{3,1},{5,3},{7,5},{8,14},{10,8},{12,... | collective-permute-start | bytes 1769480 | tf_op jit(solution)/shard_map/cond/branch_1_fun/ppermute | solution.py:17
  108.9 13.0 %collective-permute-start.2 = (bf16[4,288,128]{2,1,0:T(8,128)(2,1)S(1)}, bf16[4,288,128]{2,1,0:T(8,128)(2,1)S(1)}, u32[]{:S(2)}, u32[]{:S(2)}) collective-permute-start(bf16[4,288,128]{2,1,0:T(8,128)(2,1)S(1)} %slice.59), channel_id=1, source_target_pairs={{0,2},{2,4},{4,6},{6,0},{1,3},{3,5},{5,7},{7,1},{8,10},{10,12},{12... | collective-permute-start | bytes 884744 | tf_op jit(solution)/shard_map/cond/branch_1_fun/ppermute | solution.py:17
  111.8 10.1 %collective-permute-start.3 = (bf16[4,288,128]{2,1,0:T(8,128)(2,1)S(1)}, bf16[4,288,128]{2,1,0:T(8,128)(2,1)S(1)}, u32[]{:S(2)}, u32[]{:S(2)}) collective-permute-start(bf16[4,288,128]{2,1,0:T(8,128)(2,1)S(1)} %slice.60), channel_id=1, source_target_pairs={{0,6},{2,0},{4,2},{6,4},{1,7},{3,1},{5,3},{7,5},{8,14},{10,8},{12,... | collective-permute-start | bytes 884744 | tf_op jit(solution)/shard_map/cond/branch_1_fun/ppermute | solution.py:17
  115.5 16.4 %collective-permute-start.5 = (bf16[288,4096]{1,0:T(8,128)(2,1)}, bf16[288,4096]{1,0:T(8,128)(2,1)}, u32[]{:S(2)}, u32[]{:S(2)}) collective-permute-start(bf16[288,4096]{1,0:T(8,128)(2,1)} %merge.1), channel_id=1, source_target_pairs={{0,64},{64,0},{1,65},{65,1},{2,66},{66,2},{3,67},{67,3},{4,68},{68... | collective-permute-start | bytes 7077896 | tf_op jit(solution)/shard_map/cond/branch_1_fun/ppermute | solution.py:17
  127.3 9.1 %collective-permute-start.4 = (bf16[288,4096]{1,0:T(8,128)(2,1)}, bf16[288,4096]{1,0:T(8,128)(2,1)}, u32[]{:S(2)}, u32[]{:S(2)}) collective-permute-start(bf16[288,4096]{1,0:T(8,128)(2,1)} %norm.1), channel_id=1, source_target_pairs={{0,64},{64,0},{1,65},{65,1},{2,66},{66,2},{3,67},{67,3},{4,68},{68... | collective-permute-start | bytes 7077896 | tf_op jit(solution)/shard_map/cond/branch_1_fun/ppermute | solution.py:17
  194.9 6.5 %collective-permute-start.11 = (bf16[2,96,512]{2,1,0:T(8,128)(2,1)S(1)}, bf16[2,96,512]{2,1,0:T(8,128)(2,1)S(1)}, u32[]{:S(2)}, u32[]{:S(2)}) collective-permute-start(bf16[2,96,512]{2,1,0:T(8,128)(2,1)S(1)} %broadcast_select_fusion.2), channel_id=1, source_target_pairs={{0,64},{64,0},{1,65},{65,1},{2,66},{66,2},{3,67},{67,3},{4,68},{68... | collective-permute-start | bytes 589832 | tf_op jit(solution)/shard_map/ppermute | solution.py:17
Sparse Core Ops, SparseCore 0:
  11.1 65.0 reduce-scatter.2
  90.7 47.6 all-gather.1
  147.8 45.9 reduce-scatter.4
